TPU v7x, 128 devices: a whole 4x4x4 slice. The times are simulated.
128 devices in a mesh: row: 16 (over z, y), col: 8 (over x, core).
Axes of the slice: x: 4, y: 4, z: 4, core: 2. Of those that a mesh axis runs over, the one named last changes fastest.
Arguments:
- readouts: bfloat16 [128, 128, 256], P('row', 'col'), may hold values from -6 to 6
- w_embed: bfloat16 [8, 64], replicated, may hold values from -2 to 2
- w_up: bfloat16 [3, 9, 64, 64], replicated, may hold values from -0.25 to 0.25
- merge_in: bfloat16 [256, 256], replicated, may hold values from -0.375 to 0.375
- merge_out: bfloat16 [256, 64], replicated, may hold values from -0.5 to 0.5
- down_in: bfloat16 [128, 256], replicated, may hold values from -0.5 to 0.5
- down_out: bfloat16 [256, 64], replicated, may hold values from -0.375 to 0.375
- w_down: bfloat16 [3, 9, 64, 64], replicated, may hold values from -0.25 to 0.25
- w_head: bfloat16 [64, 4], replicated, may hold values from -0.75 to 0.75
- qubit_slot: int32 [128, 8, 64], P('row', 'col'), may hold values from 0 to 63, each once within a row
Outputs:
- logits: float32 [32, 128, 512], P(None, 'row', 'col')
Inputs may be any that keep to these rules, and one draw needn't show every extreme that they name: For each lattice row and each column tile, qubit_slot lists every number of 0 to 63 exactly once.
All inputs are finite; a program needn't handle non-finite values.
Results may differ from a plain program's by a relative error of at most 0.04.
Values may be sent and summed in bfloat16 or wider, within the bound.
No kernel may reach another device: no remote copies, remote signals or barrier semaphores. Data moves between devices by JAX's collectives and lax.ppermute only.
A program may use at most 128 MiB of HBM per device.

v0:
```python
import functools

import jax
import jax.numpy as jnp
from jax import lax
from jax.experimental import pallas as pl
from jax.experimental.pallas import tpu as pltpu
from jax.sharding import PartitionSpec as P

norm_eps = 1e-05
bf16 = jnp.bfloat16
f32 = jnp.float32
n_row = 16
n_col = 8
samples = 32
vmem_bytes = 48 * 1024 * 1024


def dot(left, right):
    return jnp.dot(left, right, preferred_element_type=f32)


def low_half(shape):
    return lax.broadcasted_iota(jnp.int32, shape, len(shape) - 1) < 64


def whole_call(body, out_shapes, scratch, args, smem=()):
    specs = [
        pl.BlockSpec(memory_space=pltpu.SMEM) if i in smem else pl.BlockSpec(memory_space=pltpu.VMEM)
        for i in range(len(args))
    ]
    return pl.pallas_call(
        body,
        out_shape=out_shapes,
        in_specs=specs,
        out_specs=jax.tree.map(lambda _: pl.BlockSpec(memory_space=pltpu.VMEM), out_shapes),
        scratch_shapes=scratch,
        compiler_params=pltpu.CompilerParams(vmem_limit_bytes=vmem_bytes),
    )(*args)


def arr(shape, dtype=bf16):
    return jax.ShapeDtypeStruct(shape, dtype)


def fill_quad_weights(src, out, layer, from_odd):
    zero = jnp.zeros((64, 64), bf16)

    def tap_of(step, parity_in, parity_out):
        place_in = 1 - parity_in if from_odd else parity_in
        place_out = parity_out if from_odd else 1 - parity_out
        tap = 2 * step + place_in - place_out
        return tap if 0 <= tap <= 2 else None

    for di in range(2):
        for dj in range(2):
            for a in range(2):
                for b in range(2):
                    base = ((di * 2 + dj) * 4 + a * 2 + b) * 64
                    for oa in range(2):
                        tap_row = tap_of(di, a, oa)
                        blocks = []
                        for ob in range(2):
                            tap_col = tap_of(dj, b, ob)
                            if tap_row is None or tap_col is None:
                                blocks.append(zero)
                            else:
                                blocks.append(src[layer, 3 * tap_row + tap_col])
                        out[layer, base : base + 64, oa * 128 : oa * 128 + 128] = jnp.concatenate(
                            blocks, axis=1
                        )


def prep_up_body(w_up, w_embed, merge_out, wq, we, mo):
    for layer in range(3):
        fill_quad_weights(w_up, wq, layer, layer % 2 == 0)
    tiled = jnp.concatenate([w_embed[...].astype(f32)] * 16, axis=0)
    none = jnp.zeros((128, 64), f32)
    for a in range(2):
        for b in range(2):
            q = 2 * a + b
            pair = [tiled, none] if b == 0 else [none, tiled]
            we[q * 128 : q * 128 + 128, a * 128 : a * 128 + 128] = jnp.concatenate(
                pair, axis=1
            ).astype(bf16)
            we[q * 128 : q * 128 + 128, (1 - a) * 128 : (1 - a) * 128 + 128] = jnp.zeros(
                (128, 128), bf16
            )
    mo[...] = jnp.concatenate([merge_out[...], merge_out[...]], axis=1)


def prep_down_body(w_down, down_in, down_out, head_tiled, wq, di0, do0, do, wh):
    for layer in range(3):
        fill_quad_weights(w_down, wq, layer, layer % 2 == 1)
    zero = jnp.zeros((64, 256), bf16)
    parent = down_in[0:64, :]
    child = down_in[64:128, :]
    di0[0:64, 0:256] = child
    di0[0:64, 256:512] = zero
    di0[64:128, 0:256] = zero
    di0[64:128, 256:512] = child
    di0[128:192, 0:256] = parent
    di0[128:192, 256:512] = parent
    di0[192:256, 0:256] = zero
    di0[192:256, 256:512] = zero
    back = down_out[...]
    none = jnp.zeros((256, 64), bf16)
    do0[0:256, :] = jnp.concatenate([back, none], axis=1)
    do0[256:512, :] = jnp.concatenate([none, back], axis=1)
    do[...] = jnp.concatenate([back, back], axis=1)
    lane = lax.broadcasted_iota(jnp.int32, (64, 128), 1)
    head = head_tiled[...].astype(f32)
    for quad in range(9):
        for a in range(2):
            for b in range(2):
                base = quad * 256 + (a * 2 + b) * 64
                column = 2 * quad - b
                if 0 <= column < 16:
                    first = a * 64 + 4 * column
                    kept = jnp.where((lane >= first) & (lane < first + 4), head, 0.0)
                else:
                    kept = jnp.zeros((64, 128), f32)
                wh[base : base + 64, :] = kept.astype(bf16)


def conv_layer(src, dst, weights, rows, cols, to_odd):
    low = low_half((cols, samples, 128))

    def step(i, carry):
        here = src[i, 0:cols]
        right = src[i, 1 : cols + 1]
        below = src[i + 1, 0:cols]
        corner = src[i + 1, 1 : cols + 1]
        stacked = jnp.concatenate([here, right, below, corner], axis=-1)
        update = dot(stacked.reshape(cols * samples, 1024), weights[...])
        update = jnp.maximum(update, 0.0).reshape(cols, samples, 256)
        if to_odd:
            old0 = jnp.where(low, corner[..., 0:128], below[..., 0:128])
            old1 = jnp.where(low, right[..., 128:256], here[..., 128:256])
        else:
            old0 = jnp.where(low, here[..., 0:128], right[..., 0:128])
            old1 = jnp.where(low, below[..., 128:256], corner[..., 128:256])
        dst[i, :, :, 0:128] = (old0.astype(f32) + update[..., 0:128]).astype(bf16)
        dst[i, :, :, 128:256] = (old1.astype(f32) + update[..., 128:256]).astype(bf16)
        return carry

    lax.fori_loop(0, rows, step, 0)


def spread_tiles(place, own, row_a, row_b, col_a, col_b, ext):
    row_even = place[0] % 2 == 0
    col_even = place[1] % 2 == 0
    after_row = jnp.where(row_even, 16, 0)
    before_row = jnp.where(row_even, 0, 16)
    after_col = jnp.where(col_even, 3, 0)
    before_col = jnp.where(col_even, 0, 3)
    for tile, ref, start in ((0, own, 8), (1, row_a, after_row), (2, row_b, before_row)):
        cells = ref[...].astype(f32)
        ext[pl.ds(start, 8), 1] = cells[:, 0:8]
        ext[pl.ds(start, 8), 2] = cells[:, 8:16]
        ext[pl.ds(start, 8), after_col] = col_a[tile].astype(f32)
        ext[pl.ds(start, 8), before_col] = col_b[tile].astype(f32)


def embed_quads(ext, we, lhs, dst, halo):
    rows = 4 + halo
    cols = 8 + halo
    first = 8 - halo
    sub = lax.broadcasted_iota(jnp.int32, (16, 128), 0)
    lane = lax.broadcasted_iota(jnp.int32, (16, 128), 1)
    own_lanes = (lane // 8 == sub).astype(f32)

    def step(i, carry):
        for quad in range(cols):
            for a in range(2):
                row = first + 2 * i + (1 - a)
                for b in range(2):
                    col = first + 2 * quad + (1 - b)
                    cell = ext[row, col // 8, col % 8 : col % 8 + 1, :]
                    for half in range(2):
                        part = cell[:, half * 128 : half * 128 + 128]
                        spread = jnp.broadcast_to(part, (16, 128)) * own_lanes
                        start = quad * 32 + half * 16
                        q = 2 * a + b
                        lhs[start : start + 16, q * 128 : q * 128 + 128] = spread.astype(bf16)
        embedded = dot(lhs[...], we[...]).astype(bf16)
        dst[i] = embedded.reshape(cols, samples, 256)
        return carry

    lax.fori_loop(0, rows, step, 0)


def merge_pair(top, bottom, merge_in, mo):
    count = top.shape[0]
    stacked = jnp.concatenate([top, bottom], axis=-1).reshape(count * samples, 256)
    hidden = jnp.maximum(dot(stacked, merge_in), 0.0).astype(bf16)
    return dot(hidden, mo).astype(bf16).reshape(count, samples, 128)


def merge_quads(src, dst, merge_in, mo, rows, cols):
    def step(i, carry):
        stacked = src[i].reshape(cols * samples, 256)
        hidden = jnp.maximum(dot(stacked, merge_in[...]), 0.0).astype(bf16)
        dst[i] = dot(hidden, mo[...]).astype(bf16).reshape(cols, samples, 128)
        return carry

    lax.fori_loop(0, rows, step, 0)


def paired_columns(cells):
    count = cells.shape[0] // 2
    split = cells.reshape(count, 2, samples, 128)
    low = low_half((count, samples, 128))
    return jnp.where(low, split[:, 0], split[:, 1])


def up_own_body(
    place, own, row_a, row_b, col_a, col_b, wq, we, merge_in, mo, out, ext, lhs, f0, f1, f2, f3, l1
):
    spread_tiles(place, own, row_a, row_b, col_a, col_b, ext)
    embed_quads(ext, we, lhs, f0, 3)
    conv_layer(f0, f1, wq.at[0], 6, 10, False)
    conv_layer(f1, f2, wq.at[1], 5, 9, True)
    conv_layer(f2, f3, wq.at[2], 4, 8, False)
    merge_quads(f3, l1, merge_in, mo, 4, 8)
    top = jnp.concatenate([paired_columns(l1[0]), paired_columns(l1[2])], axis=0)
    bottom = jnp.concatenate([paired_columns(l1[1]), paired_columns(l1[3])], axis=0)
    l2 = merge_pair(top, bottom, merge_in[...], mo[...])
    l3 = merge_pair(paired_columns(l2[0:4]), paired_columns(l2[4:8]), merge_in[...], mo[...])
    out[...] = paired_columns(l3)[0]


def up_wide_first_body(place, own, row_a, row_b, col_a, col_b, wq, we, f1, ext, lhs, f0):
    spread_tiles(place, own, row_a, row_b, col_a, col_b, ext)
    embed_quads(ext, we, lhs, f0, 7)
    conv_layer(f0, f1, wq.at[0], 10, 14, False)


def up_wide_second_body(f1, wq, f3, f2):
    conv_layer(f1, f2, wq.at[1], 9, 13, True)
    conv_layer(f2, f3, wq.at[2], 8, 12, False)


def up_wide_merge_body(f3, merge_in, mo, l1, l2):
    merge_quads(f3, l1, merge_in, mo, 8, 12)
    for i in range(4):
        l2[i] = merge_pair(
            paired_columns(l1[2 * i]), paired_columns(l1[2 * i + 1]), merge_in[...], mo[...]
        )


def mid_body(place, z0, z1, z2, z3, merge_in, mo, a3, a4, p5, send1, send3, strip, l4s):
    row = place[0]
    col = place[1]
    deep = row // 4
    high = row % 4
    wide = col // 2
    core = col % 2
    for m, ref in enumerate((z0, z1, z2, z3)):
        for n in range(4):
            for k in range(2):
                strip[deep ^ m, high ^ n, core ^ k] = ref[n, k]
    cells = strip[...].reshape(8, 2, 2, samples, 128)
    l4 = merge_pair(
        cells[:, 0].reshape(16, samples, 128),
        cells[:, 1].reshape(16, samples, 128),
        merge_in[...],
        mo[...],
    )
    l4s[...] = l4.reshape(8, 2, samples, 128)
    pairs = paired_columns(l4).reshape(4, 2, samples, 128)
    l5 = merge_pair(pairs[:, 0], pairs[:, 1], merge_in[...], mo[...])
    packed = paired_columns(l5)
    p5[...] = packed
    low = low_half((samples, 128))
    wide_even = wide % 2 == 0
    for d in range(3):
        line = (row + d + (n_row - 1)) % n_row
        left = strip[line // 4, line % 4, 0]
        right = strip[line // 4, line % 4, 1]
        a3[d, 0] = left
        a3[d, 1] = right
        left4 = l4s[line // 2, 0]
        right4 = l4s[line // 2, 1]
        a4[d, 0] = left4
        a4[d, 1] = right4
        to_right = jnp.where(low, right4, right)
        to_left = jnp.where(low, left, left4)
        send1[d] = jnp.where(wide_even, to_right, to_left)
        send3[d] = jnp.where(wide_even, to_left, to_right)
    send1[3:5] = packed
    send3[3:5] = packed


def both_lanes(cells):
    wide = cells.astype(f32)
    turned = pltpu.roll(wide, 64, wide.ndim - 1)
    low = low_half(wide.shape)
    return jnp.where(low, wide, turned).astype(bf16), jnp.where(low, turned, wide).astype(bf16)


def refine(parent, child, down_in, do):
    count = parent.shape[0]
    low = low_half(parent.shape)
    joined = jnp.where(low, parent, child).reshape(count * samples, 128)
    inner = jnp.maximum(dot(joined, down_in), 0.0).astype(bf16)
    outcome = dot(inner, do).reshape(count, samples, 128)
    return (outcome + child.astype(f32) + parent.astype(f32)).astype(bf16)


def descent_body(
    place,
    slots,
    a3,
    a4,
    p5,
    q1,
    q2,
    q3,
    f3,
    l1,
    l2,
    merge_in,
    mo,
    down_in,
    do,
    di0,
    do0,
    wq,
    wh,
    out,
    l5s,
    c6s,
    c3s,
    p3s,
    c2s,
    n0,
    r1,
    r2,
    r3,
):
    row = place[0]
    col = place[1]
    wide = col // 2
    core = col % 2
    wide_even = wide % 2 == 0
    merge_weights = merge_in[...]
    back_weights = mo[...]
    in_weights = down_in[...]
    out_weights = do[...]

    for m, ref, start in ((0, p5, 0), (1, q1, 3), (2, q2, 0), (3, q3, 3)):
        for pair in range(2):
            first, second = both_lanes(ref[start + pair])
            l5s[wide ^ m, 2 * pair] = first
            l5s[wide ^ m, 2 * pair + 1] = second
    grid = l5s[...].reshape(2, 2, 2, 2, samples, 128)
    low4 = low_half((4, samples, 128))
    top = jnp.where(
        low4,
        grid[:, 0, :, 0].reshape(4, samples, 128),
        grid[:, 1, :, 0].reshape(4, samples, 128),
    )
    bottom = jnp.where(
        low4,
        grid[:, 0, :, 1].reshape(4, samples, 128),
        grid[:, 1, :, 1].reshape(4, samples, 128),
    )
    l6 = merge_pair(top, bottom, merge_weights, back_weights)
    low1 = low_half((1, samples, 128))
    l7 = merge_pair(
        jnp.where(low1, l6[0:1], l6[2:3]),
        jnp.where(low1, l6[1:2], l6[3:4]),
        merge_weights,
        back_weights,
    )
    c6s[...] = refine(
        jnp.broadcast_to(l7, (4, samples, 128)), l6, in_weights, out_weights
    ).reshape(2, 2, samples, 128)

    side = jnp.where(core == 0, (wide + 3) % 4, (wide + 1) % 4)
    lines = [(row + d + (n_row - 1)) % n_row for d in range(3)]
    parents5 = []
    children5 = []
    for place_x in (wide, side):
        for line in lines:
            deep = line // 4
            parents5.append(c6s[place_x // 2, deep // 2])
            children5.append(l5s[place_x, deep])
    c5 = refine(jnp.stack(parents5), jnp.stack(children5), in_weights, out_weights)

    from_first = jnp.logical_xor(wide_even, core == 0)
    side_cells = jnp.where(from_first, q1[0:3], q3[0:3])
    side_low, side_high = both_lanes(side_cells)
    side4 = jnp.where(core == 0, side_low, side_high)
    side3 = jnp.where(core == 0, side_high, side_low)
    own4 = a4[...]
    children4 = jnp.concatenate([own4[:, 0], own4[:, 1], side4], axis=0)
    parents4 = jnp.concatenate([c5[0:3], c5[0:3], c5[3:6]], axis=0)
    c4 = refine(parents4, children4, in_weights, out_weights)
    own3_0, own3_1 = both_lanes(a3[:, 0])
    own3_2, own3_3 = both_lanes(a3[:, 1])
    for k, cells in enumerate((side3, own3_0, own3_1, own3_2, own3_3, side3)):
        c3s[k] = cells
    for k, start in enumerate((6, 0, 0, 3, 3, 6)):
        p3s[k] = c4[start : start + 3]
    window = pl.ds(2 * core, 4)
    c3 = refine(
        p3s[window].reshape(12, samples, 128),
        c3s[window].reshape(12, samples, 128),
        in_weights,
        out_weights,
    ).reshape(4, 3, samples, 128)
    parents2 = jnp.stack([c3[j, i] for i in (0, 1, 1, 2) for j in (0, 1, 1, 2, 2, 3)])
    c2s[...] = refine(
        parents2, l2[...].reshape(24, samples, 128), in_weights, out_weights
    ).reshape(4, 6, samples, 128)

    sub = lax.broadcasted_iota(jnp.int32, (128, 128), 0)
    lane = lax.broadcasted_iota(jnp.int32, (128, 128), 1)
    averager = jnp.where((sub < 64) == (lane < 64), 1.0 / 64, 0.0).astype(bf16)

    def fine_row(i, carry):
        parent = c2s[i // 2]
        parent = jnp.broadcast_to(parent[:, None], (6, 2, samples, 128)).reshape(12, samples, 128)
        c1 = refine(parent, l1[i], in_weights, out_weights)
        c1_wide = c1.astype(f32).reshape(12 * samples, 128)
        for a in range(2):
            child = f3[i, :, :, a * 128 : a * 128 + 128]
            joined = jnp.concatenate([child, c1], axis=-1).reshape(12 * samples, 256)
            inner = jnp.maximum(dot(joined, di0[...]), 0.0).astype(bf16)
            fine = dot(inner, do0[...])
            fine = fine + child.astype(f32).reshape(12 * samples, 128) + c1_wide
            mean = dot((fine * fine).astype(bf16), averager)
            normed = fine * lax.rsqrt(mean + norm_eps)
            n0[i, :, :, a * 128 : a * 128 + 128] = normed.astype(bf16).reshape(12, samples, 128)
        return carry

    lax.fori_loop(0, 8, fine_row, 0)
    conv_layer(n0, r1, wq.at[0], 7, 11, True)
    conv_layer(r1, r2, wq.at[1], 6, 10, False)
    conv_layer(r2, r3, wq.at[2], 5, 9, True)
    stacked = jnp.concatenate(
        [r3[:, quad].reshape(5 * samples, 256) for quad in range(9)], axis=-1
    )
    cell_logits = dot(stacked, wh[...]).reshape(5, samples, 128)
    coarse = cell_logits.astype(bf16)
    rest = (cell_logits - coarse.astype(f32)).astype(bf16)
    places = lax.broadcasted_iota(jnp.int32, (128, 64), 0)
    for i in range(8):
        quad_row = (i + 1) // 2
        chosen = (places == slots[i : i + 1, :] + 64 * (i % 2)).astype(bf16)
        out[:, i, :] = dot(coarse[quad_row], chosen) + dot(rest[quad_row], chosen)


def swap(value, partner):
    pairs = []
    for r in range(n_row):
        for c in range(n_col):
            pr, pc = partner(r, c)
            pairs.append((r * n_col + c, pr * n_col + pc))
    return lax.ppermute(value, ("row", "col"), pairs)


def pair_after(i, count):
    return i ^ 1


def pair_before(i, count):
    return (((i - 1) % count ^ 1) + 1) % count


def on_device(
    readouts, w_embed, w_up, merge_in, merge_out, down_in, down_out, w_down, w_head, qubit_slot
):
    row = lax.axis_index("row")
    col = lax.axis_index("col")
    place = jnp.stack([row, col]).astype(jnp.int32)
    col_even = col % 2 == 0

    row_a = swap(readouts, lambda r, c: (pair_after(r, n_row), c))
    row_b = swap(readouts, lambda r, c: (pair_before(r, n_row), c))
    tiles = jnp.stack([readouts, row_a, row_b])
    left = tiles[:, :, 0:8]
    right = tiles[:, :, 8:16]
    col_a = swap(jnp.where(col_even, right, left), lambda r, c: (r, pair_after(c, n_col)))
    col_b = swap(jnp.where(col_even, left, right), lambda r, c: (r, pair_before(c, n_col)))

    wq_up, we, mo = whole_call(
        prep_up_body,
        (arr((3, 1024, 256)), arr((512, 256)), arr((256, 128))),
        [],
        (w_up, w_embed, merge_out),
    )
    wq_down, di0, do0, do, wh = whole_call(
        prep_down_body,
        (
            arr((3, 1024, 256)),
            arr((256, 512)),
            arr((512, 128)),
            arr((256, 128)),
            arr((2304, 128)),
        ),
        [],
        (w_down, down_in, down_out, jnp.tile(w_head, (1, 32))),
    )

    tile_args = (place, readouts, row_a, row_b, col_a, col_b)
    quads = lambda rows, cols: pltpu.VMEM((rows, cols, samples, 256), bf16)
    ext = pltpu.VMEM((24, 4, 8, 256), f32)
    l3 = whole_call(
        up_own_body,
        arr((samples, 128)),
        [
            ext,
            pltpu.VMEM((11 * samples, 512), bf16),
            quads(7, 11),
            quads(6, 10),
            quads(5, 9),
            quads(4, 8),
            pltpu.VMEM((4, 8, samples, 128), bf16),
        ],
        (*tile_args, wq_up, we, merge_in, mo),
        smem=(0,),
    )

    pair = jnp.stack([l3, swap(l3, lambda r, c: (r, c ^ 1))])
    four = jnp.stack([pair] + [swap(pair, lambda r, c, m=m: (r ^ m, c)) for m in (1, 2, 3)])
    f1 = whole_call(
        up_wide_first_body,
        arr((10, 14, samples, 256)),
        [ext, pltpu.VMEM((15 * samples, 512), bf16), quads(11, 15)],
        (*tile_args, wq_up, we),
        smem=(0,),
    )
    strips = [four] + [swap(four, lambda r, c, m=m: (r ^ (4 * m), c)) for m in (1, 2, 3)]
    f3 = whole_call(
        up_wide_second_body, arr((8, 12, samples, 256)), [quads(9, 13)], (f1, wq_up)
    )
    a3, a4, p5, send1, send3 = whole_call(
        mid_body,
        (
            arr((3, 2, samples, 128)),
            arr((3, 2, samples, 128)),
            arr((2, samples, 128)),
            arr((5, samples, 128)),
            arr((5, samples, 128)),
        ),
        [pltpu.VMEM((4, 4, 2, samples, 128), bf16), pltpu.VMEM((8, 2, samples, 128), bf16)],
        (place, *strips, merge_in, mo),
        smem=(0,),
    )
    q1 = swap(send1, lambda r, c: (r, c ^ 2))
    q2 = swap(p5, lambda r, c: (r, c ^ 4))
    q3 = swap(send3, lambda r, c: (r, c ^ 6))
    l1, l2 = whole_call(
        up_wide_merge_body,
        (arr((8, 12, samples, 128)), arr((4, 6, samples, 128))),
        [],
        (f3, merge_in, mo),
    )
    slots = qubit_slot.reshape(qubit_slot.shape[0], qubit_slot.shape[2])
    return whole_call(
        descent_body,
        arr((samples, 8, 64), f32),
        [
            pltpu.VMEM((4, 4, samples, 128), bf16),
            pltpu.VMEM((2, 2, samples, 128), bf16),
            pltpu.VMEM((6, 3, samples, 128), bf16),
            pltpu.VMEM((6, 3, samples, 128), bf16),
            pltpu.VMEM((4, 6, samples, 128), bf16),
            quads(8, 12),
            quads(7, 11),
            quads(6, 10),
            quads(5, 9),
        ],
        (
            place,
            slots,
            a3,
            a4,
            p5,
            q1,
            q2,
            q3,
            f3,
            l1,
            l2,
            merge_in,
            mo,
            down_in,
            do,
            di0,
            do0,
            wq_down,
            wh,
        ),
        smem=(0,),
    )


def solution(mesh):
    placed = (P("row", "col", None), P(), P(), P(), P(), P(), P(), P(), P(), P("row", "col", None))
    return jax.shard_map(
        on_device, mesh=mesh, in_specs=placed, out_specs=P(None, "row", "col"), check_vma=False
    )
```

profile of v0, /device:TPU:0, one launch (start us, length us, event | category | flops | bytes accessed | tf_op | source)
XLA Modules:
  0.0 90.0 jit_solution(5842463767755812326)
XLA Ops:
  0.0 1.7 %collective-permute-start = (bf16[8,16,256]{2,1,0:T(8,128)(2,1)}, bf16[8,16,256]{2,1,0:T(8,128)(2,1)S(1)}, u32[]{:S(2)}, u32[]{:S(2)}) collective-permute-start(bf16[8,16,256]{2,1,0:T(8,128)(2,1)} %own.3), channel_id=1, source_target_pairs={{0,8},{1,9},{2,10},{3,11},{4,12},{5,13},{6,14},{7,15},{8,0},{9,1},... | collective-permute-start | bytes 196616 | tf_op jit(solution)/shard_map/ppermute | solution.py:462
  1.7 5.7 %collective-permute-start.1 = (bf16[8,16,256]{2,1,0:T(8,128)(2,1)}, bf16[8,16,256]{2,1,0:T(8,128)(2,1)S(1)}, u32[]{:S(2)}, u32[]{:S(2)}) collective-permute-start(bf16[8,16,256]{2,1,0:T(8,128)(2,1)} %own.3), channel_id=1, source_target_pairs={{0,120},{1,121},{2,122},{3,123},{4,124},{5,125},{6,126},{7,127},{8... | collective-permute-start | bytes 196616 | tf_op jit(solution)/shard_map/ppermute | solution.py:462
  7.3 0.9 copy.14.merge_out
  8.2 1.0 %copy-done.5 = bf16[3,9,64,64]{3,2,1,0:T(8,128)(2,1)S(1)} copy-done((bf16[3,9,64,64]{3,2,1,0:T(8,128)(2,1)S(1)}, bf16[3,9,64,64]{3,2,1,0:T(8,128)(2,1)}, u32[]{:S(2)}) %copy-start.5) | copy-done | bytes 221208
  10.3 0.9 pad_maximum_fusion
  11.3 2.9 %collective-permute-start.3 = (bf16[3,8,8,256]{3,2,1,0:T(8,128)(2,1)S(1)}, bf16[3,8,8,256]{3,2,1,0:T(8,128)(2,1)S(1)}, u32[]{:S(2)}, u32[]{:S(2)}) collective-permute-start(bf16[3,8,8,256]{3,2,1,0:T(8,128)(2,1)S(1)} %get-tuple-element.35), channel_id=1, source_target_pairs={{0,7},{1,2},{2,1},{3,4},{4,3},{5,6},{6,5},{7,0},{8,15},{9,10},{10,... | collective-permute-start | bytes 294920 | tf_op jit(solution)/shard_map/ppermute | solution.py:462
  14.2 2.4 %collective-permute-done.3.col_b = bf16[3,8,8,256]{3,2,1,0:T(8,128)(2,1)S(1)} collective-permute-done((bf16[3,8,8,256]{3,2,1,0:T(8,128)(2,1)S(1)}, bf16[3,8,8,256]{3,2,1,0:T(8,128)(2,1)S(1)}, u32[]{:S(2)}, u32[]{:S(2)}) %collective-permute-start.3) | collective-permute-done | bytes 98336 | tf_op jit(solution)/shard_map/ppermute | solution.py:462
  16.6 0.9 %copy-done = bf16[256,256]{1,0:T(8,128)(2,1)S(1)} copy-done((bf16[256,256]{1,0:T(8,128)(2,1)S(1)}, bf16[256,256]{1,0:T(8,128)(2,1)}, u32[]{:S(2)}) %copy-start) | copy-done | bytes 131096
  17.5 0.8 copy-done.2
  18.4 9.3 %shard_map.101 = bf16[32,128]{1,0:T(8,128)(2,1)S(1)} custom-call(s32[2]{0:T(128)S(1)} %pad_add_fusion.place, bf16[8,16,256]{2,1,0:T(8,128)(2,1)S(1)} %copy-done.2, bf16[8,16,256]{2,1,0:T(8,128)(2,1)S(1)} %collective-permute-done.row_a, bf16[8,16,256]{2,1,0:T(8,128)(2,1)S(1)} %collective-permute-done.1.row_b, ...), custom_call_target="tpu_custom_call" | custom-call | tf_op jit(solution)/shard_map/pallas_call | solution.py:32
  27.8 1.2 %collective-permute-done.4 = bf16[32,128]{1,0:T(8,128)(2,1)S(1)} collective-permute-done((bf16[32,128]{1,0:T(8,128)(2,1)S(1)}, bf16[32,128]{1,0:T(8,128)(2,1)S(1)}, u32[]{:S(2)}, u32[]{:S(2)}) %collective-permute-start.4) | collective-permute-done | bytes 8224 | tf_op jit(solution)/shard_map/ppermute | solution.py:462
  29.1 4.0 %collective-permute-start.5 = (bf16[2,32,128]{2,1,0:T(8,128)(2,1)S(1)}, bf16[2,32,128]{2,1,0:T(8,128)(2,1)S(1)}, u32[]{:S(2)}, u32[]{:S(2)}) collective-permute-start(bf16[2,32,128]{2,1,0:T(8,128)(2,1)S(1)} %get-tuple-element.38), channel_id=1, source_target_pairs={{0,8},{1,9},{2,10},{3,11},{4,12},{5,13},{6,14},{7,15},{8,0},{9,1},... | collective-permute-start | bytes 49160 | tf_op jit(solution)/shard_map/ppermute | solution.py:462
  33.0 0.9 collective-permute-done.7
  34.9 1.4 %collective-permute-start.8 = (bf16[4,2,32,128]{3,2,1,0:T(8,128)(2,1)S(1)}, bf16[4,2,32,128]{3,2,1,0:T(8,128)(2,1)S(1)}, u32[]{:S(2)}, u32[]{:S(2)}) collective-permute-start(bf16[4,2,32,128]{3,2,1,0:T(8,128)(2,1)S(1)} %pad_maximum_fusion.1.z0), channel_id=1, source_target_pairs={{0,32},{1,33},{2,34},{3,35},{4,36},{5,37},{6,38},{7,39},{8,40},{9,... | collective-permute-start | bytes 196616 | tf_op jit(solution)/shard_map/ppermute | solution.py:462
  36.3 4.8 %collective-permute-start.9 = (bf16[4,2,32,128]{3,2,1,0:T(8,128)(2,1)S(1)}, bf16[4,2,32,128]{3,2,1,0:T(8,128)(2,1)S(1)}, u32[]{:S(2)}, u32[]{:S(2)}) collective-permute-start(bf16[4,2,32,128]{3,2,1,0:T(8,128)(2,1)S(1)} %pad_maximum_fusion.1.z0), channel_id=1, source_target_pairs={{0,64},{1,65},{2,66},{3,67},{4,68},{5,69},{6,70},{7,71},{8,72},{9,... | collective-permute-start | bytes 196616 | tf_op jit(solution)/shard_map/ppermute | solution.py:462
  41.1 3.0 %collective-permute-done.9.z2 = bf16[4,2,32,128]{3,2,1,0:T(8,128)(2,1)S(1)} collective-permute-done((bf16[4,2,32,128]{3,2,1,0:T(8,128)(2,1)S(1)}, bf16[4,2,32,128]{3,2,1,0:T(8,128)(2,1)S(1)}, u32[]{:S(2)}, u32[]{:S(2)}) %collective-permute-start.9) | collective-permute-done | bytes 65568 | tf_op jit(solution)/shard_map/ppermute | solution.py:462
  44.2 2.4 %collective-permute-done.10.z3 = bf16[4,2,32,128]{3,2,1,0:T(8,128)(2,1)S(1)} collective-permute-done((bf16[4,2,32,128]{3,2,1,0:T(8,128)(2,1)S(1)}, bf16[4,2,32,128]{3,2,1,0:T(8,128)(2,1)S(1)}, u32[]{:S(2)}, u32[]{:S(2)}) %collective-permute-start.10) | collective-permute-done | bytes 65568 | tf_op jit(solution)/shard_map/ppermute | solution.py:462
  46.6 1.2 %shard_map.102 = (bf16[3,2,32,128]{3,2,1,0:T(8,128)(2,1)S(1)}, bf16[3,2,32,128]{3,2,1,0:T(8,128)(2,1)S(1)}, bf16[2,32,128]{2,1,0:T(8,128)(2,1)S(1)}, bf16[5,32,1...) custom-call(s32[2]{0:T(128)S(1)} %pad_add_fusion.place, bf16[4,2,32,128]{3,2,1,0:T(8,128)(2,1)S(1)} %pad_maximum_fusion.1.z0, ...), custom_call_target="tpu_custom_call" | custom-call | tf_op jit(solution)/shard_map/pallas_call | solution.py:32
  48.2 2.6 %collective-permute-start.13 = (bf16[5,32,128]{2,1,0:T(8,128)(2,1)S(1)}, bf16[5,32,128]{2,1,0:T(8,128)(2,1)S(1)}, u32[]{:S(2)}, u32[]{:S(2)}) collective-permute-start(bf16[5,32,128]{2,1,0:T(8,128)(2,1)S(1)} %get-tuple-element.27), channel_id=1, source_target_pairs={{0,6},{1,7},{2,4},{3,5},{4,2},{5,3},{6,0},{7,1},{8,14},{9,15},{10,... | collective-permute-start | bytes 122888 | tf_op jit(solution)/shard_map/ppermute | solution.py:462
  50.8 1.4 %collective-permute-start.12 = (bf16[2,32,128]{2,1,0:T(8,128)(2,1)S(1)}, bf16[2,32,128]{2,1,0:T(8,128)(2,1)S(1)}, u32[]{:S(2)}, u32[]{:S(2)}) collective-permute-start(bf16[2,32,128]{2,1,0:T(8,128)(2,1)S(1)} %get-tuple-element.25.p5), channel_id=1, source_target_pairs={{0,4},{1,5},{2,6},{3,7},{4,0},{5,1},{6,2},{7,3},{8,12},{9,13},{10,... | collective-permute-start | bytes 49160 | tf_op jit(solution)/shard_map/ppermute | solution.py:462
  52.9 8.1 %shard_map.103.f1 = bf16[10,14,32,256]{3,2,1,0:T(8,128)(2,1)S(1)} custom-call(s32[2]{0:T(128)S(1)} %pad_add_fusion.place, bf16[8,16,256]{2,1,0:T(8,128)(2,1)S(1)} %copy-done.3, bf16[8,16,256]{2,1,0:T(8,128)(2,1)S(1)} %collective-permute-done.row_a, bf16[8,16,256]{2,1,0:T(8,128)(2,1)S(1)} %collective-permute-done.1.row_b, ...), custom_call_target="tpu_custom_call" | custom-call | tf_op jit(solution)/shard_map/pallas_call | solution.py:32
  61.0 6.6 %shard_map.104.f3 = bf16[8,12,32,256]{3,2,1,0:T(8,128)(2,1)S(1)} custom-call(bf16[10,14,32,256]{3,2,1,0:T(8,128)(2,1)S(1)} %shard_map.103.f1, bf16[3,1024,256]{2,1,0:T(8,128)(2,1)S(1)} %get-tuple-element.20.wq), custom_call_target="tpu_custom_call" | custom-call | tf_op jit(solution)/shard_map/pallas_call | solution.py:32
  67.6 3.6 %shard_map.105 = (bf16[8,12,32,128]{3,2,1,0:T(8,128)(2,1)S(1)}, bf16[4,6,32,128]{3,2,1,0:T(8,128)(2,1)S(1)}) custom-call(bf16[8,12,32,256]{3,2,1,0:T(8,128)(2,1)S(1)} %shard_map.104.f3, bf16[256,256]{1,0:T(8,128)(2,1)S(1)} %copy-done.1, bf16[256,128]{1,0:T(8,128)(2,1)S(1)} %get-tuple-element.22.mo), custom_call_target="tpu_custom_call" | custom-call | tf_op jit(solution)/shard_map/pallas_call | solution.py:32
  71.2 18.8 %shard_map.107 = f32[32,8,64]{2,1,0:T(8,128)} custom-call(s32[2]{0:T(128)S(1)} %pad_add_fusion.place, s32[8,64]{1,0:T(8,128)S(1)} %bitcast.18, bf16[3,2,32,128]{3,2,1,0:T(8,128)(2,1)S(1)} %get-tuple-element.23.a3, bf16[3,2,32,128]{3,2,1,0:T(8,128)(2,1)S(1)} %get-tuple-element.24.a4, bf16[2,32,128]{2,1,0:T(8,128)(2,1)S(1)} %get-tuple-element.25.p5, ...), custom_call_target="tpu_custom_call" | custom-call | tf_op jit(solution)/shard_map/pallas_call | solution.py:32
  (43 shorter events, 3.7 us)
Async XLA Ops:
  0.0 10.3 %collective-permute-start = (bf16[8,16,256]{2,1,0:T(8,128)(2,1)}, bf16[8,16,256]{2,1,0:T(8,128)(2,1)S(1)}, u32[]{:S(2)}, u32[]{:S(2)}) collective-permute-start(bf16[8,16,256]{2,1,0:T(8,128)(2,1)} %own.3), channel_id=1, source_target_pairs={{0,8},{1,9},{2,10},{3,11},{4,12},{5,13},{6,14},{7,15},{8,0},{9,1},... | collective-permute-start | bytes 196616 | tf_op jit(solution)/shard_map/ppermute | solution.py:462
  1.7 8.6 %collective-permute-start.1 = (bf16[8,16,256]{2,1,0:T(8,128)(2,1)}, bf16[8,16,256]{2,1,0:T(8,128)(2,1)S(1)}, u32[]{:S(2)}, u32[]{:S(2)}) collective-permute-start(bf16[8,16,256]{2,1,0:T(8,128)(2,1)} %own.3), channel_id=1, source_target_pairs={{0,120},{1,121},{2,122},{3,123},{4,124},{5,125},{6,126},{7,127},{8... | collective-permute-start | bytes 196616 | tf_op jit(solution)/shard_map/ppermute | solution.py:462
  8.2 1.0 %copy-start.5 = (bf16[3,9,64,64]{3,2,1,0:T(8,128)(2,1)S(1)}, bf16[3,9,64,64]{3,2,1,0:T(8,128)(2,1)}, u32[]{:S(2)}) copy-start(bf16[3,9,64,64]{3,2,1,0:T(8,128)(2,1)} %w_up.1) | copy-start | bytes 663556
  11.2 41.0 %copy-start.9 = (bf16[256,64]{0,1:T(8,128)(2,1)S(1)}, bf16[256,64]{0,1:T(8,128)(2,1)}, u32[]{:S(2)}) copy-start(bf16[256,64]{0,1:T(8,128)(2,1)} %param.16) | copy-start | bytes 98308
  11.2 3.0 %collective-permute-start.2 = (bf16[3,8,8,256]{3,2,1,0:T(8,128)(2,1)S(1)}, bf16[3,8,8,256]{3,2,1,0:T(8,128)(2,1)S(1)}, u32[]{:S(2)}, u32[]{:S(2)}) collective-permute-start(bf16[3,8,8,256]{3,2,1,0:T(8,128)(2,1)S(1)} %get-tuple-element.36), channel_id=1, source_target_pairs={{0,1},{1,0},{2,3},{3,2},{4,5},{5,4},{6,7},{7,6},{8,9},{9,8},{10,11... | collective-permute-start | bytes 294920 | tf_op jit(solution)/shard_map/ppermute | solution.py:462
  11.3 5.3 %collective-permute-start.3 = (bf16[3,8,8,256]{3,2,1,0:T(8,128)(2,1)S(1)}, bf16[3,8,8,256]{3,2,1,0:T(8,128)(2,1)S(1)}, u32[]{:S(2)}, u32[]{:S(2)}) collective-permute-start(bf16[3,8,8,256]{3,2,1,0:T(8,128)(2,1)S(1)} %get-tuple-element.35), channel_id=1, source_target_pairs={{0,7},{1,2},{2,1},{3,4},{4,3},{5,6},{6,5},{7,0},{8,15},{9,10},{10,... | collective-permute-start | bytes 294920 | tf_op jit(solution)/shard_map/ppermute | solution.py:462
  16.6 0.9 %copy-start = (bf16[256,256]{1,0:T(8,128)(2,1)S(1)}, bf16[256,256]{1,0:T(8,128)(2,1)}, u32[]{:S(2)}) copy-start(bf16[256,256]{1,0:T(8,128)(2,1)} %merge_in.7) | copy-start | bytes 393220
  17.5 0.8 copy-start.2
  18.4 33.9 %copy-start.10 = (bf16[64,4]{0,1:T(4,128)(2,1)S(1)}, bf16[64,4]{0,1:T(4,128)(2,1)}, u32[]{:S(2)}) copy-start(bf16[64,4]{0,1:T(4,128)(2,1)} %param.18) | copy-start | bytes 1540
  18.4 34.0 %copy-start.4 = (bf16[3,9,64,64]{3,2,1,0:T(8,128)(2,1)S(1)}, bf16[3,9,64,64]{3,2,1,0:T(8,128)(2,1)}, u32[]{:S(2)}) copy-start(bf16[3,9,64,64]{3,2,1,0:T(8,128)(2,1)} %w_down.1) | copy-start | bytes 663556
  18.4 34.0 %copy-start.6 = (bf16[128,256]{1,0:T(8,128)(2,1)S(1)}, bf16[128,256]{1,0:T(8,128)(2,1)}, u32[]{:S(2)}) copy-start(bf16[128,256]{1,0:T(8,128)(2,1)} %down_in.3) | copy-start | bytes 196612
  18.4 34.5 %copy-start.3 = (bf16[8,16,256]{2,1,0:T(8,128)(2,1)S(1)}, bf16[8,16,256]{2,1,0:T(8,128)(2,1)}, u32[]{:S(2)}) copy-start(bf16[8,16,256]{2,1,0:T(8,128)(2,1)} %own.3) | copy-start | bytes 196612
  27.7 1.3 %collective-permute-start.4 = (bf16[32,128]{1,0:T(8,128)(2,1)S(1)}, bf16[32,128]{1,0:T(8,128)(2,1)S(1)}, u32[]{:S(2)}, u32[]{:S(2)}) collective-permute-start(bf16[32,128]{1,0:T(8,128)(2,1)S(1)} %shard_map.101), channel_id=1, source_target_pairs={{0,1},{1,0},{2,3},{3,2},{4,5},{5,4},{6,7},{7,6},{8,9},{9,8},{10,11... | collective-permute-start | bytes 24584 | tf_op jit(solution)/shard_map/ppermute | solution.py:462
  28.9 4.9 %collective-permute-start.7 = (bf16[2,32,128]{2,1,0:T(8,128)(2,1)S(1)}, bf16[2,32,128]{2,1,0:T(8,128)(2,1)S(1)}, u32[]{:S(2)}, u32[]{:S(2)}) collective-permute-start(bf16[2,32,128]{2,1,0:T(8,128)(2,1)S(1)} %get-tuple-element.38), channel_id=1, source_target_pairs={{0,24},{1,25},{2,26},{3,27},{4,28},{5,29},{6,30},{7,31},{8,16},{9,... | collective-permute-start | bytes 49160 | tf_op jit(solution)/shard_map/ppermute | solution.py:462
  29.1 5.4 %collective-permute-start.6 = (bf16[2,32,128]{2,1,0:T(8,128)(2,1)S(1)}, bf16[2,32,128]{2,1,0:T(8,128)(2,1)S(1)}, u32[]{:S(2)}, u32[]{:S(2)}) collective-permute-start(bf16[2,32,128]{2,1,0:T(8,128)(2,1)S(1)} %get-tuple-element.38), channel_id=1, source_target_pairs={{0,16},{1,17},{2,18},{3,19},{4,20},{5,21},{6,22},{7,23},{8,24},{9,... | collective-permute-start | bytes 49160 | tf_op jit(solution)/shard_map/ppermute | solution.py:462
  29.1 5.9 %collective-permute-start.5 = (bf16[2,32,128]{2,1,0:T(8,128)(2,1)S(1)}, bf16[2,32,128]{2,1,0:T(8,128)(2,1)S(1)}, u32[]{:S(2)}, u32[]{:S(2)}) collective-permute-start(bf16[2,32,128]{2,1,0:T(8,128)(2,1)S(1)} %get-tuple-element.38), channel_id=1, source_target_pairs={{0,8},{1,9},{2,10},{3,11},{4,12},{5,13},{6,14},{7,15},{8,0},{9,1},... | collective-permute-start | bytes 49160 | tf_op jit(solution)/shard_map/ppermute | solution.py:462
  34.9 6.2 %collective-permute-start.8 = (bf16[4,2,32,128]{3,2,1,0:T(8,128)(2,1)S(1)}, bf16[4,2,32,128]{3,2,1,0:T(8,128)(2,1)S(1)}, u32[]{:S(2)}, u32[]{:S(2)}) collective-permute-start(bf16[4,2,32,128]{3,2,1,0:T(8,128)(2,1)S(1)} %pad_maximum_fusion.1.z0), channel_id=1, source_target_pairs={{0,32},{1,33},{2,34},{3,35},{4,36},{5,37},{6,38},{7,39},{8,40},{9,... | collective-permute-start | bytes 196616 | tf_op jit(solution)/shard_map/ppermute | solution.py:462
  36.3 7.8 %collective-permute-start.9 = (bf16[4,2,32,128]{3,2,1,0:T(8,128)(2,1)S(1)}, bf16[4,2,32,128]{3,2,1,0:T(8,128)(2,1)S(1)}, u32[]{:S(2)}, u32[]{:S(2)}) collective-permute-start(bf16[4,2,32,128]{3,2,1,0:T(8,128)(2,1)S(1)} %pad_maximum_fusion.1.z0), channel_id=1, source_target_pairs={{0,64},{1,65},{2,66},{3,67},{4,68},{5,69},{6,70},{7,71},{8,72},{9,... | collective-permute-start | bytes 196616 | tf_op jit(solution)/shard_map/ppermute | solution.py:462
  41.1 5.5 %collective-permute-start.10 = (bf16[4,2,32,128]{3,2,1,0:T(8,128)(2,1)S(1)}, bf16[4,2,32,128]{3,2,1,0:T(8,128)(2,1)S(1)}, u32[]{:S(2)}, u32[]{:S(2)}) collective-permute-start(bf16[4,2,32,128]{3,2,1,0:T(8,128)(2,1)S(1)} %pad_maximum_fusion.1.z0), channel_id=1, source_target_pairs={{0,96},{1,97},{2,98},{3,99},{4,100},{5,101},{6,102},{7,103},{8,104... | collective-permute-start | bytes 196616 | tf_op jit(solution)/shard_map/ppermute | solution.py:462
  47.8 23.4 %collective-permute-start.11 = (bf16[5,32,128]{2,1,0:T(8,128)(2,1)S(1)}, bf16[5,32,128]{2,1,0:T(8,128)(2,1)S(1)}, u32[]{:S(2)}, u32[]{:S(2)}) collective-permute-start(bf16[5,32,128]{2,1,0:T(8,128)(2,1)S(1)} %get-tuple-element.26), channel_id=1, source_target_pairs={{0,2},{1,3},{2,0},{3,1},{4,6},{5,7},{6,4},{7,5},{8,10},{9,11},{10,... | collective-permute-start | bytes 122888 | tf_op jit(solution)/shard_map/ppermute | solution.py:462
  48.2 22.9 %collective-permute-start.13 = (bf16[5,32,128]{2,1,0:T(8,128)(2,1)S(1)}, bf16[5,32,128]{2,1,0:T(8,128)(2,1)S(1)}, u32[]{:S(2)}, u32[]{:S(2)}) collective-permute-start(bf16[5,32,128]{2,1,0:T(8,128)(2,1)S(1)} %get-tuple-element.27), channel_id=1, source_target_pairs={{0,6},{1,7},{2,4},{3,5},{4,2},{5,3},{6,0},{7,1},{8,14},{9,15},{10,... | collective-permute-start | bytes 122888 | tf_op jit(solution)/shard_map/ppermute | solution.py:462
  50.8 20.3 %collective-permute-start.12 = (bf16[2,32,128]{2,1,0:T(8,128)(2,1)S(1)}, bf16[2,32,128]{2,1,0:T(8,128)(2,1)S(1)}, u32[]{:S(2)}, u32[]{:S(2)}) collective-permute-start(bf16[2,32,128]{2,1,0:T(8,128)(2,1)S(1)} %get-tuple-element.25.p5), channel_id=1, source_target_pairs={{0,4},{1,5},{2,6},{3,7},{4,0},{5,1},{6,2},{7,3},{8,12},{9,13},{10,... | collective-permute-start | bytes 49160 | tf_op jit(solution)/shard_map/ppermute | solution.py:462
  61.0 6.6 %copy-start.1 = (bf16[256,256]{1,0:T(8,128)(2,1)S(1)}, bf16[256,256]{1,0:T(8,128)(2,1)}, u32[]{:S(2)}) copy-start(bf16[256,256]{1,0:T(8,128)(2,1)} %merge_in.7) | copy-start | bytes 393220
  67.6 3.6 %copy-start.7 = (s32[8,1,64]{2,1,0:T(1,128)S(1)}, s32[8,1,64]{2,1,0:T(1,128)}, u32[]{:S(2)}) copy-start(s32[8,1,64]{2,1,0:T(1,128)} %param.19) | copy-start | bytes 6148
  (1 other events, 0.7 us)
where the time goes:
time: 90.4 us; the launch traced here: 90 us
  Pallas kernels  48.3 us (53%)
  starting transfers between devices  25 us (28%)
  waiting for transfers between devices  10.9 us (12%)
  local copies, waits for them, and re-layouts  4.55 us (5%)
  other arithmetic  0.98 us (1%)
    pallas_call x8, Pallas kernels, whole_call(): pl.pallas_call(body, out_shape=out_shapes, in_specs=specs, out_specs=jax....  48.3 us
    ppermute x14, starting transfers between devices, swap(): return lax.ppermute(value, ('row', 'col'), pairs)  25 us
    ppermute x14, waiting for transfers between devices, swap(): return lax.ppermute(value, ('row', 'col'), pairs)  10.9 us
    unnamed x24, local copies, waits for them, and re-layouts  4.45 us
  transfers between devices with their start and end apart: 14, of which 7 were waited for; matrix products, arithmetic and copies ran while one was open for 1% of the time, Pallas kernels for 21%

commit v1 on v0

--- a/solution.py
+++ b/solution.py
@@ -24,9 +24,11 @@
     return lax.broadcasted_iota(jnp.int32, shape, len(shape) - 1) < 64
 
 
-def whole_call(body, out_shapes, scratch, args, smem=()):
+def whole_call(body, out_shapes, scratch, args, smem=(), outside=()):
     specs = [
-        pl.BlockSpec(memory_space=pltpu.SMEM) if i in smem else pl.BlockSpec(memory_space=pltpu.VMEM)
+        pl.BlockSpec(
+            memory_space=pltpu.SMEM if i in smem else pltpu.HBM if i in outside else pltpu.VMEM
+        )
         for i in range(len(args))
     ]
     return pl.pallas_call(
@@ -71,10 +73,40 @@
                         )
 
 
-def prep_up_body(w_up, w_embed, merge_out, wq, we, mo):
+def dot_rows(left, right):
+    return lax.dot_general(left, right, (((0,), (0,)), ((), ())), preferred_element_type=f32)
+
+
+def lane_copies(first, second):
+    row = lax.broadcasted_iota(jnp.int32, (64, 128), 0)
+    lane = lax.broadcasted_iota(jnp.int32, (64, 128), 1)
+    kept = jnp.where(lane < 64, first, second) > 0
+    return jnp.where(kept & (row == lane % 64), 1.0, 0.0).astype(bf16)
+
+
+def copies_in(sems, *pairs):
+    copies = [pltpu.make_async_copy(src, dst, sems.at[i]) for i, (src, dst) in enumerate(pairs)]
+    for copy in copies:
+        copy.start()
+    return copies
+
+
+def prep_up_body(
+    own, w_up, w_embed, merge_in, merge_out_t, own_out, wq, we, mi, mo, w_up_s, w_embed_s, mo_s, sems
+):
+    copies = copies_in(
+        sems,
+        (w_up, w_up_s),
+        (w_embed, w_embed_s),
+        (merge_out_t, mo_s),
+        (own, own_out),
+        (merge_in, mi),
+    )
+    copies[0].wait()
     for layer in range(3):
-        fill_quad_weights(w_up, wq, layer, layer % 2 == 0)
-    tiled = jnp.concatenate([w_embed[...].astype(f32)] * 16, axis=0)
+        fill_quad_weights(w_up_s, wq, layer, layer % 2 == 0)
+    copies[1].wait()
+    tiled = jnp.concatenate([w_embed_s[...].astype(f32)] * 16, axis=0)
     none = jnp.zeros((128, 64), f32)
     for a in range(2):
         for b in range(2):
@@ -86,15 +118,38 @@
             we[q * 128 : q * 128 + 128, (1 - a) * 128 : (1 - a) * 128 + 128] = jnp.zeros(
                 (128, 128), bf16
             )
-    mo[...] = jnp.concatenate([merge_out[...], merge_out[...]], axis=1)
-
-
-def prep_down_body(w_down, down_in, down_out, head_tiled, wq, di0, do0, do, wh):
+    copies[2].wait()
+    mo[...] = dot_rows(mo_s[...], lane_copies(1, 1)).astype(bf16)
+    copies[3].wait()
+    copies[4].wait()
+
+
+def prep_down_body(
+    w_down,
+    down_in,
+    down_out_t,
+    w_head_t,
+    wq,
+    di,
+    di0,
+    do0,
+    do,
+    wh,
+    w_down_s,
+    do_s,
+    head_s,
+    sems,
+):
+    copies = copies_in(
+        sems, (w_down, w_down_s), (down_in, di), (down_out_t, do_s), (w_head_t, head_s)
+    )
+    copies[0].wait()
     for layer in range(3):
-        fill_quad_weights(w_down, wq, layer, layer % 2 == 1)
+        fill_quad_weights(w_down_s, wq, layer, layer % 2 == 0)
+    copies[1].wait()
     zero = jnp.zeros((64, 256), bf16)
-    parent = down_in[0:64, :]
-    child = down_in[64:128, :]
+    parent = di[0:64, :]
+    child = di[64:128, :]
     di0[0:64, 0:256] = child
     di0[0:64, 256:512] = zero
     di0[64:128, 0:256] = zero
@@ -103,30 +158,28 @@
     di0[128:192, 256:512] = parent
     di0[192:256, 0:256] = zero
     di0[192:256, 256:512] = zero
-    back = down_out[...]
-    none = jnp.zeros((256, 64), bf16)
-    do0[0:256, :] = jnp.concatenate([back, none], axis=1)
-    do0[256:512, :] = jnp.concatenate([none, back], axis=1)
-    do[...] = jnp.concatenate([back, back], axis=1)
+    copies[2].wait()
+    back = do_s[...]
+    do0[0:256, :] = dot_rows(back, lane_copies(1, 0)).astype(bf16)
+    do0[256:512, :] = dot_rows(back, lane_copies(0, 1)).astype(bf16)
+    do[...] = dot_rows(back, lane_copies(1, 1)).astype(bf16)
+    copies[3].wait()
+    output = lax.broadcasted_iota(jnp.int32, (4, 128), 0)
+    lane = lax.broadcasted_iota(jnp.int32, (4, 128), 1)
+    head = dot_rows(head_s[...], jnp.where(lane % 4 == output, 1.0, 0.0).astype(bf16))
     lane = lax.broadcasted_iota(jnp.int32, (64, 128), 1)
-    head = head_tiled[...].astype(f32)
-    for quad in range(9):
+    for quad in range(8):
         for a in range(2):
             for b in range(2):
                 base = quad * 256 + (a * 2 + b) * 64
-                column = 2 * quad - b
-                if 0 <= column < 16:
-                    first = a * 64 + 4 * column
-                    kept = jnp.where((lane >= first) & (lane < first + 4), head, 0.0)
-                else:
-                    kept = jnp.zeros((64, 128), f32)
+                first = a * 64 + 4 * (2 * quad + b)
+                kept = jnp.where((lane >= first) & (lane < first + 4), head, 0.0)
                 wh[base : base + 64, :] = kept.astype(bf16)
 
 
 def conv_layer(src, dst, weights, rows, cols, to_odd):
     low = low_half((cols, samples, 128))
-
-    def step(i, carry):
+    for i in range(rows):
         here = src[i, 0:cols]
         right = src[i, 1 : cols + 1]
         below = src[i + 1, 0:cols]
@@ -142,52 +195,47 @@
             old1 = jnp.where(low, below[..., 128:256], corner[..., 128:256])
         dst[i, :, :, 0:128] = (old0.astype(f32) + update[..., 0:128]).astype(bf16)
         dst[i, :, :, 128:256] = (old1.astype(f32) + update[..., 128:256]).astype(bf16)
-        return carry
-
-    lax.fori_loop(0, rows, step, 0)
-
-
-def spread_tiles(place, own, row_a, row_b, col_a, col_b, ext):
+
+
+def spread_tiles(place, tiles, col_a, col_b, ext):
     row_even = place[0] % 2 == 0
     col_even = place[1] % 2 == 0
     after_row = jnp.where(row_even, 16, 0)
     before_row = jnp.where(row_even, 0, 16)
     after_col = jnp.where(col_even, 3, 0)
     before_col = jnp.where(col_even, 0, 3)
-    for tile, ref, start in ((0, own, 8), (1, row_a, after_row), (2, row_b, before_row)):
-        cells = ref[...].astype(f32)
+    for tile, start in ((0, 8), (1, after_row), (2, before_row)):
+        cells = tiles[tile].astype(f32)
         ext[pl.ds(start, 8), 1] = cells[:, 0:8]
         ext[pl.ds(start, 8), 2] = cells[:, 8:16]
         ext[pl.ds(start, 8), after_col] = col_a[tile].astype(f32)
         ext[pl.ds(start, 8), before_col] = col_b[tile].astype(f32)
 
 
-def embed_quads(ext, we, lhs, dst, halo):
+def embed_quads(ext, we, dst, halo):
     rows = 4 + halo
     cols = 8 + halo
     first = 8 - halo
     sub = lax.broadcasted_iota(jnp.int32, (16, 128), 0)
     lane = lax.broadcasted_iota(jnp.int32, (16, 128), 1)
     own_lanes = (lane // 8 == sub).astype(f32)
-
-    def step(i, carry):
+    for i in range(rows):
+        quads = []
         for quad in range(cols):
+            parts = []
             for a in range(2):
                 row = first + 2 * i + (1 - a)
                 for b in range(2):
                     col = first + 2 * quad + (1 - b)
                     cell = ext[row, col // 8, col % 8 : col % 8 + 1, :]
-                    for half in range(2):
-                        part = cell[:, half * 128 : half * 128 + 128]
-                        spread = jnp.broadcast_to(part, (16, 128)) * own_lanes
-                        start = quad * 32 + half * 16
-                        q = 2 * a + b
-                        lhs[start : start + 16, q * 128 : q * 128 + 128] = spread.astype(bf16)
-        embedded = dot(lhs[...], we[...]).astype(bf16)
+                    halves = [
+                        jnp.broadcast_to(cell[:, k : k + 128], (16, 128)) * own_lanes
+                        for k in (0, 128)
+                    ]
+                    parts.append(jnp.concatenate(halves, axis=0).astype(bf16))
+            quads.append(jnp.concatenate(parts, axis=-1))
+        embedded = dot(jnp.concatenate(quads, axis=0), we[...]).astype(bf16)
         dst[i] = embedded.reshape(cols, samples, 256)
-        return carry
-
-    lax.fori_loop(0, rows, step, 0)
 
 
 def merge_pair(top, bottom, merge_in, mo):
@@ -198,13 +246,10 @@
 
 
 def merge_quads(src, dst, merge_in, mo, rows, cols):
-    def step(i, carry):
+    for i in range(rows):
         stacked = src[i].reshape(cols * samples, 256)
         hidden = jnp.maximum(dot(stacked, merge_in[...]), 0.0).astype(bf16)
         dst[i] = dot(hidden, mo[...]).astype(bf16).reshape(cols, samples, 128)
-        return carry
-
-    lax.fori_loop(0, rows, step, 0)
 
 
 def paired_columns(cells):
@@ -214,11 +259,9 @@
     return jnp.where(low, split[:, 0], split[:, 1])
 
 
-def up_own_body(
-    place, own, row_a, row_b, col_a, col_b, wq, we, merge_in, mo, out, ext, lhs, f0, f1, f2, f3, l1
-):
-    spread_tiles(place, own, row_a, row_b, col_a, col_b, ext)
-    embed_quads(ext, we, lhs, f0, 3)
+def up_own_body(place, tiles, col_a, col_b, wq, we, merge_in, mo, out, ext, f0, f1, f2, f3, l1):
+    spread_tiles(place, tiles, col_a, col_b, ext)
+    embed_quads(ext, we, f0, 3)
     conv_layer(f0, f1, wq.at[0], 6, 10, False)
     conv_layer(f1, f2, wq.at[1], 5, 9, True)
     conv_layer(f2, f3, wq.at[2], 4, 8, False)
@@ -230,9 +273,9 @@
     out[...] = paired_columns(l3)[0]
 
 
-def up_wide_first_body(place, own, row_a, row_b, col_a, col_b, wq, we, f1, ext, lhs, f0):
-    spread_tiles(place, own, row_a, row_b, col_a, col_b, ext)
-    embed_quads(ext, we, lhs, f0, 7)
+def up_wide_first_body(place, tiles, col_a, col_b, wq, we, f1, ext, f0):
+    spread_tiles(place, tiles, col_a, col_b, ext)
+    embed_quads(ext, we, f0, 7)
     conv_layer(f0, f1, wq.at[0], 10, 14, False)
 
 
@@ -420,37 +463,37 @@
     lane = lax.broadcasted_iota(jnp.int32, (128, 128), 1)
     averager = jnp.where((sub < 64) == (lane < 64), 1.0 / 64, 0.0).astype(bf16)
 
-    def fine_row(i, carry):
+    low11 = low_half((11, samples, 128))
+    for i in range(8):
         parent = c2s[i // 2]
         parent = jnp.broadcast_to(parent[:, None], (6, 2, samples, 128)).reshape(12, samples, 128)
         c1 = refine(parent, l1[i], in_weights, out_weights)
         c1_wide = c1.astype(f32).reshape(12 * samples, 128)
         for a in range(2):
+            row_to = i - (1 - a)
+            if not 0 <= row_to < 7:
+                continue
             child = f3[i, :, :, a * 128 : a * 128 + 128]
             joined = jnp.concatenate([child, c1], axis=-1).reshape(12 * samples, 256)
             inner = jnp.maximum(dot(joined, di0[...]), 0.0).astype(bf16)
             fine = dot(inner, do0[...])
             fine = fine + child.astype(f32).reshape(12 * samples, 128) + c1_wide
             mean = dot((fine * fine).astype(bf16), averager)
-            normed = fine * lax.rsqrt(mean + norm_eps)
-            n0[i, :, :, a * 128 : a * 128 + 128] = normed.astype(bf16).reshape(12, samples, 128)
-        return carry
-
-    lax.fori_loop(0, 8, fine_row, 0)
-    conv_layer(n0, r1, wq.at[0], 7, 11, True)
-    conv_layer(r1, r2, wq.at[1], 6, 10, False)
-    conv_layer(r2, r3, wq.at[2], 5, 9, True)
+            normed = (fine * lax.rsqrt(mean + norm_eps)).astype(bf16).reshape(12, samples, 128)
+            n0[row_to, :, :, a * 128 : a * 128 + 128] = jnp.where(low11, normed[1:12], normed[0:11])
+    conv_layer(n0, r1, wq.at[0], 6, 10, False)
+    conv_layer(r1, r2, wq.at[1], 5, 9, True)
+    conv_layer(r2, r3, wq.at[2], 4, 8, False)
     stacked = jnp.concatenate(
-        [r3[:, quad].reshape(5 * samples, 256) for quad in range(9)], axis=-1
-    )
-    cell_logits = dot(stacked, wh[...]).reshape(5, samples, 128)
+        [r3[:, quad].reshape(4 * samples, 256) for quad in range(8)], axis=-1
+    )
+    cell_logits = dot(stacked, wh[...]).reshape(4, samples, 128)
     coarse = cell_logits.astype(bf16)
     rest = (cell_logits - coarse.astype(f32)).astype(bf16)
     places = lax.broadcasted_iota(jnp.int32, (128, 64), 0)
     for i in range(8):
-        quad_row = (i + 1) // 2
         chosen = (places == slots[i : i + 1, :] + 64 * (i % 2)).astype(bf16)
-        out[:, i, :] = dot(coarse[quad_row], chosen) + dot(rest[quad_row], chosen)
+        out[:, i, :] = dot(coarse[i // 2], chosen) + dot(rest[i // 2], chosen)
 
 
 def swap(value, partner):
@@ -480,32 +523,50 @@
 
     row_a = swap(readouts, lambda r, c: (pair_after(r, n_row), c))
     row_b = swap(readouts, lambda r, c: (pair_before(r, n_row), c))
-    tiles = jnp.stack([readouts, row_a, row_b])
+    own, wq_up, we, mi, mo = whole_call(
+        prep_up_body,
+        (
+            arr((8, 16, 256)),
+            arr((3, 1024, 256)),
+            arr((512, 256)),
+            arr((256, 256)),
+            arr((256, 128)),
+        ),
+        [
+            pltpu.VMEM((3, 9, 64, 64), bf16),
+            pltpu.VMEM((8, 64), bf16),
+            pltpu.VMEM((64, 256), bf16),
+            pltpu.SemaphoreType.DMA((5,)),
+        ],
+        (readouts, w_up, w_embed, merge_in, merge_out.T),
+        outside=(0, 1, 2, 3, 4),
+    )
+    tiles = jnp.stack([own, row_a, row_b])
     left = tiles[:, :, 0:8]
     right = tiles[:, :, 8:16]
     col_a = swap(jnp.where(col_even, right, left), lambda r, c: (r, pair_after(c, n_col)))
     col_b = swap(jnp.where(col_even, left, right), lambda r, c: (r, pair_before(c, n_col)))
-
-    wq_up, we, mo = whole_call(
-        prep_up_body,
-        (arr((3, 1024, 256)), arr((512, 256)), arr((256, 128))),
-        [],
-        (w_up, w_embed, merge_out),
-    )
-    wq_down, di0, do0, do, wh = whole_call(
+    w_down, tiles = lax.optimization_barrier((w_down, tiles))
+    wq_down, di, di0, do0, do, wh = whole_call(
         prep_down_body,
         (
             arr((3, 1024, 256)),
+            arr((128, 256)),
             arr((256, 512)),
             arr((512, 128)),
             arr((256, 128)),
-            arr((2304, 128)),
+            arr((2048, 128)),
         ),
-        [],
-        (w_down, down_in, down_out, jnp.tile(w_head, (1, 32))),
-    )
-
-    tile_args = (place, readouts, row_a, row_b, col_a, col_b)
+        [
+            pltpu.VMEM((3, 9, 64, 64), bf16),
+            pltpu.VMEM((64, 256), bf16),
+            pltpu.VMEM((4, 64), bf16),
+            pltpu.SemaphoreType.DMA((4,)),
+        ],
+        (w_down, down_in, down_out.T, w_head.T),
+        outside=(0, 1, 2, 3),
+    )
+
     quads = lambda rows, cols: pltpu.VMEM((rows, cols, samples, 256), bf16)
     ext = pltpu.VMEM((24, 4, 8, 256), f32)
     l3 = whole_call(
@@ -513,30 +574,32 @@
         arr((samples, 128)),
         [
             ext,
-            pltpu.VMEM((11 * samples, 512), bf16),
             quads(7, 11),
             quads(6, 10),
             quads(5, 9),
             quads(4, 8),
             pltpu.VMEM((4, 8, samples, 128), bf16),
         ],
-        (*tile_args, wq_up, we, merge_in, mo),
+        (place, tiles, col_a, col_b, wq_up, we, mi, mo),
         smem=(0,),
     )
 
     pair = jnp.stack([l3, swap(l3, lambda r, c: (r, c ^ 1))])
     four = jnp.stack([pair] + [swap(pair, lambda r, c, m=m: (r ^ m, c)) for m in (1, 2, 3)])
+    col_a, pair = lax.optimization_barrier((col_a, pair))
     f1 = whole_call(
         up_wide_first_body,
         arr((10, 14, samples, 256)),
-        [ext, pltpu.VMEM((15 * samples, 512), bf16), quads(11, 15)],
-        (*tile_args, wq_up, we),
+        [ext, quads(11, 15)],
+        (place, tiles, col_a, col_b, wq_up, we),
         smem=(0,),
     )
+    four, f1 = lax.optimization_barrier((four, f1))
     strips = [four] + [swap(four, lambda r, c, m=m: (r ^ (4 * m), c)) for m in (1, 2, 3)]
     f3 = whole_call(
         up_wide_second_body, arr((8, 12, samples, 256)), [quads(9, 13)], (f1, wq_up)
     )
+    strips[3], f3 = lax.optimization_barrier((strips[3], f3))
     a3, a4, p5, send1, send3 = whole_call(
         mid_body,
         (
@@ -547,7 +610,7 @@
             arr((5, samples, 128)),
         ),
         [pltpu.VMEM((4, 4, 2, samples, 128), bf16), pltpu.VMEM((8, 2, samples, 128), bf16)],
-        (place, *strips, merge_in, mo),
+        (place, *strips, mi, mo),
         smem=(0,),
     )
     q1 = swap(send1, lambda r, c: (r, c ^ 2))
@@ -557,7 +620,7 @@
         up_wide_merge_body,
         (arr((8, 12, samples, 128)), arr((4, 6, samples, 128))),
         [],
-        (f3, merge_in, mo),
+        (f3, mi, mo),
     )
     slots = qubit_slot.reshape(qubit_slot.shape[0], qubit_slot.shape[2])
     return whole_call(
@@ -569,10 +632,10 @@
             pltpu.VMEM((6, 3, samples, 128), bf16),
             pltpu.VMEM((6, 3, samples, 128), bf16),
             pltpu.VMEM((4, 6, samples, 128), bf16),
-            quads(8, 12),
             quads(7, 11),
             quads(6, 10),
             quads(5, 9),
+            quads(4, 8),
         ],
         (
             place,
@@ -586,9 +649,9 @@
             f3,
             l1,
             l2,
-            merge_in,
+            mi,
             mo,
-            down_in,
+            di,
             do,
             di0,
             do0,

time: 90.4 us -> 63 us (0.70)
  Pallas kernels: 48.3 us -> 31.4 us
  waiting for transfers between devices: 10.9 us -> 5.29 us
  starting transfers between devices: 25 us -> 21.1 us
    pallas_call x8, Pallas kernels: 48.3 us -> 31.4 us  [whole_call(): pl.pallas_call(body, out_shape=out_shapes, in_specs=specs, out_specs=jax....]
    ppermute x14, waiting for transfers between devices: 10.9 us -> 5.29 us  [swap(): return lax.ppermute(value, ('row', 'col'), pairs)]
    ppermute x14, starting transfers between devices: 25 us -> 21.1 us  [swap(): return lax.ppermute(value, ('row', 'col'), pairs)]
    unnamed x24 -> x20, local copies, waits for them, and re-layouts: 4.45 us -> 4.23 us
  transfers between devices with their start and end apart: 14 -> 14, of which waited for: 7 -> 3; matrix products, arithmetic and copies ran while one was open for 1% -> 0% of each run, Pallas kernels for 21% -> 21%
where the time goes in v1:
time: 63 us; the launch traced here: 62.3 us
  Pallas kernels  31.4 us (50%)
  starting transfers between devices  21.1 us (33%)
  waiting for transfers between devices  5.29 us (8%)
  local copies, waits for them, and re-layouts  4.23 us (7%)
    pallas_call x8, Pallas kernels, whole_call(): pl.pallas_call(body, out_shape=out_shapes, in_specs=specs, out_specs=jax....  31.4 us
    ppermute x14, starting transfers between devices, swap(): return lax.ppermute(value, ('row', 'col'), pairs)  21.1 us
    ppermute x14, waiting for transfers between devices, swap(): return lax.ppermute(value, ('row', 'col'), pairs)  5.29 us
    unnamed x20, local copies, waits for them, and re-layouts  4.23 us
  transfers between devices with their start and end apart: 14, of which 3 were waited for; matrix products, arithmetic and copies ran while one was open for 0% of the time, Pallas kernels for 21%

profile of v1, /device:TPU:0, one launch (start us, length us, event | category | flops | bytes accessed | tf_op | source)
XLA Modules:
  0.0 62.3 jit_solution(3807600004279349519)
XLA Ops:
  0.0 6.6 %collective-permute-start.1 = (bf16[8,16,256]{2,1,0:T(8,128)(2,1)}, bf16[8,16,256]{2,1,0:T(8,128)(2,1)S(1)}, u32[]{:S(2)}, u32[]{:S(2)}) collective-permute-start(bf16[8,16,256]{2,1,0:T(8,128)(2,1)} %own.1), channel_id=1, source_target_pairs={{0,120},{1,121},{2,122},{3,123},{4,124},{5,125},{6,126},{7,127},{8... | collective-permute-start | bytes 196616 | tf_op jit(solution)/shard_map/ppermute | solution.py:505
  6.6 1.0 %copy-done = bf16[3,9,64,64]{3,2,1,0:T(8,128)(2,1)S(1)} copy-done((bf16[3,9,64,64]{3,2,1,0:T(8,128)(2,1)S(1)}, bf16[3,9,64,64]{3,2,1,0:T(8,128)(2,1)}, u32[]{:S(2)}) %copy-start) | copy-done | bytes 221208
  7.6 0.9 %copy-done.2 = bf16[256,256]{1,0:T(8,128)(2,1)S(1)} copy-done((bf16[256,256]{1,0:T(8,128)(2,1)S(1)}, bf16[256,256]{1,0:T(8,128)(2,1)}, u32[]{:S(2)}) %copy-start.2) | copy-done | bytes 131096
  8.5 0.8 %copy-done.4 = bf16[8,16,256]{2,1,0:T(8,128)(2,1)S(1)} copy-done((bf16[8,16,256]{2,1,0:T(8,128)(2,1)S(1)}, bf16[8,16,256]{2,1,0:T(8,128)(2,1)}, u32[]{:S(2)}) %copy-start.4) | copy-done | bytes 65560
  9.3 0.8 %copy-done.6 = bf16[256,64]{0,1:T(8,128)(2,1)S(1)} copy-done((bf16[256,64]{0,1:T(8,128)(2,1)S(1)}, bf16[256,64]{0,1:T(8,128)(2,1)}, u32[]{:S(2)}) %copy-start.6) | copy-done | bytes 32792
  10.1 0.7 %copy-done.8 = bf16[8,64]{1,0:T(8,128)(2,1)S(1)} copy-done((bf16[8,64]{1,0:T(8,128)(2,1)S(1)}, bf16[8,64]{1,0:T(8,128)(2,1)}, u32[]{:S(2)}) %copy-start.8) | copy-done | bytes 1048
  10.8 1.2 %shard_map.100 = (bf16[8,16,256]{2,1,0:T(8,128)(2,1)S(1)}, bf16[3,1024,256]{2,1,0:T(8,128)(2,1)S(1)}, bf16[512,256]{1,0:T(8,128)(2,1)S(1)}, bf16[256,256]{1,0:T(8,128)(2,1)S(1)}, bf16[256,128]{1,0:T(8,128)(2,1)S(1)}) custom-call(bf16[8,16,256]{2,1,0:T(8,128)(2,1)S(1)} %copy-done.4, bf16[3,9,64,64]{3,2,1,0:T(8,128)(2,1)S(1)} %copy-done, ...), custom_call_target="tpu_custom_call" | custom-call | tf_op jit(solution)/shard_map/pallas_call | solution.py:34
  12.1 2.0 %collective-permute-start.3 = (bf16[3,8,8,256]{3,2,1,0:T(8,128)(2,1)S(1)}, bf16[3,8,8,256]{3,2,1,0:T(8,128)(2,1)S(1)}, u32[]{:S(2)}, u32[]{:S(2)}) collective-permute-start(bf16[3,8,8,256]{3,2,1,0:T(8,128)(2,1)S(1)} %get-tuple-element.55), channel_id=1, source_target_pairs={{0,7},{1,2},{2,1},{3,4},{4,3},{5,6},{6,5},{7,0},{8,15},{9,10},{10,... | collective-permute-start | bytes 294920 | tf_op jit(solution)/shard_map/ppermute | solution.py:505
  14.2 3.3 %collective-permute-done.3.col_b = bf16[3,8,8,256]{3,2,1,0:T(8,128)(2,1)S(1)} collective-permute-done((bf16[3,8,8,256]{3,2,1,0:T(8,128)(2,1)S(1)}, bf16[3,8,8,256]{3,2,1,0:T(8,128)(2,1)S(1)}, u32[]{:S(2)}, u32[]{:S(2)}) %collective-permute-start.3) | collective-permute-done | bytes 98336 | tf_op jit(solution)/shard_map/ppermute | solution.py:505
  17.4 4.6 %shard_map.101 = bf16[32,128]{1,0:T(8,128)(2,1)S(1)} custom-call(s32[2]{0:T(128)S(1)} %pad_add_fusion.place, bf16[3,8,16,256]{3,2,1,0:T(8,128)(2,1)S(1)} %pad_maximum_fusion.tiles, bf16[3,8,8,256]{3,2,1,0:T(8,128)(2,1)S(1)} %collective-permute-done.2.col_a, bf16[3,8,8,256]{3,2,1,0:T(8,128)(2,1)S(1)} %collective-permute-done.3.col_b, ...), custom_call_target="tpu_custom_call" | custom-call | tf_op jit(solution)/shard_map/pallas_call | solution.py:34
  22.2 1.2 %collective-permute-done.4 = bf16[32,128]{1,0:T(8,128)(2,1)S(1)} collective-permute-done((bf16[32,128]{1,0:T(8,128)(2,1)S(1)}, bf16[32,128]{1,0:T(8,128)(2,1)S(1)}, u32[]{:S(2)}, u32[]{:S(2)}) %collective-permute-start.4) | collective-permute-done | bytes 8224 | tf_op jit(solution)/shard_map/ppermute | solution.py:505
  23.3 4.1 %collective-permute-start.6 = (bf16[2,32,128]{2,1,0:T(8,128)(2,1)S(1)}, bf16[2,32,128]{2,1,0:T(8,128)(2,1)S(1)}, u32[]{:S(2)}, u32[]{:S(2)}) collective-permute-start(bf16[2,32,128]{2,1,0:T(8,128)(2,1)S(1)} %get-tuple-element.58), channel_id=1, source_target_pairs={{0,16},{1,17},{2,18},{3,19},{4,20},{5,21},{6,22},{7,23},{8,24},{9,... | collective-permute-start | bytes 49160 | tf_op jit(solution)/shard_map/ppermute | solution.py:505
  27.4 4.7 %shard_map.102.f1 = bf16[10,14,32,256]{3,2,1,0:T(8,128)(2,1)S(1)} custom-call(s32[2]{0:T(128)S(1)} %pad_add_fusion.place, bf16[3,8,16,256]{3,2,1,0:T(8,128)(2,1)S(1)} %pad_maximum_fusion.tiles, bf16[3,8,8,256]{3,2,1,0:T(8,128)(2,1)S(1)} %collective-permute-done.2.col_a, bf16[3,8,8,256]{3,2,1,0:T(8,128)(2,1)S(1)} %collective-permute-done.3.col_b, ...), custom_call_target="tpu_custom_call" | custom-call | tf_op jit(solution)/shard_map/pallas_call | solution.py:34
  32.2 0.8 %collective-permute-start.10 = (bf16[4,2,32,128]{3,2,1,0:T(8,128)(2,1)S(1)}, bf16[4,2,32,128]{3,2,1,0:T(8,128)(2,1)S(1)}, u32[]{:S(2)}, u32[]{:S(2)}) collective-permute-start(bf16[4,2,32,128]{3,2,1,0:T(8,128)(2,1)S(1)} %pad_maximum_fusion.1.z0), channel_id=1, source_target_pairs={{0,96},{1,97},{2,98},{3,99},{4,100},{5,101},{6,102},{7,103},{8,104... | collective-permute-start | bytes 196616 | tf_op jit(solution)/shard_map/ppermute | solution.py:505
  33.0 3.4 %collective-permute-start.8 = (bf16[4,2,32,128]{3,2,1,0:T(8,128)(2,1)S(1)}, bf16[4,2,32,128]{3,2,1,0:T(8,128)(2,1)S(1)}, u32[]{:S(2)}, u32[]{:S(2)}) collective-permute-start(bf16[4,2,32,128]{3,2,1,0:T(8,128)(2,1)S(1)} %pad_maximum_fusion.1.z0), channel_id=1, source_target_pairs={{0,32},{1,33},{2,34},{3,35},{4,36},{5,37},{6,38},{7,39},{8,40},{9,... | collective-permute-start | bytes 196616 | tf_op jit(solution)/shard_map/ppermute | solution.py:505
  36.4 4.2 %shard_map.103.f3 = bf16[8,12,32,256]{3,2,1,0:T(8,128)(2,1)S(1)} custom-call(bf16[10,14,32,256]{3,2,1,0:T(8,128)(2,1)S(1)} %shard_map.102.f1, bf16[3,1024,256]{2,1,0:T(8,128)(2,1)S(1)} %get-tuple-element.32.wq), custom_call_target="tpu_custom_call" | custom-call | tf_op jit(solution)/shard_map/pallas_call | solution.py:34
  40.7 1.2 %shard_map.104 = (bf16[3,2,32,128]{3,2,1,0:T(8,128)(2,1)S(1)}, bf16[3,2,32,128]{3,2,1,0:T(8,128)(2,1)S(1)}, bf16[2,32,128]{2,1,0:T(8,128)(2,1)S(1)}, bf16[5,32,1...) custom-call(s32[2]{0:T(128)S(1)} %pad_add_fusion.place, bf16[4,2,32,128]{3,2,1,0:T(8,128)(2,1)S(1)} %pad_maximum_fusion.1.z0, ...), custom_call_target="tpu_custom_call" | custom-call | tf_op jit(solution)/shard_map/pallas_call | solution.py:34
  41.9 0.4 collective-permute-start.11
  42.2 2.1 %collective-permute-start.13 = (bf16[5,32,128]{2,1,0:T(8,128)(2,1)S(1)}, bf16[5,32,128]{2,1,0:T(8,128)(2,1)S(1)}, u32[]{:S(2)}, u32[]{:S(2)}) collective-permute-start(bf16[5,32,128]{2,1,0:T(8,128)(2,1)S(1)} %get-tuple-element.44), channel_id=1, source_target_pairs={{0,6},{1,7},{2,4},{3,5},{4,2},{5,3},{6,0},{7,1},{8,14},{9,15},{10,... | collective-permute-start | bytes 122888 | tf_op jit(solution)/shard_map/ppermute | solution.py:505
  44.3 1.7 %collective-permute-start.12 = (bf16[2,32,128]{2,1,0:T(8,128)(2,1)S(1)}, bf16[2,32,128]{2,1,0:T(8,128)(2,1)S(1)}, u32[]{:S(2)}, u32[]{:S(2)}) collective-permute-start(bf16[2,32,128]{2,1,0:T(8,128)(2,1)S(1)} %get-tuple-element.42.p5), channel_id=1, source_target_pairs={{0,4},{1,5},{2,6},{3,7},{4,0},{5,1},{6,2},{7,3},{8,12},{9,13},{10,... | collective-permute-start | bytes 49160 | tf_op jit(solution)/shard_map/ppermute | solution.py:505
  46.0 1.3 %shard_map.106 = (bf16[3,1024,256]{2,1,0:T(8,128)(2,1)S(1)}, bf16[128,256]{1,0:T(8,128)(2,1)S(1)}, bf16[256,512]{1,0:T(8,128)(2,1)S(1)}, bf16[512,128]{1,0:T(8,1...) custom-call(bf16[3,9,64,64]{3,2,1,0:T(8,128)(2,1)S(1)} %copy-done.1, ...), custom_call_target="tpu_custom_call" | custom-call | tf_op jit(solution)/shard_map/pallas_call | solution.py:34
  47.3 1.4 %shard_map.105 = (bf16[8,12,32,128]{3,2,1,0:T(8,128)(2,1)S(1)}, bf16[4,6,32,128]{3,2,1,0:T(8,128)(2,1)S(1)}) custom-call(bf16[8,12,32,256]{3,2,1,0:T(8,128)(2,1)S(1)} %shard_map.103.f3, bf16[256,256]{1,0:T(8,128)(2,1)S(1)} %get-tuple-element.34.merge_in, bf16[256,128]{1,0:T(8,128)(2,1)S(1)} %get-tuple-element.35.mo), custom_call_target="tpu_custom_call" | custom-call | tf_op jit(solution)/shard_map/pallas_call | solution.py:34
  48.7 0.8 %collective-permute-done.12.q2 = bf16[2,32,128]{2,1,0:T(8,128)(2,1)S(1)} collective-permute-done((bf16[2,32,128]{2,1,0:T(8,128)(2,1)S(1)}, bf16[2,32,128]{2,1,0:T(8,128)(2,1)S(1)}, u32[]{:S(2)}, u32[]{:S(2)}) %collective-permute-start.12) | collective-permute-done | bytes 16416 | tf_op jit(solution)/shard_map/ppermute | solution.py:505
  49.6 12.7 %shard_map.107 = f32[32,8,64]{2,1,0:T(8,128)} custom-call(s32[2]{0:T(128)S(1)} %pad_add_fusion.place, s32[8,64]{1,0:T(8,128)S(1)} %bitcast.20, bf16[3,2,32,128]{3,2,1,0:T(8,128)(2,1)S(1)} %get-tuple-element.40.a3, bf16[3,2,32,128]{3,2,1,0:T(8,128)(2,1)S(1)} %get-tuple-element.41.a4, bf16[2,32,128]{2,1,0:T(8,128)(2,1)S(1)} %get-tuple-element.42.p5, ...), custom_call_target="tpu_custom_call" | custom-call | tf_op jit(solution)/shard_map/pallas_call | solution.py:34
  (37 shorter events, 0.3 us)
Async XLA Ops:
  0.0 12.0 %collective-permute-start.1 = (bf16[8,16,256]{2,1,0:T(8,128)(2,1)}, bf16[8,16,256]{2,1,0:T(8,128)(2,1)S(1)}, u32[]{:S(2)}, u32[]{:S(2)}) collective-permute-start(bf16[8,16,256]{2,1,0:T(8,128)(2,1)} %own.1), channel_id=1, source_target_pairs={{0,120},{1,121},{2,122},{3,123},{4,124},{5,125},{6,126},{7,127},{8... | collective-permute-start | bytes 196616 | tf_op jit(solution)/shard_map/ppermute | solution.py:505
  6.6 5.5 %collective-permute-start = (bf16[8,16,256]{2,1,0:T(8,128)(2,1)}, bf16[8,16,256]{2,1,0:T(8,128)(2,1)S(1)}, u32[]{:S(2)}, u32[]{:S(2)}) collective-permute-start(bf16[8,16,256]{2,1,0:T(8,128)(2,1)} %own.1), channel_id=1, source_target_pairs={{0,8},{1,9},{2,10},{3,11},{4,12},{5,13},{6,14},{7,15},{8,0},{9,1},... | collective-permute-start | bytes 196616 | tf_op jit(solution)/shard_map/ppermute | solution.py:505
  6.6 1.0 %copy-start = (bf16[3,9,64,64]{3,2,1,0:T(8,128)(2,1)S(1)}, bf16[3,9,64,64]{3,2,1,0:T(8,128)(2,1)}, u32[]{:S(2)}) copy-start(bf16[3,9,64,64]{3,2,1,0:T(8,128)(2,1)} %w_up.1) | copy-start | bytes 663556
  7.6 0.9 %copy-start.2 = (bf16[256,256]{1,0:T(8,128)(2,1)S(1)}, bf16[256,256]{1,0:T(8,128)(2,1)}, u32[]{:S(2)}) copy-start(bf16[256,256]{1,0:T(8,128)(2,1)} %merge_in.1) | copy-start | bytes 393220
  8.5 0.8 %copy-start.4 = (bf16[8,16,256]{2,1,0:T(8,128)(2,1)S(1)}, bf16[8,16,256]{2,1,0:T(8,128)(2,1)}, u32[]{:S(2)}) copy-start(bf16[8,16,256]{2,1,0:T(8,128)(2,1)} %own.1) | copy-start | bytes 196612
  9.3 0.8 %copy-start.6 = (bf16[256,64]{0,1:T(8,128)(2,1)S(1)}, bf16[256,64]{0,1:T(8,128)(2,1)}, u32[]{:S(2)}) copy-start(bf16[256,64]{0,1:T(8,128)(2,1)} %param.14) | copy-start | bytes 98308
  10.1 0.7 %copy-start.8 = (bf16[8,64]{1,0:T(8,128)(2,1)S(1)}, bf16[8,64]{1,0:T(8,128)(2,1)}, u32[]{:S(2)}) copy-start(bf16[8,64]{1,0:T(8,128)(2,1)} %w_embed.1) | copy-start | bytes 3076
  12.1 5.3 %collective-permute-start.3 = (bf16[3,8,8,256]{3,2,1,0:T(8,128)(2,1)S(1)}, bf16[3,8,8,256]{3,2,1,0:T(8,128)(2,1)S(1)}, u32[]{:S(2)}, u32[]{:S(2)}) collective-permute-start(bf16[3,8,8,256]{3,2,1,0:T(8,128)(2,1)S(1)} %get-tuple-element.55), channel_id=1, source_target_pairs={{0,7},{1,2},{2,1},{3,4},{4,3},{5,6},{6,5},{7,0},{8,15},{9,10},{10,... | collective-permute-start | bytes 294920 | tf_op jit(solution)/shard_map/ppermute | solution.py:505
  14.1 3.3 %collective-permute-start.2 = (bf16[3,8,8,256]{3,2,1,0:T(8,128)(2,1)S(1)}, bf16[3,8,8,256]{3,2,1,0:T(8,128)(2,1)S(1)}, u32[]{:S(2)}, u32[]{:S(2)}) collective-permute-start(bf16[3,8,8,256]{3,2,1,0:T(8,128)(2,1)S(1)} %get-tuple-element.56), channel_id=1, source_target_pairs={{0,1},{1,0},{2,3},{3,2},{4,5},{5,4},{6,7},{7,6},{8,9},{9,8},{10,11... | collective-permute-start | bytes 294920 | tf_op jit(solution)/shard_map/ppermute | solution.py:505
  22.1 1.2 %collective-permute-start.4 = (bf16[32,128]{1,0:T(8,128)(2,1)S(1)}, bf16[32,128]{1,0:T(8,128)(2,1)S(1)}, u32[]{:S(2)}, u32[]{:S(2)}) collective-permute-start(bf16[32,128]{1,0:T(8,128)(2,1)S(1)} %shard_map.101), channel_id=1, source_target_pairs={{0,1},{1,0},{2,3},{3,2},{4,5},{5,4},{6,7},{7,6},{8,9},{9,8},{10,11... | collective-permute-start | bytes 24584 | tf_op jit(solution)/shard_map/ppermute | solution.py:505
  23.3 8.8 %collective-permute-start.7 = (bf16[2,32,128]{2,1,0:T(8,128)(2,1)S(1)}, bf16[2,32,128]{2,1,0:T(8,128)(2,1)S(1)}, u32[]{:S(2)}, u32[]{:S(2)}) collective-permute-start(bf16[2,32,128]{2,1,0:T(8,128)(2,1)S(1)} %get-tuple-element.58), channel_id=1, source_target_pairs={{0,24},{1,25},{2,26},{3,27},{4,28},{5,29},{6,30},{7,31},{8,16},{9,... | collective-permute-start | bytes 49160 | tf_op jit(solution)/shard_map/ppermute | solution.py:505
  23.3 8.8 %collective-permute-start.6 = (bf16[2,32,128]{2,1,0:T(8,128)(2,1)S(1)}, bf16[2,32,128]{2,1,0:T(8,128)(2,1)S(1)}, u32[]{:S(2)}, u32[]{:S(2)}) collective-permute-start(bf16[2,32,128]{2,1,0:T(8,128)(2,1)S(1)} %get-tuple-element.58), channel_id=1, source_target_pairs={{0,16},{1,17},{2,18},{3,19},{4,20},{5,21},{6,22},{7,23},{8,24},{9,... | collective-permute-start | bytes 49160 | tf_op jit(solution)/shard_map/ppermute | solution.py:505
  27.4 4.7 %collective-permute-start.5 = (bf16[2,32,128]{2,1,0:T(8,128)(2,1)S(1)}, bf16[2,32,128]{2,1,0:T(8,128)(2,1)S(1)}, u32[]{:S(2)}, u32[]{:S(2)}) collective-permute-start(bf16[2,32,128]{2,1,0:T(8,128)(2,1)S(1)} %get-tuple-element.58), channel_id=1, source_target_pairs={{0,8},{1,9},{2,10},{3,11},{4,12},{5,13},{6,14},{7,15},{8,0},{9,1},... | collective-permute-start | bytes 49160 | tf_op jit(solution)/shard_map/ppermute | solution.py:505
  32.2 13.9 %copy-start.1 = (bf16[3,9,64,64]{3,2,1,0:T(8,128)(2,1)S(1)}, bf16[3,9,64,64]{3,2,1,0:T(8,128)(2,1)}, u32[]{:S(2)}) copy-start(bf16[3,9,64,64]{3,2,1,0:T(8,128)(2,1)} %w_down) | copy-start | bytes 663556
  32.2 13.9 %copy-start.3 = (bf16[128,256]{1,0:T(8,128)(2,1)S(1)}, bf16[128,256]{1,0:T(8,128)(2,1)}, u32[]{:S(2)}) copy-start(bf16[128,256]{1,0:T(8,128)(2,1)} %down_in.1) | copy-start | bytes 196612
  32.2 13.9 %copy-start.5 = (bf16[256,64]{0,1:T(8,128)(2,1)S(1)}, bf16[256,64]{0,1:T(8,128)(2,1)}, u32[]{:S(2)}) copy-start(bf16[256,64]{0,1:T(8,128)(2,1)} %param.16) | copy-start | bytes 98308
  32.2 13.9 %copy-start.9 = (bf16[64,4]{0,1:T(4,128)(2,1)S(1)}, bf16[64,4]{0,1:T(4,128)(2,1)}, u32[]{:S(2)}) copy-start(bf16[64,4]{0,1:T(4,128)(2,1)} %param.18) | copy-start | bytes 1540
  32.2 8.4 %collective-permute-start.10 = (bf16[4,2,32,128]{3,2,1,0:T(8,128)(2,1)S(1)}, bf16[4,2,32,128]{3,2,1,0:T(8,128)(2,1)S(1)}, u32[]{:S(2)}, u32[]{:S(2)}) collective-permute-start(bf16[4,2,32,128]{3,2,1,0:T(8,128)(2,1)S(1)} %pad_maximum_fusion.1.z0), channel_id=1, source_target_pairs={{0,96},{1,97},{2,98},{3,99},{4,100},{5,101},{6,102},{7,103},{8,104... | collective-permute-start | bytes 196616 | tf_op jit(solution)/shard_map/ppermute | solution.py:505
  33.0 7.7 %collective-permute-start.9 = (bf16[4,2,32,128]{3,2,1,0:T(8,128)(2,1)S(1)}, bf16[4,2,32,128]{3,2,1,0:T(8,128)(2,1)S(1)}, u32[]{:S(2)}, u32[]{:S(2)}) collective-permute-start(bf16[4,2,32,128]{3,2,1,0:T(8,128)(2,1)S(1)} %pad_maximum_fusion.1.z0), channel_id=1, source_target_pairs={{0,64},{1,65},{2,66},{3,67},{4,68},{5,69},{6,70},{7,71},{8,72},{9,... | collective-permute-start | bytes 196616 | tf_op jit(solution)/shard_map/ppermute | solution.py:505
  33.0 7.7 %collective-permute-start.8 = (bf16[4,2,32,128]{3,2,1,0:T(8,128)(2,1)S(1)}, bf16[4,2,32,128]{3,2,1,0:T(8,128)(2,1)S(1)}, u32[]{:S(2)}, u32[]{:S(2)}) collective-permute-start(bf16[4,2,32,128]{3,2,1,0:T(8,128)(2,1)S(1)} %pad_maximum_fusion.1.z0), channel_id=1, source_target_pairs={{0,32},{1,33},{2,34},{3,35},{4,36},{5,37},{6,38},{7,39},{8,40},{9,... | collective-permute-start | bytes 196616 | tf_op jit(solution)/shard_map/ppermute | solution.py:505
  40.6 9.0 %copy-start.7 = (s32[8,1,64]{2,1,0:T(1,128)S(1)}, s32[8,1,64]{2,1,0:T(1,128)}, u32[]{:S(2)}) copy-start(s32[8,1,64]{2,1,0:T(1,128)} %param.19) | copy-start | bytes 6148
  41.9 7.7 %collective-permute-start.11 = (bf16[5,32,128]{2,1,0:T(8,128)(2,1)S(1)}, bf16[5,32,128]{2,1,0:T(8,128)(2,1)S(1)}, u32[]{:S(2)}, u32[]{:S(2)}) collective-permute-start(bf16[5,32,128]{2,1,0:T(8,128)(2,1)S(1)} %get-tuple-element.43), channel_id=1, source_target_pairs={{0,2},{1,3},{2,0},{3,1},{4,6},{5,7},{6,4},{7,5},{8,10},{9,11},{10,... | collective-permute-start | bytes 122888 | tf_op jit(solution)/shard_map/ppermute | solution.py:505
  42.2 7.3 %collective-permute-start.13 = (bf16[5,32,128]{2,1,0:T(8,128)(2,1)S(1)}, bf16[5,32,128]{2,1,0:T(8,128)(2,1)S(1)}, u32[]{:S(2)}, u32[]{:S(2)}) collective-permute-start(bf16[5,32,128]{2,1,0:T(8,128)(2,1)S(1)} %get-tuple-element.44), channel_id=1, source_target_pairs={{0,6},{1,7},{2,4},{3,5},{4,2},{5,3},{6,0},{7,1},{8,14},{9,15},{10,... | collective-permute-start | bytes 122888 | tf_op jit(solution)/shard_map/ppermute | solution.py:505
  44.3 5.2 %collective-permute-start.12 = (bf16[2,32,128]{2,1,0:T(8,128)(2,1)S(1)}, bf16[2,32,128]{2,1,0:T(8,128)(2,1)S(1)}, u32[]{:S(2)}, u32[]{:S(2)}) collective-permute-start(bf16[2,32,128]{2,1,0:T(8,128)(2,1)S(1)} %get-tuple-element.42.p5), channel_id=1, source_target_pairs={{0,4},{1,5},{2,6},{3,7},{4,0},{5,1},{6,2},{7,3},{8,12},{9,13},{10,... | collective-permute-start | bytes 49160 | tf_op jit(solution)/shard_map/ppermute | solution.py:505

commit v2 on v1

--- a/solution.py
+++ b/solution.py
@@ -13,7 +13,7 @@
 n_row = 16
 n_col = 8
 samples = 32
-vmem_bytes = 48 * 1024 * 1024
+vmem_bytes = 20 * 1024 * 1024
 
 
 def dot(left, right):
@@ -25,6 +25,10 @@
 
 
 def whole_call(body, out_shapes, scratch, args, smem=(), outside=()):
+    args = [
+        pltpu.with_memory_space_constraint(x, pltpu.HBM) if i in outside else x
+        for i, x in enumerate(args)
+    ]
     specs = [
         pl.BlockSpec(
             memory_space=pltpu.SMEM if i in smem else pltpu.HBM if i in outside else pltpu.VMEM
@@ -177,27 +181,49 @@
                 wh[base : base + 64, :] = kept.astype(bf16)
 
 
-def conv_layer(src, dst, weights, rows, cols, to_odd):
-    low = low_half((cols, samples, 128))
-    for i in range(rows):
-        here = src[i, 0:cols]
-        right = src[i, 1 : cols + 1]
-        below = src[i + 1, 0:cols]
-        corner = src[i + 1, 1 : cols + 1]
+def row_chunks(first, last, cols):
+    step = max(1, 14 // cols)
+    return [(i, min(i + step, last)) for i in range(first, last, step)]
+
+
+def conv_block(src, dst, weights, row_range, col_range, to_odd, src_at=(0, 0), dst_at=(0, 0)):
+    c0, c1 = col_range
+    cols = c1 - c0
+    for r0, r1 in row_chunks(*row_range, cols):
+        rows = r1 - r0
+        i, j = r0 - src_at[0], c0 - src_at[1]
+        here = src[i : i + rows, j : j + cols]
+        right = src[i : i + rows, j + 1 : j + 1 + cols]
+        below = src[i + 1 : i + 1 + rows, j : j + cols]
+        corner = src[i + 1 : i + 1 + rows, j + 1 : j + 1 + cols]
         stacked = jnp.concatenate([here, right, below, corner], axis=-1)
-        update = dot(stacked.reshape(cols * samples, 1024), weights[...])
-        update = jnp.maximum(update, 0.0).reshape(cols, samples, 256)
+        update = dot(stacked.reshape(rows * cols * samples, 1024), weights[...])
+        update = jnp.maximum(update, 0.0).reshape(rows, cols, samples, 256)
+        low = low_half((rows, cols, samples, 128))
         if to_odd:
             old0 = jnp.where(low, corner[..., 0:128], below[..., 0:128])
             old1 = jnp.where(low, right[..., 128:256], here[..., 128:256])
         else:
             old0 = jnp.where(low, here[..., 0:128], right[..., 0:128])
             old1 = jnp.where(low, below[..., 128:256], corner[..., 128:256])
-        dst[i, :, :, 0:128] = (old0.astype(f32) + update[..., 0:128]).astype(bf16)
-        dst[i, :, :, 128:256] = (old1.astype(f32) + update[..., 128:256]).astype(bf16)
-
-
-def spread_tiles(place, tiles, col_a, col_b, ext):
+        new0 = (old0.astype(f32) + update[..., 0:128]).astype(bf16)
+        new1 = (old1.astype(f32) + update[..., 128:256]).astype(bf16)
+        i, j = r0 - dst_at[0], c0 - dst_at[1]
+        dst[i : i + rows, j : j + cols, :, 0:128] = new0
+        dst[i : i + rows, j : j + cols, :, 128:256] = new1
+
+
+def spread_tiles(place, tiles, ext):
+    row_even = place[0] % 2 == 0
+    after_row = jnp.where(row_even, 16, 0)
+    before_row = jnp.where(row_even, 0, 16)
+    for tile, start in ((0, 8), (1, after_row), (2, before_row)):
+        cells = tiles[tile].astype(f32)
+        ext[pl.ds(start, 8), 1] = cells[:, 0:8]
+        ext[pl.ds(start, 8), 2] = cells[:, 8:16]
+
+
+def spread_sides(place, col_a, col_b, ext):
     row_even = place[0] % 2 == 0
     col_even = place[1] % 2 == 0
     after_row = jnp.where(row_even, 16, 0)
@@ -205,37 +231,63 @@
     after_col = jnp.where(col_even, 3, 0)
     before_col = jnp.where(col_even, 0, 3)
     for tile, start in ((0, 8), (1, after_row), (2, before_row)):
-        cells = tiles[tile].astype(f32)
-        ext[pl.ds(start, 8), 1] = cells[:, 0:8]
-        ext[pl.ds(start, 8), 2] = cells[:, 8:16]
         ext[pl.ds(start, 8), after_col] = col_a[tile].astype(f32)
         ext[pl.ds(start, 8), before_col] = col_b[tile].astype(f32)
 
 
-def embed_quads(ext, we, dst, halo):
-    rows = 4 + halo
-    cols = 8 + halo
-    first = 8 - halo
+def embed_block(ext, we, dst, row_range, col_range, dst_at=(0, 0)):
+    c0, c1 = col_range
+    cols = c1 - c0
     sub = lax.broadcasted_iota(jnp.int32, (16, 128), 0)
     lane = lax.broadcasted_iota(jnp.int32, (16, 128), 1)
     own_lanes = (lane // 8 == sub).astype(f32)
-    for i in range(rows):
+    for r0, r1 in row_chunks(*row_range, cols):
         quads = []
-        for quad in range(cols):
-            parts = []
-            for a in range(2):
-                row = first + 2 * i + (1 - a)
-                for b in range(2):
-                    col = first + 2 * quad + (1 - b)
-                    cell = ext[row, col // 8, col % 8 : col % 8 + 1, :]
-                    halves = [
-                        jnp.broadcast_to(cell[:, k : k + 128], (16, 128)) * own_lanes
-                        for k in (0, 128)
-                    ]
-                    parts.append(jnp.concatenate(halves, axis=0).astype(bf16))
-            quads.append(jnp.concatenate(parts, axis=-1))
+        for i in range(r0, r1):
+            for quad in range(c0, c1):
+                parts = []
+                for a in range(2):
+                    row = 1 + 2 * i + (1 - a)
+                    for b in range(2):
+                        col = 1 + 2 * quad + (1 - b)
+                        cell = ext[row, col // 8, col % 8 : col % 8 + 1, :]
+                        halves = [
+                            jnp.broadcast_to(cell[:, k : k + 128], (16, 128)) * own_lanes
+                            for k in (0, 128)
+                        ]
+                        parts.append(jnp.concatenate(halves, axis=0).astype(bf16))
+                quads.append(jnp.concatenate(parts, axis=-1))
         embedded = dot(jnp.concatenate(quads, axis=0), we[...]).astype(bf16)
-        dst[i] = embedded.reshape(cols, samples, 256)
+        i, j = r0 - dst_at[0], c0 - dst_at[1]
+        dst[i : i + r1 - r0, j : j + cols] = embedded.reshape(r1 - r0, cols, samples, 256)
+
+
+def merge_block(src, dst, merge_in, mo, row_range, col_range):
+    c0, c1 = col_range
+    cols = c1 - c0
+    for r0, r1 in row_chunks(*row_range, cols):
+        stacked = src[r0:r1, c0:c1].reshape((r1 - r0) * cols * samples, 256)
+        hidden = jnp.maximum(dot(stacked, merge_in[...]), 0.0).astype(bf16)
+        merged = dot(hidden, mo[...]).astype(bf16)
+        dst[r0:r1, c0:c1] = merged.reshape(r1 - r0, cols, samples, 128)
+
+
+def blocks_ring(rows, cols):
+    return [
+        ((0, 2), (0, cols)),
+        ((2, rows - 2), (0, 2)),
+        ((2, rows - 2), (cols - 2, cols)),
+        ((rows - 2, rows), (0, cols)),
+    ]
+
+
+def copy_rim(dst, inner, sides, rows, cols):
+    for place, row in ((2, 0), (rows - 3, rows - 5)):
+        dst[place, 2:4] = sides[0, row, 0:2]
+        dst[place, 4 : cols - 4] = inner[row]
+        dst[place, cols - 4 : cols - 2] = sides[1, row, 1:3]
+    dst[3 : rows - 3, 2] = sides[0, 1 : rows - 5, 0]
+    dst[3 : rows - 3, cols - 3] = sides[1, 1 : rows - 5, 2]
 
 
 def merge_pair(top, bottom, merge_in, mo):
@@ -245,13 +297,6 @@
     return dot(hidden, mo).astype(bf16).reshape(count, samples, 128)
 
 
-def merge_quads(src, dst, merge_in, mo, rows, cols):
-    for i in range(rows):
-        stacked = src[i].reshape(cols * samples, 256)
-        hidden = jnp.maximum(dot(stacked, merge_in[...]), 0.0).astype(bf16)
-        dst[i] = dot(hidden, mo[...]).astype(bf16).reshape(cols, samples, 128)
-
-
 def paired_columns(cells):
     count = cells.shape[0] // 2
     split = cells.reshape(count, 2, samples, 128)
@@ -259,37 +304,103 @@
     return jnp.where(low, split[:, 0], split[:, 1])
 
 
-def up_own_body(place, tiles, col_a, col_b, wq, we, merge_in, mo, out, ext, f0, f1, f2, f3, l1):
-    spread_tiles(place, tiles, col_a, col_b, ext)
-    embed_quads(ext, we, f0, 3)
-    conv_layer(f0, f1, wq.at[0], 6, 10, False)
-    conv_layer(f1, f2, wq.at[1], 5, 9, True)
-    conv_layer(f2, f3, wq.at[2], 4, 8, False)
-    merge_quads(f3, l1, merge_in, mo, 4, 8)
-    top = jnp.concatenate([paired_columns(l1[0]), paired_columns(l1[2])], axis=0)
-    bottom = jnp.concatenate([paired_columns(l1[1]), paired_columns(l1[3])], axis=0)
+def up_inner_body(place, tiles, wq, we, merge_in, mo, f0, f1, f2, f3, l1, ext):
+    at = (2, 4)
+    spread_tiles(place, tiles, ext)
+    embed_block(ext, we, f0, (2, 9), (4, 11), at)
+    conv_block(f0, f1, wq.at[0], (2, 8), (4, 10), False, at, at)
+    conv_block(f1, f2, wq.at[1], (2, 7), (4, 9), True, at, at)
+    conv_block(f2, f3, wq.at[2], (2, 6), (4, 8), False, at, at)
+    merge_block(f3, l1, merge_in, mo, (0, 4), (0, 4))
+
+
+def up_own_body(
+    place,
+    tiles,
+    col_a,
+    col_b,
+    wq,
+    we,
+    merge_in,
+    mo,
+    i0,
+    i1,
+    i2,
+    il1,
+    s0,
+    s1,
+    s2,
+    s3,
+    l1,
+    out,
+    ext,
+):
+    spread_tiles(place, tiles, ext)
+    spread_sides(place, col_a, col_b, ext)
+    for ref, inner, rows, cols in ((s0, i0, 7, 7), (s1, i1, 6, 6), (s2, i2, 5, 5)):
+        ref[0, :, 2] = inner[:, 0]
+        ref[1, :, 0] = inner[:, cols - 1]
+    left = (2, 4)
+    for k, cols in ((0, left), (1, (11, 13))):
+        embed_block(ext, we, s0.at[k], (2, 9), cols, (2, 2 if k == 0 else 10))
+    for k, cols in ((0, left), (1, (10, 12))):
+        src_at = (2, 2 if k == 0 else 10)
+        dst_at = (2, 2 if k == 0 else 9)
+        conv_block(s0.at[k], s1.at[k], wq.at[0], (2, 8), cols, False, src_at, dst_at)
+    for k, cols in ((0, left), (1, (9, 11))):
+        src_at = (2, 2 if k == 0 else 9)
+        dst_at = (2, 2 if k == 0 else 8)
+        conv_block(s1.at[k], s2.at[k], wq.at[1], (2, 7), cols, True, src_at, dst_at)
+    for k, cols in ((0, left), (1, (8, 10))):
+        src_at = (2, 2 if k == 0 else 8)
+        conv_block(s2.at[k], s3.at[k], wq.at[2], (2, 6), cols, False, src_at, (2, cols[0]))
+    merged = merge_pair(
+        s3[..., 0:128].reshape(16, samples, 128),
+        s3[..., 128:256].reshape(16, samples, 128),
+        merge_in[...],
+        mo[...],
+    ).reshape(2, 4, 2, samples, 128)
+    cells = jnp.concatenate([merged[0], il1[...], merged[1]], axis=1)
+    l1[...] = cells
+    top = jnp.concatenate([paired_columns(cells[0]), paired_columns(cells[2])], axis=0)
+    bottom = jnp.concatenate([paired_columns(cells[1]), paired_columns(cells[3])], axis=0)
     l2 = merge_pair(top, bottom, merge_in[...], mo[...])
     l3 = merge_pair(paired_columns(l2[0:4]), paired_columns(l2[4:8]), merge_in[...], mo[...])
     out[...] = paired_columns(l3)[0]
 
 
-def up_wide_first_body(place, tiles, col_a, col_b, wq, we, f1, ext, f0):
-    spread_tiles(place, tiles, col_a, col_b, ext)
-    embed_quads(ext, we, f0, 7)
-    conv_layer(f0, f1, wq.at[0], 10, 14, False)
-
-
-def up_wide_second_body(f1, wq, f3, f2):
-    conv_layer(f1, f2, wq.at[1], 9, 13, True)
-    conv_layer(f2, f3, wq.at[2], 8, 12, False)
-
-
-def up_wide_merge_body(f3, merge_in, mo, l1, l2):
-    merge_quads(f3, l1, merge_in, mo, 8, 12)
-    for i in range(4):
-        l2[i] = merge_pair(
-            paired_columns(l1[2 * i]), paired_columns(l1[2 * i + 1]), merge_in[...], mo[...]
+def up_ring_first_body(place, tiles, col_a, col_b, wq, we, i0, s0, i1, s1, f1, ext, f0):
+    spread_tiles(place, tiles, ext)
+    spread_sides(place, col_a, col_b, ext)
+    copy_rim(f0, i0, s0, 11, 15)
+    for block in blocks_ring(11, 15):
+        embed_block(ext, we, f0, *block)
+    for block in blocks_ring(10, 14):
+        conv_block(f0, f1, wq.at[0], *block, False)
+    copy_rim(f1, i1, s1, 10, 14)
+
+
+def up_ring_second_body(f1, wq, i2, s2, i3, s3, f3, f2):
+    copy_rim(f2, i2, s2, 9, 13)
+    for block in blocks_ring(9, 13):
+        conv_block(f1, f2, wq.at[1], *block, True)
+    for block in blocks_ring(8, 12):
+        conv_block(f2, f3, wq.at[2], *block, False)
+    f3[2:6, 4:8] = i3[...]
+    f3[2:6, 2:4] = s3[0]
+    f3[2:6, 8:10] = s3[1]
+
+
+def up_ring_merge_body(f3, merge_in, mo, own1, l1, l2):
+    for block in blocks_ring(8, 12):
+        merge_block(f3, l1, merge_in, mo, *block)
+    l1[2:6, 2:10] = own1[...]
+    for i in (0, 2):
+        top = jnp.concatenate([paired_columns(l1[2 * i]), paired_columns(l1[2 * i + 2])], axis=0)
+        bottom = jnp.concatenate(
+            [paired_columns(l1[2 * i + 1]), paired_columns(l1[2 * i + 3])], axis=0
         )
+        l2[i : i + 2] = merge_pair(top, bottom, merge_in[...], mo[...]).reshape(2, 6, samples, 128)
 
 
 def mid_body(place, z0, z1, z2, z3, merge_in, mo, a3, a4, p5, send1, send3, strip, l4s):
@@ -481,9 +592,9 @@
             mean = dot((fine * fine).astype(bf16), averager)
             normed = (fine * lax.rsqrt(mean + norm_eps)).astype(bf16).reshape(12, samples, 128)
             n0[row_to, :, :, a * 128 : a * 128 + 128] = jnp.where(low11, normed[1:12], normed[0:11])
-    conv_layer(n0, r1, wq.at[0], 6, 10, False)
-    conv_layer(r1, r2, wq.at[1], 5, 9, True)
-    conv_layer(r2, r3, wq.at[2], 4, 8, False)
+    conv_block(n0, r1, wq.at[0], (0, 6), (0, 10), False)
+    conv_block(r1, r2, wq.at[1], (0, 5), (0, 9), True)
+    conv_block(r2, r3, wq.at[2], (0, 4), (0, 8), False)
     stacked = jnp.concatenate(
         [r3[:, quad].reshape(4 * samples, 256) for quad in range(8)], axis=-1
     )
@@ -546,7 +657,6 @@
     right = tiles[:, :, 8:16]
     col_a = swap(jnp.where(col_even, right, left), lambda r, c: (r, pair_after(c, n_col)))
     col_b = swap(jnp.where(col_even, left, right), lambda r, c: (r, pair_before(c, n_col)))
-    w_down, tiles = lax.optimization_barrier((w_down, tiles))
     wq_down, di, di0, do0, do, wh = whole_call(
         prep_down_body,
         (
@@ -569,35 +679,52 @@
 
     quads = lambda rows, cols: pltpu.VMEM((rows, cols, samples, 256), bf16)
     ext = pltpu.VMEM((24, 4, 8, 256), f32)
-    l3 = whole_call(
+    i0, i1, i2, i3, il1 = whole_call(
+        up_inner_body,
+        (
+            arr((7, 7, samples, 256)),
+            arr((6, 6, samples, 256)),
+            arr((5, 5, samples, 256)),
+            arr((4, 4, samples, 256)),
+            arr((4, 4, samples, 128)),
+        ),
+        [ext],
+        (place, tiles, wq_up, we, mi, mo),
+        smem=(0,),
+    )
+    i0, col_a, col_b = lax.optimization_barrier((i0, col_a, col_b))
+    s0, s1, s2, s3, own1, l3 = whole_call(
         up_own_body,
-        arr((samples, 128)),
-        [
-            ext,
-            quads(7, 11),
-            quads(6, 10),
-            quads(5, 9),
-            quads(4, 8),
-            pltpu.VMEM((4, 8, samples, 128), bf16),
-        ],
-        (place, tiles, col_a, col_b, wq_up, we, mi, mo),
+        (
+            arr((2, 7, 3, samples, 256)),
+            arr((2, 6, 3, samples, 256)),
+            arr((2, 5, 3, samples, 256)),
+            arr((2, 4, 2, samples, 256)),
+            arr((4, 8, samples, 128)),
+            arr((samples, 128)),
+        ),
+        [ext],
+        (place, tiles, col_a, col_b, wq_up, we, mi, mo, i0, i1, i2, il1),
         smem=(0,),
     )
 
     pair = jnp.stack([l3, swap(l3, lambda r, c: (r, c ^ 1))])
     four = jnp.stack([pair] + [swap(pair, lambda r, c, m=m: (r ^ m, c)) for m in (1, 2, 3)])
-    col_a, pair = lax.optimization_barrier((col_a, pair))
+    s0, pair = lax.optimization_barrier((s0, pair))
     f1 = whole_call(
-        up_wide_first_body,
+        up_ring_first_body,
         arr((10, 14, samples, 256)),
         [ext, quads(11, 15)],
-        (place, tiles, col_a, col_b, wq_up, we),
+        (place, tiles, col_a, col_b, wq_up, we, i0, s0, i1, s1),
         smem=(0,),
     )
     four, f1 = lax.optimization_barrier((four, f1))
     strips = [four] + [swap(four, lambda r, c, m=m: (r ^ (4 * m), c)) for m in (1, 2, 3)]
     f3 = whole_call(
-        up_wide_second_body, arr((8, 12, samples, 256)), [quads(9, 13)], (f1, wq_up)
+        up_ring_second_body,
+        arr((8, 12, samples, 256)),
+        [quads(9, 13)],
+        (f1, wq_up, i2, s2, i3, s3),
     )
     strips[3], f3 = lax.optimization_barrier((strips[3], f3))
     a3, a4, p5, send1, send3 = whole_call(
@@ -617,10 +744,10 @@
     q2 = swap(p5, lambda r, c: (r, c ^ 4))
     q3 = swap(send3, lambda r, c: (r, c ^ 6))
     l1, l2 = whole_call(
-        up_wide_merge_body,
+        up_ring_merge_body,
         (arr((8, 12, samples, 128)), arr((4, 6, samples, 128))),
         [],
-        (f3, mi, mo),
+        (f3, mi, mo, own1),
     )
     slots = qubit_slot.reshape(qubit_slot.shape[0], qubit_slot.shape[2])
     return whole_call(

time: 63 us -> 58.2 us (0.924)
  local copies, waits for them, and re-layouts: 4.23 us -> 0.01 us
  waiting for transfers between devices: 5.29 us -> 6.31 us
  Pallas kernels: 31.4 us -> 30.7 us
    unnamed x20 -> x2, local copies, waits for them, and re-layouts: 4.23 us -> 0.01 us
    ppermute x14, waiting for transfers between devices: 5.29 us -> 6.31 us  [swap(): return lax.ppermute(value, ('row', 'col'), pairs)]
    pallas_call x8 -> x9, Pallas kernels: 31.4 us -> 30.7 us  [whole_call(): pl.pallas_call(body, out_shape=out_shapes, in_specs=specs, out_specs=jax....]
  transfers between devices with their start and end apart: 14 -> 14, of which waited for: 3 -> 6; matrix products, arithmetic and copies ran while one was open for 0% -> 0% of each run, Pallas kernels for 21% -> 23%
where the time goes in v2:
time: 58.2 us; the launch traced here: 58.1 us
  Pallas kernels  30.7 us (53%)
  starting transfers between devices  20.8 us (36%)
  waiting for transfers between devices  6.31 us (11%)
    pallas_call x9, Pallas kernels, whole_call(): pl.pallas_call(body, out_shape=out_shapes, in_specs=specs, out_specs=jax....  30.7 us
    ppermute x14, starting transfers between devices, swap(): return lax.ppermute(value, ('row', 'col'), pairs)  20.8 us
    ppermute x14, waiting for transfers between devices, swap(): return lax.ppermute(value, ('row', 'col'), pairs)  6.31 us
  transfers between devices with their start and end apart: 14, of which 6 were waited for; matrix products, arithmetic and copies ran while one was open for 0% of the time, Pallas kernels for 23%

profile of v2, /device:TPU:0, one launch (start us, length us, event | category | flops | bytes accessed | tf_op | source)
XLA Modules:
  0.0 58.1 jit_solution(13994587166293385066)
XLA Ops:
  0.0 6.6 %collective-permute-start.1 = (bf16[8,16,256]{2,1,0:T(8,128)(2,1)}, bf16[8,16,256]{2,1,0:T(8,128)(2,1)S(1)}, u32[]{:S(2)}, u32[]{:S(2)}) collective-permute-start(bf16[8,16,256]{2,1,0:T(8,128)(2,1)} %own.1), channel_id=1, source_target_pairs={{0,120},{1,121},{2,122},{3,123},{4,124},{5,125},{6,126},{7,127},{8... | collective-permute-start | bytes 196616 | tf_op jit(solution)/shard_map/ppermute | solution.py:616
  6.6 1.7 %shard_map.100 = (bf16[8,16,256]{2,1,0:T(8,128)(2,1)S(1)}, bf16[3,1024,256]{2,1,0:T(8,128)(2,1)S(1)}, bf16[512,256]{1,0:T(8,128)(2,1)S(1)}, bf16[256,256]{1,0:T(8,128)(2,1)S(1)}, bf16[256,128]{1,0:T(8,128)(2,1)S(1)}) custom-call(bf16[8,16,256]{2,1,0:T(8,128)(2,1)} %own.1, bf16[3,9,64,64]{3,2,1,0:T(8,128)(2,1)} %w_up.1, bf16[8,64]{1,0:T(8,128)(2,1)} %w_embed.1, ...), custom_call_target="tpu_custom_call" | custom-call | tf_op jit(solution)/shard_map/pallas_call | solution.py:38
  8.3 0.7 %collective-permute-done.1 = bf16[8,16,256]{2,1,0:T(8,128)(2,1)S(1)} collective-permute-done((bf16[8,16,256]{2,1,0:T(8,128)(2,1)}, bf16[8,16,256]{2,1,0:T(8,128)(2,1)S(1)}, u32[]{:S(2)}, u32[]{:S(2)}) %collective-permute-start.1) | collective-permute-done | bytes 65568 | tf_op jit(solution)/shard_map/ppermute | solution.py:616
  9.0 2.0 %collective-permute-done = bf16[8,16,256]{2,1,0:T(8,128)(2,1)S(1)} collective-permute-done((bf16[8,16,256]{2,1,0:T(8,128)(2,1)}, bf16[8,16,256]{2,1,0:T(8,128)(2,1)S(1)}, u32[]{:S(2)}, u32[]{:S(2)}) %collective-permute-start) | collective-permute-done | bytes 65568 | tf_op jit(solution)/shard_map/ppermute | solution.py:616
  11.1 0.8 %collective-permute-start.3 = (bf16[3,8,8,256]{3,2,1,0:T(8,128)(2,1)S(1)}, bf16[3,8,8,256]{3,2,1,0:T(8,128)(2,1)S(1)}, u32[]{:S(2)}, u32[]{:S(2)}) collective-permute-start(bf16[3,8,8,256]{3,2,1,0:T(8,128)(2,1)S(1)} %get-tuple-element.79), channel_id=1, source_target_pairs={{0,7},{1,2},{2,1},{3,4},{4,3},{5,6},{6,5},{7,0},{8,15},{9,10},{10,... | collective-permute-start | bytes 294920 | tf_op jit(solution)/shard_map/ppermute | solution.py:616
  12.0 0.8 %collective-permute-start.2 = (bf16[3,8,8,256]{3,2,1,0:T(8,128)(2,1)S(1)}, bf16[3,8,8,256]{3,2,1,0:T(8,128)(2,1)S(1)}, u32[]{:S(2)}, u32[]{:S(2)}) collective-permute-start(bf16[3,8,8,256]{3,2,1,0:T(8,128)(2,1)S(1)} %get-tuple-element.80), channel_id=1, source_target_pairs={{0,1},{1,0},{2,3},{3,2},{4,5},{5,4},{6,7},{7,6},{8,9},{9,8},{10,11... | collective-permute-start | bytes 294920 | tf_op jit(solution)/shard_map/ppermute | solution.py:616
  12.9 3.1 %shard_map.101 = (bf16[7,7,32,256]{3,2,1,0:T(8,128)(2,1)S(1)}, bf16[6,6,32,256]{3,2,1,0:T(8,128)(2,1)S(1)}, bf16[5,5,32,256]{3,2,1,0:T(8,128)(2,1)S(1)}, bf16[4,...) custom-call(s32[2]{0:T(128)S(1)} %pad_add_fusion.place, bf16[3,8,16,256]{3,2,1,0:T(8,128)(2,1)S(1)} %pad_maximum_fusion.tiles, ...), custom_call_target="tpu_custom_call" | custom-call | tf_op jit(solution)/shard_map/pallas_call | solution.py:38
  16.4 3.0 %shard_map.102 = (bf16[2,7,3,32,256]{4,3,2,1,0:T(8,128)(2,1)S(1)}, bf16[2,6,3,32,256]{4,3,2,1,0:T(8,128)(2,1)S(1)}, bf16[2,5,3,32,256]{4,3,2,1,0:T(8,128)(2,1)S(...) custom-call(s32[2]{0:T(128)S(1)} %pad_add_fusion.place, ...), custom_call_target="tpu_custom_call" | custom-call | tf_op jit(solution)/shard_map/pallas_call | solution.py:38
  19.6 1.2 %collective-permute-done.4 = bf16[32,128]{1,0:T(8,128)(2,1)S(1)} collective-permute-done((bf16[32,128]{1,0:T(8,128)(2,1)S(1)}, bf16[32,128]{1,0:T(8,128)(2,1)S(1)}, u32[]{:S(2)}, u32[]{:S(2)}) %collective-permute-start.4) | collective-permute-done | bytes 8224 | tf_op jit(solution)/shard_map/ppermute | solution.py:616
  20.8 2.1 %collective-permute-start.6 = (bf16[2,32,128]{2,1,0:T(8,128)(2,1)S(1)}, bf16[2,32,128]{2,1,0:T(8,128)(2,1)S(1)}, u32[]{:S(2)}, u32[]{:S(2)}) collective-permute-start(bf16[2,32,128]{2,1,0:T(8,128)(2,1)S(1)} %get-tuple-element.82), channel_id=1, source_target_pairs={{0,16},{1,17},{2,18},{3,19},{4,20},{5,21},{6,22},{7,23},{8,24},{9,... | collective-permute-start | bytes 49160 | tf_op jit(solution)/shard_map/ppermute | solution.py:616
  22.9 2.0 %collective-permute-start.5 = (bf16[2,32,128]{2,1,0:T(8,128)(2,1)S(1)}, bf16[2,32,128]{2,1,0:T(8,128)(2,1)S(1)}, u32[]{:S(2)}, u32[]{:S(2)}) collective-permute-start(bf16[2,32,128]{2,1,0:T(8,128)(2,1)S(1)} %get-tuple-element.82), channel_id=1, source_target_pairs={{0,8},{1,9},{2,10},{3,11},{4,12},{5,13},{6,14},{7,15},{8,0},{9,1},... | collective-permute-start | bytes 49160 | tf_op jit(solution)/shard_map/ppermute | solution.py:616
  24.8 3.0 %shard_map.103.f1 = bf16[10,14,32,256]{3,2,1,0:T(8,128)(2,1)S(1)} custom-call(s32[2]{0:T(128)S(1)} %pad_add_fusion.place, bf16[3,8,16,256]{3,2,1,0:T(8,128)(2,1)S(1)} %pad_maximum_fusion.tiles, bf16[3,8,8,256]{3,2,1,0:T(8,128)(2,1)S(1)} %collective-permute-done.2.col_a, bf16[3,8,8,256]{3,2,1,0:T(8,128)(2,1)S(1)} %collective-permute-done.3.col_b, ...), custom_call_target="tpu_custom_call" | custom-call | tf_op jit(solution)/shard_map/pallas_call | solution.py:38
  27.9 2.1 %collective-permute-start.10 = (bf16[4,2,32,128]{3,2,1,0:T(8,128)(2,1)S(1)}, bf16[4,2,32,128]{3,2,1,0:T(8,128)(2,1)S(1)}, u32[]{:S(2)}, u32[]{:S(2)}) collective-permute-start(bf16[4,2,32,128]{3,2,1,0:T(8,128)(2,1)S(1)} %pad_maximum_fusion.1.z0), channel_id=1, source_target_pairs={{0,96},{1,97},{2,98},{3,99},{4,100},{5,101},{6,102},{7,103},{8,104... | collective-permute-start | bytes 196616 | tf_op jit(solution)/shard_map/ppermute | solution.py:616
  30.0 2.1 %collective-permute-start.8 = (bf16[4,2,32,128]{3,2,1,0:T(8,128)(2,1)S(1)}, bf16[4,2,32,128]{3,2,1,0:T(8,128)(2,1)S(1)}, u32[]{:S(2)}, u32[]{:S(2)}) collective-permute-start(bf16[4,2,32,128]{3,2,1,0:T(8,128)(2,1)S(1)} %pad_maximum_fusion.1.z0), channel_id=1, source_target_pairs={{0,32},{1,33},{2,34},{3,35},{4,36},{5,37},{6,38},{7,39},{8,40},{9,... | collective-permute-start | bytes 196616 | tf_op jit(solution)/shard_map/ppermute | solution.py:616
  32.0 2.8 %shard_map.104.f3 = bf16[8,12,32,256]{3,2,1,0:T(8,128)(2,1)S(1)} custom-call(bf16[10,14,32,256]{3,2,1,0:T(8,128)(2,1)S(1)} %shard_map.103.f1, bf16[3,1024,256]{2,1,0:T(8,128)(2,1)S(1)} %get-tuple-element.43.wq, bf16[5,5,32,256]{3,2,1,0:T(8,128)(2,1)S(1)} %get-tuple-element.52.i2, bf16[2,5,3,32,256]{4,3,2,1,0:T(8,128)(2,1)S(1)} %get-tuple-element.60.s2, ...), custom_call_target="tpu_custom_call" | custom-call | tf_op jit(solution)/shard_map/pallas_call | solution.py:38
  34.8 0.9 %collective-permute-done.9.z2 = bf16[4,2,32,128]{3,2,1,0:T(8,128)(2,1)S(1)} collective-permute-done((bf16[4,2,32,128]{3,2,1,0:T(8,128)(2,1)S(1)}, bf16[4,2,32,128]{3,2,1,0:T(8,128)(2,1)S(1)}, u32[]{:S(2)}, u32[]{:S(2)}) %collective-permute-start.9) | collective-permute-done | bytes 65568 | tf_op jit(solution)/shard_map/ppermute | solution.py:616
  35.8 1.2 %shard_map.105 = (bf16[3,2,32,128]{3,2,1,0:T(8,128)(2,1)S(1)}, bf16[3,2,32,128]{3,2,1,0:T(8,128)(2,1)S(1)}, bf16[2,32,128]{2,1,0:T(8,128)(2,1)S(1)}, bf16[5,32,1...) custom-call(s32[2]{0:T(128)S(1)} %pad_add_fusion.place, bf16[4,2,32,128]{3,2,1,0:T(8,128)(2,1)S(1)} %pad_maximum_fusion.1.z0, ...), custom_call_target="tpu_custom_call" | custom-call | tf_op jit(solution)/shard_map/pallas_call | solution.py:38
  37.0 1.2 %collective-permute-start.11 = (bf16[5,32,128]{2,1,0:T(8,128)(2,1)S(1)}, bf16[5,32,128]{2,1,0:T(8,128)(2,1)S(1)}, u32[]{:S(2)}, u32[]{:S(2)}) collective-permute-start(bf16[5,32,128]{2,1,0:T(8,128)(2,1)S(1)} %get-tuple-element.67), channel_id=1, source_target_pairs={{0,2},{1,3},{2,0},{3,1},{4,6},{5,7},{6,4},{7,5},{8,10},{9,11},{10,... | collective-permute-start | bytes 122888 | tf_op jit(solution)/shard_map/ppermute | solution.py:616
  38.1 1.8 %collective-permute-start.13 = (bf16[5,32,128]{2,1,0:T(8,128)(2,1)S(1)}, bf16[5,32,128]{2,1,0:T(8,128)(2,1)S(1)}, u32[]{:S(2)}, u32[]{:S(2)}) collective-permute-start(bf16[5,32,128]{2,1,0:T(8,128)(2,1)S(1)} %get-tuple-element.68), channel_id=1, source_target_pairs={{0,6},{1,7},{2,4},{3,5},{4,2},{5,3},{6,0},{7,1},{8,14},{9,15},{10,... | collective-permute-start | bytes 122888 | tf_op jit(solution)/shard_map/ppermute | solution.py:616
  39.9 1.2 %collective-permute-start.12 = (bf16[2,32,128]{2,1,0:T(8,128)(2,1)S(1)}, bf16[2,32,128]{2,1,0:T(8,128)(2,1)S(1)}, u32[]{:S(2)}, u32[]{:S(2)}) collective-permute-start(bf16[2,32,128]{2,1,0:T(8,128)(2,1)S(1)} %get-tuple-element.66.p5), channel_id=1, source_target_pairs={{0,4},{1,5},{2,6},{3,7},{4,0},{5,1},{6,2},{7,3},{8,12},{9,13},{10,... | collective-permute-start | bytes 49160 | tf_op jit(solution)/shard_map/ppermute | solution.py:616
  41.1 1.9 %shard_map.107 = (bf16[3,1024,256]{2,1,0:T(8,128)(2,1)S(1)}, bf16[128,256]{1,0:T(8,128)(2,1)S(1)}, bf16[256,512]{1,0:T(8,128)(2,1)S(1)}, bf16[512,128]{1,0:T(8,1...) custom-call(bf16[3,9,64,64]{3,2,1,0:T(8,128)(2,1)} %w_down.1, bf16[128,256]{1,0:T(8,128)(2,1)} %down_in.1, ...), custom_call_target="tpu_custom_call" | custom-call | tf_op jit(solution)/shard_map/pallas_call | solution.py:38
  43.0 1.1 %shard_map.106 = (bf16[8,12,32,128]{3,2,1,0:T(8,128)(2,1)S(1)}, bf16[4,6,32,128]{3,2,1,0:T(8,128)(2,1)S(1)}) custom-call(bf16[8,12,32,256]{3,2,1,0:T(8,128)(2,1)S(1)} %shard_map.104.f3, bf16[256,256]{1,0:T(8,128)(2,1)S(1)} %get-tuple-element.45.merge_in, bf16[256,128]{1,0:T(8,128)(2,1)S(1)} %get-tuple-element.46.mo, ...), custom_call_target="tpu_custom_call" | custom-call | tf_op jit(solution)/shard_map/pallas_call | solution.py:38
  44.1 1.0 %collective-permute-done.12.q2 = bf16[2,32,128]{2,1,0:T(8,128)(2,1)S(1)} collective-permute-done((bf16[2,32,128]{2,1,0:T(8,128)(2,1)S(1)}, bf16[2,32,128]{2,1,0:T(8,128)(2,1)S(1)}, u32[]{:S(2)}, u32[]{:S(2)}) %collective-permute-start.12) | collective-permute-done | bytes 16416 | tf_op jit(solution)/shard_map/ppermute | solution.py:616
  45.2 12.9 %shard_map.108 = f32[32,8,64]{2,1,0:T(8,128)} custom-call(s32[2]{0:T(128)S(1)} %pad_add_fusion.place, s32[8,64]{1,0:T(8,128)S(1)} %bitcast.18, bf16[3,2,32,128]{3,2,1,0:T(8,128)(2,1)S(1)} %get-tuple-element.64.a3, bf16[3,2,32,128]{3,2,1,0:T(8,128)(2,1)S(1)} %get-tuple-element.65.a4, bf16[2,32,128]{2,1,0:T(8,128)(2,1)S(1)} %get-tuple-element.66.p5, ...), custom_call_target="tpu_custom_call" | custom-call | tf_op jit(solution)/shard_map/pallas_call | solution.py:38
  (20 shorter events, 0.7 us)
Async XLA Ops:
  0.0 9.0 %collective-permute-start.1 = (bf16[8,16,256]{2,1,0:T(8,128)(2,1)}, bf16[8,16,256]{2,1,0:T(8,128)(2,1)S(1)}, u32[]{:S(2)}, u32[]{:S(2)}) collective-permute-start(bf16[8,16,256]{2,1,0:T(8,128)(2,1)} %own.1), channel_id=1, source_target_pairs={{0,120},{1,121},{2,122},{3,123},{4,124},{5,125},{6,126},{7,127},{8... | collective-permute-start | bytes 196616 | tf_op jit(solution)/shard_map/ppermute | solution.py:616
  6.6 4.5 %collective-permute-start = (bf16[8,16,256]{2,1,0:T(8,128)(2,1)}, bf16[8,16,256]{2,1,0:T(8,128)(2,1)S(1)}, u32[]{:S(2)}, u32[]{:S(2)}) collective-permute-start(bf16[8,16,256]{2,1,0:T(8,128)(2,1)} %own.1), channel_id=1, source_target_pairs={{0,8},{1,9},{2,10},{3,11},{4,12},{5,13},{6,14},{7,15},{8,0},{9,1},... | collective-permute-start | bytes 196616 | tf_op jit(solution)/shard_map/ppermute | solution.py:616
  11.1 5.3 %collective-permute-start.3 = (bf16[3,8,8,256]{3,2,1,0:T(8,128)(2,1)S(1)}, bf16[3,8,8,256]{3,2,1,0:T(8,128)(2,1)S(1)}, u32[]{:S(2)}, u32[]{:S(2)}) collective-permute-start(bf16[3,8,8,256]{3,2,1,0:T(8,128)(2,1)S(1)} %get-tuple-element.79), channel_id=1, source_target_pairs={{0,7},{1,2},{2,1},{3,4},{4,3},{5,6},{6,5},{7,0},{8,15},{9,10},{10,... | collective-permute-start | bytes 294920 | tf_op jit(solution)/shard_map/ppermute | solution.py:616
  12.0 4.5 %collective-permute-start.2 = (bf16[3,8,8,256]{3,2,1,0:T(8,128)(2,1)S(1)}, bf16[3,8,8,256]{3,2,1,0:T(8,128)(2,1)S(1)}, u32[]{:S(2)}, u32[]{:S(2)}) collective-permute-start(bf16[3,8,8,256]{3,2,1,0:T(8,128)(2,1)S(1)} %get-tuple-element.80), channel_id=1, source_target_pairs={{0,1},{1,0},{2,3},{3,2},{4,5},{5,4},{6,7},{7,6},{8,9},{9,8},{10,11... | collective-permute-start | bytes 294920 | tf_op jit(solution)/shard_map/ppermute | solution.py:616
  19.5 1.3 %collective-permute-start.4 = (bf16[32,128]{1,0:T(8,128)(2,1)S(1)}, bf16[32,128]{1,0:T(8,128)(2,1)S(1)}, u32[]{:S(2)}, u32[]{:S(2)}) collective-permute-start(bf16[32,128]{1,0:T(8,128)(2,1)S(1)} %get-tuple-element.54), channel_id=1, source_target_pairs={{0,1},{1,0},{2,3},{3,2},{4,5},{5,4},{6,7},{7,6},{8,9},{9,8},{10,11... | collective-permute-start | bytes 24584 | tf_op jit(solution)/shard_map/ppermute | solution.py:616
  20.7 7.1 %collective-permute-start.7 = (bf16[2,32,128]{2,1,0:T(8,128)(2,1)S(1)}, bf16[2,32,128]{2,1,0:T(8,128)(2,1)S(1)}, u32[]{:S(2)}, u32[]{:S(2)}) collective-permute-start(bf16[2,32,128]{2,1,0:T(8,128)(2,1)S(1)} %get-tuple-element.82), channel_id=1, source_target_pairs={{0,24},{1,25},{2,26},{3,27},{4,28},{5,29},{6,30},{7,31},{8,16},{9,... | collective-permute-start | bytes 49160 | tf_op jit(solution)/shard_map/ppermute | solution.py:616
  20.8 7.1 %collective-permute-start.6 = (bf16[2,32,128]{2,1,0:T(8,128)(2,1)S(1)}, bf16[2,32,128]{2,1,0:T(8,128)(2,1)S(1)}, u32[]{:S(2)}, u32[]{:S(2)}) collective-permute-start(bf16[2,32,128]{2,1,0:T(8,128)(2,1)S(1)} %get-tuple-element.82), channel_id=1, source_target_pairs={{0,16},{1,17},{2,18},{3,19},{4,20},{5,21},{6,22},{7,23},{8,24},{9,... | collective-permute-start | bytes 49160 | tf_op jit(solution)/shard_map/ppermute | solution.py:616
  22.9 5.0 %collective-permute-start.5 = (bf16[2,32,128]{2,1,0:T(8,128)(2,1)S(1)}, bf16[2,32,128]{2,1,0:T(8,128)(2,1)S(1)}, u32[]{:S(2)}, u32[]{:S(2)}) collective-permute-start(bf16[2,32,128]{2,1,0:T(8,128)(2,1)S(1)} %get-tuple-element.82), channel_id=1, source_target_pairs={{0,8},{1,9},{2,10},{3,11},{4,12},{5,13},{6,14},{7,15},{8,0},{9,1},... | collective-permute-start | bytes 49160 | tf_op jit(solution)/shard_map/ppermute | solution.py:616
  27.9 7.0 %collective-permute-start.10 = (bf16[4,2,32,128]{3,2,1,0:T(8,128)(2,1)S(1)}, bf16[4,2,32,128]{3,2,1,0:T(8,128)(2,1)S(1)}, u32[]{:S(2)}, u32[]{:S(2)}) collective-permute-start(bf16[4,2,32,128]{3,2,1,0:T(8,128)(2,1)S(1)} %pad_maximum_fusion.1.z0), channel_id=1, source_target_pairs={{0,96},{1,97},{2,98},{3,99},{4,100},{5,101},{6,102},{7,103},{8,104... | collective-permute-start | bytes 196616 | tf_op jit(solution)/shard_map/ppermute | solution.py:616
  30.0 5.8 %collective-permute-start.9 = (bf16[4,2,32,128]{3,2,1,0:T(8,128)(2,1)S(1)}, bf16[4,2,32,128]{3,2,1,0:T(8,128)(2,1)S(1)}, u32[]{:S(2)}, u32[]{:S(2)}) collective-permute-start(bf16[4,2,32,128]{3,2,1,0:T(8,128)(2,1)S(1)} %pad_maximum_fusion.1.z0), channel_id=1, source_target_pairs={{0,64},{1,65},{2,66},{3,67},{4,68},{5,69},{6,70},{7,71},{8,72},{9,... | collective-permute-start | bytes 196616 | tf_op jit(solution)/shard_map/ppermute | solution.py:616
  30.0 5.8 %collective-permute-start.8 = (bf16[4,2,32,128]{3,2,1,0:T(8,128)(2,1)S(1)}, bf16[4,2,32,128]{3,2,1,0:T(8,128)(2,1)S(1)}, u32[]{:S(2)}, u32[]{:S(2)}) collective-permute-start(bf16[4,2,32,128]{3,2,1,0:T(8,128)(2,1)S(1)} %pad_maximum_fusion.1.z0), channel_id=1, source_target_pairs={{0,32},{1,33},{2,34},{3,35},{4,36},{5,37},{6,38},{7,39},{8,40},{9,... | collective-permute-start | bytes 196616 | tf_op jit(solution)/shard_map/ppermute | solution.py:616
  34.8 10.4 %copy-start = (s32[8,1,64]{2,1,0:T(1,128)S(1)}, s32[8,1,64]{2,1,0:T(1,128)}, u32[]{:S(2)}) copy-start(s32[8,1,64]{2,1,0:T(1,128)} %param.19) | copy-start | bytes 6148
  37.0 8.2 %collective-permute-start.11 = (bf16[5,32,128]{2,1,0:T(8,128)(2,1)S(1)}, bf16[5,32,128]{2,1,0:T(8,128)(2,1)S(1)}, u32[]{:S(2)}, u32[]{:S(2)}) collective-permute-start(bf16[5,32,128]{2,1,0:T(8,128)(2,1)S(1)} %get-tuple-element.67), channel_id=1, source_target_pairs={{0,2},{1,3},{2,0},{3,1},{4,6},{5,7},{6,4},{7,5},{8,10},{9,11},{10,... | collective-permute-start | bytes 122888 | tf_op jit(solution)/shard_map/ppermute | solution.py:616
  38.1 7.1 %collective-permute-start.13 = (bf16[5,32,128]{2,1,0:T(8,128)(2,1)S(1)}, bf16[5,32,128]{2,1,0:T(8,128)(2,1)S(1)}, u32[]{:S(2)}, u32[]{:S(2)}) collective-permute-start(bf16[5,32,128]{2,1,0:T(8,128)(2,1)S(1)} %get-tuple-element.68), channel_id=1, source_target_pairs={{0,6},{1,7},{2,4},{3,5},{4,2},{5,3},{6,0},{7,1},{8,14},{9,15},{10,... | collective-permute-start | bytes 122888 | tf_op jit(solution)/shard_map/ppermute | solution.py:616
  39.9 5.2 %collective-permute-start.12 = (bf16[2,32,128]{2,1,0:T(8,128)(2,1)S(1)}, bf16[2,32,128]{2,1,0:T(8,128)(2,1)S(1)}, u32[]{:S(2)}, u32[]{:S(2)}) collective-permute-start(bf16[2,32,128]{2,1,0:T(8,128)(2,1)S(1)} %get-tuple-element.66.p5), channel_id=1, source_target_pairs={{0,4},{1,5},{2,6},{3,7},{4,0},{5,1},{6,2},{7,3},{8,12},{9,13},{10,... | collective-permute-start | bytes 49160 | tf_op jit(solution)/shard_map/ppermute | solution.py:616

commit v3 on v2

--- a/solution.py
+++ b/solution.py
@@ -14,10 +14,16 @@
 n_col = 8
 samples = 32
 vmem_bytes = 20 * 1024 * 1024
+high_masks = (0, 3, 1, 2)
+deep_masks = (0, 3, 1, 2)
 
 
 def dot(left, right):
     return jnp.dot(left, right, preferred_element_type=f32)
+
+
+def relu16(wide):
+    return jnp.maximum(wide.astype(bf16), 0)
 
 
 def low_half(shape):
@@ -95,8 +101,35 @@
     return copies
 
 
-def prep_up_body(
-    own, w_up, w_embed, merge_in, merge_out_t, own_out, wq, we, mi, mo, w_up_s, w_embed_s, mo_s, sems
+def prep_body(
+    own,
+    w_up,
+    w_embed,
+    merge_in,
+    merge_out_t,
+    w_down,
+    down_in,
+    down_out_t,
+    w_head_t,
+    own_out,
+    wq,
+    we,
+    mi,
+    mo,
+    wq_down,
+    di,
+    dc,
+    dp,
+    do0,
+    do,
+    wh,
+    w_up_s,
+    w_embed_s,
+    mo_s,
+    w_down_s,
+    do_s,
+    head_s,
+    sems,
 ):
     copies = copies_in(
         sems,
@@ -105,6 +138,10 @@
         (merge_out_t, mo_s),
         (own, own_out),
         (merge_in, mi),
+        (w_down, w_down_s),
+        (down_in, di),
+        (down_out_t, do_s),
+        (w_head_t, head_s),
     )
     copies[0].wait()
     for layer in range(3):
@@ -126,48 +163,24 @@
     mo[...] = dot_rows(mo_s[...], lane_copies(1, 1)).astype(bf16)
     copies[3].wait()
     copies[4].wait()
-
-
-def prep_down_body(
-    w_down,
-    down_in,
-    down_out_t,
-    w_head_t,
-    wq,
-    di,
-    di0,
-    do0,
-    do,
-    wh,
-    w_down_s,
-    do_s,
-    head_s,
-    sems,
-):
-    copies = copies_in(
-        sems, (w_down, w_down_s), (down_in, di), (down_out_t, do_s), (w_head_t, head_s)
-    )
-    copies[0].wait()
+    copies[5].wait()
     for layer in range(3):
-        fill_quad_weights(w_down_s, wq, layer, layer % 2 == 0)
-    copies[1].wait()
+        fill_quad_weights(w_down_s, wq_down, layer, layer % 2 == 0)
+    copies[6].wait()
     zero = jnp.zeros((64, 256), bf16)
-    parent = di[0:64, :]
     child = di[64:128, :]
-    di0[0:64, 0:256] = child
-    di0[0:64, 256:512] = zero
-    di0[64:128, 0:256] = zero
-    di0[64:128, 256:512] = child
-    di0[128:192, 0:256] = parent
-    di0[128:192, 256:512] = parent
-    di0[192:256, 0:256] = zero
-    di0[192:256, 256:512] = zero
-    copies[2].wait()
+    dc[0:64, 0:256] = child
+    dc[0:64, 256:512] = zero
+    dc[64:128, 0:256] = zero
+    dc[64:128, 256:512] = child
+    dp[0:64, :] = di[0:64, :]
+    dp[64:128, :] = zero
+    copies[7].wait()
     back = do_s[...]
     do0[0:256, :] = dot_rows(back, lane_copies(1, 0)).astype(bf16)
     do0[256:512, :] = dot_rows(back, lane_copies(0, 1)).astype(bf16)
     do[...] = dot_rows(back, lane_copies(1, 1)).astype(bf16)
-    copies[3].wait()
+    copies[8].wait()
     output = lax.broadcasted_iota(jnp.int32, (4, 128), 0)
     lane = lax.broadcasted_iota(jnp.int32, (4, 128), 1)
     head = dot_rows(head_s[...], jnp.where(lane % 4 == output, 1.0, 0.0).astype(bf16))
@@ -217,7 +230,7 @@
     row_even = place[0] % 2 == 0
     after_row = jnp.where(row_even, 16, 0)
     before_row = jnp.where(row_even, 0, 16)
-    for tile, start in ((0, 8), (1, after_row), (2, before_row)):
+    for tile, start in ((0, 8), (1, before_row), (2, after_row)):
         cells = tiles[tile].astype(f32)
         ext[pl.ds(start, 8), 1] = cells[:, 0:8]
         ext[pl.ds(start, 8), 2] = cells[:, 8:16]
@@ -230,7 +243,7 @@
     before_row = jnp.where(row_even, 0, 16)
     after_col = jnp.where(col_even, 3, 0)
     before_col = jnp.where(col_even, 0, 3)
-    for tile, start in ((0, 8), (1, after_row), (2, before_row)):
+    for tile, start in ((0, 8), (1, before_row), (2, after_row)):
         ext[pl.ds(start, 8), after_col] = col_a[tile].astype(f32)
         ext[pl.ds(start, 8), before_col] = col_b[tile].astype(f32)
 
@@ -267,7 +280,7 @@
     cols = c1 - c0
     for r0, r1 in row_chunks(*row_range, cols):
         stacked = src[r0:r1, c0:c1].reshape((r1 - r0) * cols * samples, 256)
-        hidden = jnp.maximum(dot(stacked, merge_in[...]), 0.0).astype(bf16)
+        hidden = relu16(dot(stacked, merge_in[...]))
         merged = dot(hidden, mo[...]).astype(bf16)
         dst[r0:r1, c0:c1] = merged.reshape(r1 - r0, cols, samples, 128)
 
@@ -293,7 +306,7 @@
 def merge_pair(top, bottom, merge_in, mo):
     count = top.shape[0]
     stacked = jnp.concatenate([top, bottom], axis=-1).reshape(count * samples, 256)
-    hidden = jnp.maximum(dot(stacked, merge_in), 0.0).astype(bf16)
+    hidden = relu16(dot(stacked, merge_in))
     return dot(hidden, mo).astype(bf16).reshape(count, samples, 128)
 
 
@@ -317,8 +330,8 @@
 def up_own_body(
     place,
     tiles,
+    col_b,
     col_a,
-    col_b,
     wq,
     we,
     merge_in,
@@ -369,7 +382,7 @@
     out[...] = paired_columns(l3)[0]
 
 
-def up_ring_first_body(place, tiles, col_a, col_b, wq, we, i0, s0, i1, s1, f1, ext, f0):
+def up_ring_first_body(place, tiles, col_b, col_a, wq, we, i0, s0, i1, s1, f1, ext, f0):
     spread_tiles(place, tiles, ext)
     spread_sides(place, col_a, col_b, ext)
     copy_rim(f0, i0, s0, 11, 15)
@@ -391,7 +404,7 @@
     f3[2:6, 8:10] = s3[1]
 
 
-def up_ring_merge_body(f3, merge_in, mo, own1, l1, l2):
+def up_ring_merge_body(f3, merge_in, mo, own1, dc, l1, l2, child0, child1):
     for block in blocks_ring(8, 12):
         merge_block(f3, l1, merge_in, mo, *block)
     l1[2:6, 2:10] = own1[...]
@@ -401,6 +414,12 @@
             [paired_columns(l1[2 * i + 1]), paired_columns(l1[2 * i + 3])], axis=0
         )
         l2[i : i + 2] = merge_pair(top, bottom, merge_in[...], mo[...]).reshape(2, 6, samples, 128)
+    for i in range(8):
+        for a in range(2):
+            if 0 <= i - (1 - a) < 7:
+                cells = f3[i, :, :, a * 128 : a * 128 + 128].reshape(12 * samples, 128)
+                child0[i - (1 - a), a] = dot(cells, dc[...]).astype(bf16)
+        child1[i] = dot(l1[i].reshape(12 * samples, 128), dc[:, 0:256]).astype(bf16)
 
 
 def mid_body(place, z0, z1, z2, z3, merge_in, mo, a3, a4, p5, send1, send3, strip, l4s):
@@ -410,10 +429,10 @@
     high = row % 4
     wide = col // 2
     core = col % 2
-    for m, ref in enumerate((z0, z1, z2, z3)):
-        for n in range(4):
+    for m, ref in zip(deep_masks, (z0, z1, z2, z3)):
+        for n, mask in enumerate(high_masks):
             for k in range(2):
-                strip[deep ^ m, high ^ n, core ^ k] = ref[n, k]
+                strip[deep ^ m, high ^ mask, core ^ k] = ref[n, k]
     cells = strip[...].reshape(8, 2, 2, samples, 128)
     l4 = merge_pair(
         cells[:, 0].reshape(16, samples, 128),
@@ -457,7 +476,7 @@
     count = parent.shape[0]
     low = low_half(parent.shape)
     joined = jnp.where(low, parent, child).reshape(count * samples, 128)
-    inner = jnp.maximum(dot(joined, down_in), 0.0).astype(bf16)
+    inner = relu16(dot(joined, down_in))
     outcome = dot(inner, do).reshape(count, samples, 128)
     return (outcome + child.astype(f32) + parent.astype(f32)).astype(bf16)
 
@@ -478,8 +497,10 @@
     mo,
     down_in,
     do,
-    di0,
+    dp,
     do0,
+    child0,
+    child1,
     wq,
     wh,
     out,
@@ -488,6 +509,9 @@
     c3s,
     p3s,
     c2s,
+    p2s,
+    c1s,
+    p1s,
     n0,
     r1,
     r2,
@@ -570,28 +594,41 @@
         parents2, l2[...].reshape(24, samples, 128), in_weights, out_weights
     ).reshape(4, 6, samples, 128)
 
-    sub = lax.broadcasted_iota(jnp.int32, (128, 128), 0)
-    lane = lax.broadcasted_iota(jnp.int32, (128, 128), 1)
-    averager = jnp.where((sub < 64) == (lane < 64), 1.0 / 64, 0.0).astype(bf16)
-
+    rows = 12 * samples
     low11 = low_half((11, samples, 128))
+    sub = lax.broadcasted_iota(jnp.int32, (256, 256), 0)
+    lane = lax.broadcasted_iota(jnp.int32, (256, 256), 1)
+    averager = jnp.where(sub // 64 == lane // 64, 1.0 / 64, 0.0).astype(bf16)
+    for i in range(4):
+        p2s[i] = dot(c2s[i].reshape(6 * samples, 128), dp[...]).reshape(6, samples, 256)
     for i in range(8):
-        parent = c2s[i // 2]
-        parent = jnp.broadcast_to(parent[:, None], (6, 2, samples, 128)).reshape(12, samples, 128)
-        c1 = refine(parent, l1[i], in_weights, out_weights)
-        c1_wide = c1.astype(f32).reshape(12 * samples, 128)
-        for a in range(2):
-            row_to = i - (1 - a)
-            if not 0 <= row_to < 7:
-                continue
-            child = f3[i, :, :, a * 128 : a * 128 + 128]
-            joined = jnp.concatenate([child, c1], axis=-1).reshape(12 * samples, 256)
-            inner = jnp.maximum(dot(joined, di0[...]), 0.0).astype(bf16)
-            fine = dot(inner, do0[...])
-            fine = fine + child.astype(f32).reshape(12 * samples, 128) + c1_wide
-            mean = dot((fine * fine).astype(bf16), averager)
-            normed = (fine * lax.rsqrt(mean + norm_eps)).astype(bf16).reshape(12, samples, 128)
-            n0[row_to, :, :, a * 128 : a * 128 + 128] = jnp.where(low11, normed[1:12], normed[0:11])
+        parent = c2s[i // 2].astype(f32)[:, None]
+        parent = jnp.broadcast_to(parent, (6, 2, samples, 128)).reshape(rows, 128)
+        part = jnp.broadcast_to(p2s[i // 2][:, None], (6, 2, samples, 256)).reshape(rows, 256)
+        inner = relu16(child1[i].astype(f32) + part)
+        c1 = dot(inner, out_weights) + l1[i].astype(f32).reshape(rows, 128) + parent
+        c1s[i] = c1.astype(bf16)
+    for i in range(8):
+        p1s[i] = dot(c1s[i], dp[...])
+    for i in range(8):
+        part = p1s[i]
+        part = jnp.concatenate([part, part], axis=-1)
+        context = c1s[i].astype(f32)
+        halves = [a for a in range(2) if 0 <= i - (1 - a) < 7]
+        fine = []
+        for a in halves:
+            inner = relu16(child0[i - (1 - a), a].astype(f32) + part)
+            child = f3[i, :, :, a * 128 : a * 128 + 128].astype(f32).reshape(rows, 128)
+            fine.append(dot(inner, do0[...]) + child + context)
+        fine = jnp.concatenate(fine, axis=-1)
+        width = fine.shape[-1]
+        mean = dot((fine * fine).astype(bf16), averager[:width, :width])
+        normed = (fine * lax.rsqrt(mean + norm_eps)).astype(bf16).reshape(12, samples, width)
+        for k, a in enumerate(halves):
+            part16 = normed[..., k * 128 : k * 128 + 128]
+            n0[i - (1 - a), :, :, a * 128 : a * 128 + 128] = jnp.where(
+                low11, part16[1:12], part16[0:11]
+            )
     conv_block(n0, r1, wq.at[0], (0, 6), (0, 10), False)
     conv_block(r1, r2, wq.at[1], (0, 5), (0, 9), True)
     conv_block(r2, r3, wq.at[2], (0, 4), (0, 8), False)
@@ -634,49 +671,49 @@
 
     row_a = swap(readouts, lambda r, c: (pair_after(r, n_row), c))
     row_b = swap(readouts, lambda r, c: (pair_before(r, n_row), c))
-    own, wq_up, we, mi, mo = whole_call(
-        prep_up_body,
+    own, wq_up, we, mi, mo, wq_down, di, dc, dp, do0, do, wh = whole_call(
+        prep_body,
         (
             arr((8, 16, 256)),
             arr((3, 1024, 256)),
             arr((512, 256)),
             arr((256, 256)),
             arr((256, 128)),
-        ),
-        [
-            pltpu.VMEM((3, 9, 64, 64), bf16),
-            pltpu.VMEM((8, 64), bf16),
-            pltpu.VMEM((64, 256), bf16),
-            pltpu.SemaphoreType.DMA((5,)),
-        ],
-        (readouts, w_up, w_embed, merge_in, merge_out.T),
-        outside=(0, 1, 2, 3, 4),
-    )
-    tiles = jnp.stack([own, row_a, row_b])
-    left = tiles[:, :, 0:8]
-    right = tiles[:, :, 8:16]
-    col_a = swap(jnp.where(col_even, right, left), lambda r, c: (r, pair_after(c, n_col)))
-    col_b = swap(jnp.where(col_even, left, right), lambda r, c: (r, pair_before(c, n_col)))
-    wq_down, di, di0, do0, do, wh = whole_call(
-        prep_down_body,
-        (
             arr((3, 1024, 256)),
             arr((128, 256)),
-            arr((256, 512)),
+            arr((128, 512)),
+            arr((128, 256)),
             arr((512, 128)),
             arr((256, 128)),
             arr((2048, 128)),
         ),
         [
             pltpu.VMEM((3, 9, 64, 64), bf16),
+            pltpu.VMEM((8, 64), bf16),
+            pltpu.VMEM((64, 256), bf16),
+            pltpu.VMEM((3, 9, 64, 64), bf16),
             pltpu.VMEM((64, 256), bf16),
             pltpu.VMEM((4, 64), bf16),
-            pltpu.SemaphoreType.DMA((4,)),
+            pltpu.SemaphoreType.DMA((9,)),
         ],
-        (w_down, down_in, down_out.T, w_head.T),
-        outside=(0, 1, 2, 3),
-    )
-
+        (
+            readouts,
+            w_up,
+            w_embed,
+            merge_in,
+            merge_out.T,
+            w_down,
+            down_in,
+            down_out.T,
+            w_head.T,
+        ),
+        outside=tuple(range(9)),
+    )
+    tiles = jnp.stack([own, row_b, row_a])
+    left = tiles[:, :, 0:8]
+    right = tiles[:, :, 8:16]
+    col_a = swap(jnp.where(col_even, right, left), lambda r, c: (r, pair_after(c, n_col)))
+    col_b = swap(jnp.where(col_even, left, right), lambda r, c: (r, pair_before(c, n_col)))
     quads = lambda rows, cols: pltpu.VMEM((rows, cols, samples, 256), bf16)
     ext = pltpu.VMEM((24, 4, 8, 256), f32)
     i0, i1, i2, i3, il1 = whole_call(
@@ -692,7 +729,7 @@
         (place, tiles, wq_up, we, mi, mo),
         smem=(0,),
     )
-    i0, col_a, col_b = lax.optimization_barrier((i0, col_a, col_b))
+    i0, col_b, col_a = lax.optimization_barrier((i0, col_b, col_a))
     s0, s1, s2, s3, own1, l3 = whole_call(
         up_own_body,
         (
@@ -704,22 +741,22 @@
             arr((samples, 128)),
         ),
         [ext],
-        (place, tiles, col_a, col_b, wq_up, we, mi, mo, i0, i1, i2, il1),
+        (place, tiles, col_b, col_a, wq_up, we, mi, mo, i0, i1, i2, il1),
         smem=(0,),
     )
 
     pair = jnp.stack([l3, swap(l3, lambda r, c: (r, c ^ 1))])
-    four = jnp.stack([pair] + [swap(pair, lambda r, c, m=m: (r ^ m, c)) for m in (1, 2, 3)])
+    four = jnp.stack([pair] + [swap(pair, lambda r, c, m=m: (r ^ m, c)) for m in high_masks[1:]])
     s0, pair = lax.optimization_barrier((s0, pair))
     f1 = whole_call(
         up_ring_first_body,
         arr((10, 14, samples, 256)),
         [ext, quads(11, 15)],
-        (place, tiles, col_a, col_b, wq_up, we, i0, s0, i1, s1),
+        (place, tiles, col_b, col_a, wq_up, we, i0, s0, i1, s1),
         smem=(0,),
     )
     four, f1 = lax.optimization_barrier((four, f1))
-    strips = [four] + [swap(four, lambda r, c, m=m: (r ^ (4 * m), c)) for m in (1, 2, 3)]
+    strips = [four] + [swap(four, lambda r, c, m=m: (r ^ (4 * m), c)) for m in deep_masks[1:]]
     f3 = whole_call(
         up_ring_second_body,
         arr((8, 12, samples, 256)),
@@ -743,11 +780,16 @@
     q1 = swap(send1, lambda r, c: (r, c ^ 2))
     q2 = swap(p5, lambda r, c: (r, c ^ 4))
     q3 = swap(send3, lambda r, c: (r, c ^ 6))
-    l1, l2 = whole_call(
+    l1, l2, child0, child1 = whole_call(
         up_ring_merge_body,
-        (arr((8, 12, samples, 128)), arr((4, 6, samples, 128))),
+        (
+            arr((8, 12, samples, 128)),
+            arr((4, 6, samples, 128)),
+            arr((7, 2, 12 * samples, 512)),
+            arr((8, 12 * samples, 256)),
+        ),
         [],
-        (f3, mi, mo, own1),
+        (f3, mi, mo, own1, dc),
     )
     slots = qubit_slot.reshape(qubit_slot.shape[0], qubit_slot.shape[2])
     return whole_call(
@@ -759,6 +801,9 @@
             pltpu.VMEM((6, 3, samples, 128), bf16),
             pltpu.VMEM((6, 3, samples, 128), bf16),
             pltpu.VMEM((4, 6, samples, 128), bf16),
+            pltpu.VMEM((4, 6, samples, 256), f32),
+            pltpu.VMEM((8, 12 * samples, 128), bf16),
+            pltpu.VMEM((8, 12 * samples, 256), f32),
             quads(7, 11),
             quads(6, 10),
             quads(5, 9),
@@ -780,8 +825,10 @@
             mo,
             di,
             do,
-            di0,
+            dp,
             do0,
+            child0,
+            child1,
             wq_down,
             wh,
         ),

time: 58.2 us -> 55.1 us (0.947)
  waiting for transfers between devices: 6.31 us -> 4.51 us
  Pallas kernels: 30.7 us -> 29.4 us
    ppermute x14, waiting for transfers between devices: 6.31 us -> 4.51 us  [swap(): return lax.ppermute(value, ('row', 'col'), pairs)]
    pallas_call x9 -> x8, Pallas kernels: 30.7 us -> 29.4 us  [whole_call(): pl.pallas_call(body, out_shape=out_shapes, in_specs=specs, out_specs=jax....]
  transfers between devices with their start and end apart: 14 -> 14, of which waited for: 6 -> 4; matrix products, arithmetic and copies ran while one was open for 0% -> 0% of each run, Pallas kernels for 23% -> 26%
where the time goes in v3:
time: 55.1 us; the launch traced here: 54.9 us
  Pallas kernels  29.4 us (53%)
  starting transfers between devices  20.8 us (38%)
  waiting for transfers between devices  4.51 us (8%)
    pallas_call x8, Pallas kernels, whole_call(): pl.pallas_call(body, out_shape=out_shapes, in_specs=specs, out_specs=jax....  29.4 us
    ppermute x14, starting transfers between devices, swap(): return lax.ppermute(value, ('row', 'col'), pairs)  20.8 us
    ppermute x14, waiting for transfers between devices, swap(): return lax.ppermute(value, ('row', 'col'), pairs)  4.51 us
  transfers between devices with their start and end apart: 14, of which 4 were waited for; matrix products, arithmetic and copies ran while one was open for 0% of the time, Pallas kernels for 26%

profile of v3, /device:TPU:0, one launch (start us, length us, event | category | flops | bytes accessed | tf_op | source)
XLA Modules:
  0.0 54.9 jit_solution(8307998114762533501)
XLA Ops:
  0.0 6.6 %collective-permute-start = (bf16[8,16,256]{2,1,0:T(8,128)(2,1)}, bf16[8,16,256]{2,1,0:T(8,128)(2,1)S(1)}, u32[]{:S(2)}, u32[]{:S(2)}) collective-permute-start(bf16[8,16,256]{2,1,0:T(8,128)(2,1)} %own.1), channel_id=1, source_target_pairs={{0,120},{1,121},{2,122},{3,123},{4,124},{5,125},{6,126},{7,127},{8... | collective-permute-start | bytes 196616 | tf_op jit(solution)/shard_map/ppermute | solution.py:653
  6.6 2.6 %shard_map.100 = (bf16[8,16,256]{2,1,0:T(8,128)(2,1)S(1)}, bf16[3,1024,256]{2,1,0:T(8,128)(2,1)S(1)}, bf16[512,256]{1,0:T(8,128)(2,1)S(1)}, bf16[256,256]{1,0:T(...) custom-call(bf16[8,16,256]{2,1,0:T(8,128)(2,1)} %own.1, ...), custom_call_target="tpu_custom_call" | custom-call | tf_op jit(solution)/shard_map/pallas_call | solution.py:44
  9.2 1.8 %collective-permute-done.1 = bf16[8,16,256]{2,1,0:T(8,128)(2,1)S(1)} collective-permute-done((bf16[8,16,256]{2,1,0:T(8,128)(2,1)}, bf16[8,16,256]{2,1,0:T(8,128)(2,1)S(1)}, u32[]{:S(2)}, u32[]{:S(2)}) %collective-permute-start.1) | collective-permute-done | bytes 65568 | tf_op jit(solution)/shard_map/ppermute | solution.py:653
  11.1 0.8 %collective-permute-start.2 = (bf16[3,8,8,256]{3,2,1,0:T(8,128)(2,1)S(1)}, bf16[3,8,8,256]{3,2,1,0:T(8,128)(2,1)S(1)}, u32[]{:S(2)}, u32[]{:S(2)}) collective-permute-start(bf16[3,8,8,256]{3,2,1,0:T(8,128)(2,1)S(1)} %get-tuple-element.86), channel_id=1, source_target_pairs={{0,7},{1,2},{2,1},{3,4},{4,3},{5,6},{6,5},{7,0},{8,15},{9,10},{10,... | collective-permute-start | bytes 294920 | tf_op jit(solution)/shard_map/ppermute | solution.py:653
  12.0 0.8 %collective-permute-start.3 = (bf16[3,8,8,256]{3,2,1,0:T(8,128)(2,1)S(1)}, bf16[3,8,8,256]{3,2,1,0:T(8,128)(2,1)S(1)}, u32[]{:S(2)}, u32[]{:S(2)}) collective-permute-start(bf16[3,8,8,256]{3,2,1,0:T(8,128)(2,1)S(1)} %get-tuple-element.85), channel_id=1, source_target_pairs={{0,1},{1,0},{2,3},{3,2},{4,5},{5,4},{6,7},{7,6},{8,9},{9,8},{10,11... | collective-permute-start | bytes 294920 | tf_op jit(solution)/shard_map/ppermute | solution.py:653
  12.9 3.2 %shard_map.101 = (bf16[7,7,32,256]{3,2,1,0:T(8,128)(2,1)S(1)}, bf16[6,6,32,256]{3,2,1,0:T(8,128)(2,1)S(1)}, bf16[5,5,32,256]{3,2,1,0:T(8,128)(2,1)S(1)}, bf16[4,...) custom-call(s32[2]{0:T(128)S(1)} %pad_add_fusion.place, bf16[3,8,16,256]{3,2,1,0:T(8,128)(2,1)S(1)} %pad_maximum_fusion.tiles, ...), custom_call_target="tpu_custom_call" | custom-call | tf_op jit(solution)/shard_map/pallas_call | solution.py:44
  16.0 0.4 collective-permute-done.2.col_b
  16.4 3.0 %shard_map.102 = (bf16[2,7,3,32,256]{4,3,2,1,0:T(8,128)(2,1)S(1)}, bf16[2,6,3,32,256]{4,3,2,1,0:T(8,128)(2,1)S(1)}, bf16[2,5,3,32,256]{4,3,2,1,0:T(8,128)(2,1)S(...) custom-call(s32[2]{0:T(128)S(1)} %pad_add_fusion.place, ...), custom_call_target="tpu_custom_call" | custom-call | tf_op jit(solution)/shard_map/pallas_call | solution.py:44
  19.5 0.1 collective-permute-start.4
  19.6 1.2 %collective-permute-done.4 = bf16[32,128]{1,0:T(8,128)(2,1)S(1)} collective-permute-done((bf16[32,128]{1,0:T(8,128)(2,1)S(1)}, bf16[32,128]{1,0:T(8,128)(2,1)S(1)}, u32[]{:S(2)}, u32[]{:S(2)}) %collective-permute-start.4) | collective-permute-done | bytes 8224 | tf_op jit(solution)/shard_map/ppermute | solution.py:653
  20.8 0.3 collective-permute-start.6
  21.0 4.4 %collective-permute-start.7 = (bf16[2,32,128]{2,1,0:T(8,128)(2,1)S(1)}, bf16[2,32,128]{2,1,0:T(8,128)(2,1)S(1)}, u32[]{:S(2)}, u32[]{:S(2)}) collective-permute-start(bf16[2,32,128]{2,1,0:T(8,128)(2,1)S(1)} %get-tuple-element.88), channel_id=1, source_target_pairs={{0,16},{1,17},{2,18},{3,19},{4,20},{5,21},{6,22},{7,23},{8,24},{9,... | collective-permute-start | bytes 49160 | tf_op jit(solution)/shard_map/ppermute | solution.py:653
  25.4 3.0 %shard_map.103.f1 = bf16[10,14,32,256]{3,2,1,0:T(8,128)(2,1)S(1)} custom-call(s32[2]{0:T(128)S(1)} %pad_add_fusion.place, bf16[3,8,16,256]{3,2,1,0:T(8,128)(2,1)S(1)} %pad_maximum_fusion.tiles, bf16[3,8,8,256]{3,2,1,0:T(8,128)(2,1)S(1)} %collective-permute-done.2.col_b, bf16[3,8,8,256]{3,2,1,0:T(8,128)(2,1)S(1)} %collective-permute-done.3.col_a, ...), custom_call_target="tpu_custom_call" | custom-call | tf_op jit(solution)/shard_map/pallas_call | solution.py:44
  28.5 0.1 collective-permute-start.10
  28.6 1.5 %collective-permute-start.8 = (bf16[4,2,32,128]{3,2,1,0:T(8,128)(2,1)S(1)}, bf16[4,2,32,128]{3,2,1,0:T(8,128)(2,1)S(1)}, u32[]{:S(2)}, u32[]{:S(2)}) collective-permute-start(bf16[4,2,32,128]{3,2,1,0:T(8,128)(2,1)S(1)} %pad_maximum_fusion.1.z0), channel_id=1, source_target_pairs={{0,96},{1,97},{2,98},{3,99},{4,100},{5,101},{6,102},{7,103},{8,104... | collective-permute-start | bytes 196616 | tf_op jit(solution)/shard_map/ppermute | solution.py:653
  30.1 2.0 %collective-permute-start.9 = (bf16[4,2,32,128]{3,2,1,0:T(8,128)(2,1)S(1)}, bf16[4,2,32,128]{3,2,1,0:T(8,128)(2,1)S(1)}, u32[]{:S(2)}, u32[]{:S(2)}) collective-permute-start(bf16[4,2,32,128]{3,2,1,0:T(8,128)(2,1)S(1)} %pad_maximum_fusion.1.z0), channel_id=1, source_target_pairs={{0,32},{1,33},{2,34},{3,35},{4,36},{5,37},{6,38},{7,39},{8,40},{9,... | collective-permute-start | bytes 196616 | tf_op jit(solution)/shard_map/ppermute | solution.py:653
  32.0 2.8 %shard_map.104.f3 = bf16[8,12,32,256]{3,2,1,0:T(8,128)(2,1)S(1)} custom-call(bf16[10,14,32,256]{3,2,1,0:T(8,128)(2,1)S(1)} %shard_map.103.f1, bf16[3,1024,256]{2,1,0:T(8,128)(2,1)S(1)} %get-tuple-element.46.wq, bf16[5,5,32,256]{3,2,1,0:T(8,128)(2,1)S(1)} %get-tuple-element.55.i2, bf16[2,5,3,32,256]{4,3,2,1,0:T(8,128)(2,1)S(1)} %get-tuple-element.63.s2, ...), custom_call_target="tpu_custom_call" | custom-call | tf_op jit(solution)/shard_map/pallas_call | solution.py:44
  34.9 1.2 %shard_map.105 = (bf16[3,2,32,128]{3,2,1,0:T(8,128)(2,1)S(1)}, bf16[3,2,32,128]{3,2,1,0:T(8,128)(2,1)S(1)}, bf16[2,32,128]{2,1,0:T(8,128)(2,1)S(1)}, bf16[5,32,1...) custom-call(s32[2]{0:T(128)S(1)} %pad_add_fusion.place, bf16[4,2,32,128]{3,2,1,0:T(8,128)(2,1)S(1)} %pad_maximum_fusion.1.z0, ...), custom_call_target="tpu_custom_call" | custom-call | tf_op jit(solution)/shard_map/pallas_call | solution.py:44
  36.1 1.2 %collective-permute-start.11 = (bf16[5,32,128]{2,1,0:T(8,128)(2,1)S(1)}, bf16[5,32,128]{2,1,0:T(8,128)(2,1)S(1)}, u32[]{:S(2)}, u32[]{:S(2)}) collective-permute-start(bf16[5,32,128]{2,1,0:T(8,128)(2,1)S(1)} %get-tuple-element.70), channel_id=1, source_target_pairs={{0,2},{1,3},{2,0},{3,1},{4,6},{5,7},{6,4},{7,5},{8,10},{9,11},{10,... | collective-permute-start | bytes 122888 | tf_op jit(solution)/shard_map/ppermute | solution.py:653
  37.2 1.8 %collective-permute-start.13 = (bf16[5,32,128]{2,1,0:T(8,128)(2,1)S(1)}, bf16[5,32,128]{2,1,0:T(8,128)(2,1)S(1)}, u32[]{:S(2)}, u32[]{:S(2)}) collective-permute-start(bf16[5,32,128]{2,1,0:T(8,128)(2,1)S(1)} %get-tuple-element.71), channel_id=1, source_target_pairs={{0,6},{1,7},{2,4},{3,5},{4,2},{5,3},{6,0},{7,1},{8,14},{9,15},{10,... | collective-permute-start | bytes 122888 | tf_op jit(solution)/shard_map/ppermute | solution.py:653
  39.0 1.2 %collective-permute-start.12 = (bf16[2,32,128]{2,1,0:T(8,128)(2,1)S(1)}, bf16[2,32,128]{2,1,0:T(8,128)(2,1)S(1)}, u32[]{:S(2)}, u32[]{:S(2)}) collective-permute-start(bf16[2,32,128]{2,1,0:T(8,128)(2,1)S(1)} %get-tuple-element.69.p5), channel_id=1, source_target_pairs={{0,4},{1,5},{2,6},{3,7},{4,0},{5,1},{6,2},{7,3},{8,12},{9,13},{10,... | collective-permute-start | bytes 49160 | tf_op jit(solution)/shard_map/ppermute | solution.py:653
  40.2 3.0 %shard_map.106 = (bf16[8,12,32,128]{3,2,1,0:T(8,128)(2,1)S(1)}, bf16[4,6,32,128]{3,2,1,0:T(8,128)(2,1)S(1)}, bf16[7,2,384,512]{3,2,1,0:T(8,128)(2,1)S(1)}, bf16[8,384,256]{2,1,0:T(8,128)(2,1)S(1)}) custom-call(bf16[8,12,32,256]{3,2,1,0:T(8,128)(2,1)S(1)} %shard_map.104.f3, bf16[256,256]{1,0:T(8,128)(2,1)S(1)} %get-tuple-element.48.merge_in, ...), custom_call_target="tpu_custom_call" | custom-call | tf_op jit(solution)/shard_map/pallas_call | solution.py:44
  43.2 1.1 %collective-permute-done.12.q2 = bf16[2,32,128]{2,1,0:T(8,128)(2,1)S(1)} collective-permute-done((bf16[2,32,128]{2,1,0:T(8,128)(2,1)S(1)}, bf16[2,32,128]{2,1,0:T(8,128)(2,1)S(1)}, u32[]{:S(2)}, u32[]{:S(2)}) %collective-permute-start.12) | collective-permute-done | bytes 16416 | tf_op jit(solution)/shard_map/ppermute | solution.py:653
  44.3 10.6 %shard_map.107 = f32[32,8,64]{2,1,0:T(8,128)} custom-call(s32[2]{0:T(128)S(1)} %pad_add_fusion.place, s32[8,64]{1,0:T(8,128)S(1)} %bitcast.18, bf16[3,2,32,128]{3,2,1,0:T(8,128)(2,1)S(1)} %get-tuple-element.67.a3, bf16[3,2,32,128]{3,2,1,0:T(8,128)(2,1)S(1)} %get-tuple-element.68.a4, bf16[2,32,128]{2,1,0:T(8,128)(2,1)S(1)} %get-tuple-element.69.p5, ...), custom_call_target="tpu_custom_call" | custom-call | tf_op jit(solution)/shard_map/pallas_call | solution.py:44
  (19 shorter events, 0.2 us)
Async XLA Ops:
  0.0 9.2 %collective-permute-start = (bf16[8,16,256]{2,1,0:T(8,128)(2,1)}, bf16[8,16,256]{2,1,0:T(8,128)(2,1)S(1)}, u32[]{:S(2)}, u32[]{:S(2)}) collective-permute-start(bf16[8,16,256]{2,1,0:T(8,128)(2,1)} %own.1), channel_id=1, source_target_pairs={{0,120},{1,121},{2,122},{3,123},{4,124},{5,125},{6,126},{7,127},{8... | collective-permute-start | bytes 196616 | tf_op jit(solution)/shard_map/ppermute | solution.py:653
  6.6 4.5 %collective-permute-start.1 = (bf16[8,16,256]{2,1,0:T(8,128)(2,1)}, bf16[8,16,256]{2,1,0:T(8,128)(2,1)S(1)}, u32[]{:S(2)}, u32[]{:S(2)}) collective-permute-start(bf16[8,16,256]{2,1,0:T(8,128)(2,1)} %own.1), channel_id=1, source_target_pairs={{0,8},{1,9},{2,10},{3,11},{4,12},{5,13},{6,14},{7,15},{8,0},{9,1},... | collective-permute-start | bytes 196616 | tf_op jit(solution)/shard_map/ppermute | solution.py:653
  11.1 5.3 %collective-permute-start.2 = (bf16[3,8,8,256]{3,2,1,0:T(8,128)(2,1)S(1)}, bf16[3,8,8,256]{3,2,1,0:T(8,128)(2,1)S(1)}, u32[]{:S(2)}, u32[]{:S(2)}) collective-permute-start(bf16[3,8,8,256]{3,2,1,0:T(8,128)(2,1)S(1)} %get-tuple-element.86), channel_id=1, source_target_pairs={{0,7},{1,2},{2,1},{3,4},{4,3},{5,6},{6,5},{7,0},{8,15},{9,10},{10,... | collective-permute-start | bytes 294920 | tf_op jit(solution)/shard_map/ppermute | solution.py:653
  12.0 4.5 %collective-permute-start.3 = (bf16[3,8,8,256]{3,2,1,0:T(8,128)(2,1)S(1)}, bf16[3,8,8,256]{3,2,1,0:T(8,128)(2,1)S(1)}, u32[]{:S(2)}, u32[]{:S(2)}) collective-permute-start(bf16[3,8,8,256]{3,2,1,0:T(8,128)(2,1)S(1)} %get-tuple-element.85), channel_id=1, source_target_pairs={{0,1},{1,0},{2,3},{3,2},{4,5},{5,4},{6,7},{7,6},{8,9},{9,8},{10,11... | collective-permute-start | bytes 294920 | tf_op jit(solution)/shard_map/ppermute | solution.py:653
  19.5 1.3 %collective-permute-start.4 = (bf16[32,128]{1,0:T(8,128)(2,1)S(1)}, bf16[32,128]{1,0:T(8,128)(2,1)S(1)}, u32[]{:S(2)}, u32[]{:S(2)}) collective-permute-start(bf16[32,128]{1,0:T(8,128)(2,1)S(1)} %get-tuple-element.57), channel_id=1, source_target_pairs={{0,1},{1,0},{2,3},{3,2},{4,5},{5,4},{6,7},{7,6},{8,9},{9,8},{10,11... | collective-permute-start | bytes 24584 | tf_op jit(solution)/shard_map/ppermute | solution.py:653
  20.7 7.7 %collective-permute-start.5 = (bf16[2,32,128]{2,1,0:T(8,128)(2,1)S(1)}, bf16[2,32,128]{2,1,0:T(8,128)(2,1)S(1)}, u32[]{:S(2)}, u32[]{:S(2)}) collective-permute-start(bf16[2,32,128]{2,1,0:T(8,128)(2,1)S(1)} %get-tuple-element.88), channel_id=1, source_target_pairs={{0,24},{1,25},{2,26},{3,27},{4,28},{5,29},{6,30},{7,31},{8,16},{9,... | collective-permute-start | bytes 49160 | tf_op jit(solution)/shard_map/ppermute | solution.py:653
  20.8 7.7 %collective-permute-start.6 = (bf16[2,32,128]{2,1,0:T(8,128)(2,1)S(1)}, bf16[2,32,128]{2,1,0:T(8,128)(2,1)S(1)}, u32[]{:S(2)}, u32[]{:S(2)}) collective-permute-start(bf16[2,32,128]{2,1,0:T(8,128)(2,1)S(1)} %get-tuple-element.88), channel_id=1, source_target_pairs={{0,8},{1,9},{2,10},{3,11},{4,12},{5,13},{6,14},{7,15},{8,0},{9,1},... | collective-permute-start | bytes 49160 | tf_op jit(solution)/shard_map/ppermute | solution.py:653
  21.0 7.4 %collective-permute-start.7 = (bf16[2,32,128]{2,1,0:T(8,128)(2,1)S(1)}, bf16[2,32,128]{2,1,0:T(8,128)(2,1)S(1)}, u32[]{:S(2)}, u32[]{:S(2)}) collective-permute-start(bf16[2,32,128]{2,1,0:T(8,128)(2,1)S(1)} %get-tuple-element.88), channel_id=1, source_target_pairs={{0,16},{1,17},{2,18},{3,19},{4,20},{5,21},{6,22},{7,23},{8,24},{9,... | collective-permute-start | bytes 49160 | tf_op jit(solution)/shard_map/ppermute | solution.py:653
  28.5 6.4 %collective-permute-start.10 = (bf16[4,2,32,128]{3,2,1,0:T(8,128)(2,1)S(1)}, bf16[4,2,32,128]{3,2,1,0:T(8,128)(2,1)S(1)}, u32[]{:S(2)}, u32[]{:S(2)}) collective-permute-start(bf16[4,2,32,128]{3,2,1,0:T(8,128)(2,1)S(1)} %pad_maximum_fusion.1.z0), channel_id=1, source_target_pairs={{0,64},{1,65},{2,66},{3,67},{4,68},{5,69},{6,70},{7,71},{8,72},{9,... | collective-permute-start | bytes 196616 | tf_op jit(solution)/shard_map/ppermute | solution.py:653
  28.6 6.2 %collective-permute-start.8 = (bf16[4,2,32,128]{3,2,1,0:T(8,128)(2,1)S(1)}, bf16[4,2,32,128]{3,2,1,0:T(8,128)(2,1)S(1)}, u32[]{:S(2)}, u32[]{:S(2)}) collective-permute-start(bf16[4,2,32,128]{3,2,1,0:T(8,128)(2,1)S(1)} %pad_maximum_fusion.1.z0), channel_id=1, source_target_pairs={{0,96},{1,97},{2,98},{3,99},{4,100},{5,101},{6,102},{7,103},{8,104... | collective-permute-start | bytes 196616 | tf_op jit(solution)/shard_map/ppermute | solution.py:653
  30.1 4.8 %collective-permute-start.9 = (bf16[4,2,32,128]{3,2,1,0:T(8,128)(2,1)S(1)}, bf16[4,2,32,128]{3,2,1,0:T(8,128)(2,1)S(1)}, u32[]{:S(2)}, u32[]{:S(2)}) collective-permute-start(bf16[4,2,32,128]{3,2,1,0:T(8,128)(2,1)S(1)} %pad_maximum_fusion.1.z0), channel_id=1, source_target_pairs={{0,32},{1,33},{2,34},{3,35},{4,36},{5,37},{6,38},{7,39},{8,40},{9,... | collective-permute-start | bytes 196616 | tf_op jit(solution)/shard_map/ppermute | solution.py:653
  34.8 9.5 %copy-start = (s32[8,1,64]{2,1,0:T(1,128)S(1)}, s32[8,1,64]{2,1,0:T(1,128)}, u32[]{:S(2)}) copy-start(s32[8,1,64]{2,1,0:T(1,128)} %param.19) | copy-start | bytes 6148
  36.1 8.2 %collective-permute-start.11 = (bf16[5,32,128]{2,1,0:T(8,128)(2,1)S(1)}, bf16[5,32,128]{2,1,0:T(8,128)(2,1)S(1)}, u32[]{:S(2)}, u32[]{:S(2)}) collective-permute-start(bf16[5,32,128]{2,1,0:T(8,128)(2,1)S(1)} %get-tuple-element.70), channel_id=1, source_target_pairs={{0,2},{1,3},{2,0},{3,1},{4,6},{5,7},{6,4},{7,5},{8,10},{9,11},{10,... | collective-permute-start | bytes 122888 | tf_op jit(solution)/shard_map/ppermute | solution.py:653
  37.2 7.1 %collective-permute-start.13 = (bf16[5,32,128]{2,1,0:T(8,128)(2,1)S(1)}, bf16[5,32,128]{2,1,0:T(8,128)(2,1)S(1)}, u32[]{:S(2)}, u32[]{:S(2)}) collective-permute-start(bf16[5,32,128]{2,1,0:T(8,128)(2,1)S(1)} %get-tuple-element.71), channel_id=1, source_target_pairs={{0,6},{1,7},{2,4},{3,5},{4,2},{5,3},{6,0},{7,1},{8,14},{9,15},{10,... | collective-permute-start | bytes 122888 | tf_op jit(solution)/shard_map/ppermute | solution.py:653
  39.0 5.2 %collective-permute-start.12 = (bf16[2,32,128]{2,1,0:T(8,128)(2,1)S(1)}, bf16[2,32,128]{2,1,0:T(8,128)(2,1)S(1)}, u32[]{:S(2)}, u32[]{:S(2)}) collective-permute-start(bf16[2,32,128]{2,1,0:T(8,128)(2,1)S(1)} %get-tuple-element.69.p5), channel_id=1, source_target_pairs={{0,4},{1,5},{2,6},{3,7},{4,0},{5,1},{6,2},{7,3},{8,12},{9,13},{10,... | collective-permute-start | bytes 49160 | tf_op jit(solution)/shard_map/ppermute | solution.py:653

commit v4 on v3

--- a/solution.py
+++ b/solution.py
@@ -14,7 +14,7 @@
 n_col = 8
 samples = 32
 vmem_bytes = 20 * 1024 * 1024
-high_masks = (0, 3, 1, 2)
+high_masks = (0, 2, 3, 1)
 deep_masks = (0, 3, 1, 2)
 
 
@@ -123,6 +123,8 @@
     do0,
     do,
     wh,
+    w2,
+    w7,
     w_up_s,
     w_embed_s,
     mo_s,
@@ -180,6 +182,9 @@
     do0[0:256, :] = dot_rows(back, lane_copies(1, 0)).astype(bf16)
     do0[256:512, :] = dot_rows(back, lane_copies(0, 1)).astype(bf16)
     do[...] = dot_rows(back, lane_copies(1, 1)).astype(bf16)
+    w2[0:128, :] = dp[...]
+    w2[128:384, :] = dot(do[...], dp[...]).astype(bf16)
+    w7[...] = dot(mo[...], dp[...]).astype(bf16)
     copies[8].wait()
     output = lax.broadcasted_iota(jnp.int32, (4, 128), 0)
     lane = lax.broadcasted_iota(jnp.int32, (4, 128), 1)
@@ -382,12 +387,13 @@
     out[...] = paired_columns(l3)[0]
 
 
-def up_ring_first_body(place, tiles, col_b, col_a, wq, we, i0, s0, i1, s1, f1, ext, f0):
-    spread_tiles(place, tiles, ext)
-    spread_sides(place, col_a, col_b, ext)
+def up_ring_embed_body(ext, we, i0, s0, f0):
     copy_rim(f0, i0, s0, 11, 15)
     for block in blocks_ring(11, 15):
         embed_block(ext, we, f0, *block)
+
+
+def up_ring_first_body(f0, wq, i1, s1, f1):
     for block in blocks_ring(10, 14):
         conv_block(f0, f1, wq.at[0], *block, False)
     copy_rim(f1, i1, s1, 10, 14)
@@ -472,15 +478,6 @@
     return jnp.where(low, wide, turned).astype(bf16), jnp.where(low, turned, wide).astype(bf16)
 
 
-def refine(parent, child, down_in, do):
-    count = parent.shape[0]
-    low = low_half(parent.shape)
-    joined = jnp.where(low, parent, child).reshape(count * samples, 128)
-    inner = relu16(dot(joined, down_in))
-    outcome = dot(inner, do).reshape(count, samples, 128)
-    return (outcome + child.astype(f32) + parent.astype(f32)).astype(bf16)
-
-
 def descent_body(
     place,
     slots,
@@ -495,9 +492,11 @@
     l2,
     merge_in,
     mo,
-    down_in,
     do,
+    dc,
     dp,
+    w2,
+    w7,
     do0,
     child0,
     child1,
@@ -506,8 +505,7 @@
     out,
     l5s,
     c6s,
-    c3s,
-    p3s,
+    g6s,
     c2s,
     p2s,
     c1s,
@@ -524,7 +522,9 @@
     wide_even = wide % 2 == 0
     merge_weights = merge_in[...]
     back_weights = mo[...]
-    in_weights = down_in[...]
+    child_weights = dc[:, 0:256]
+    parent_weights = dp[...]
+    step_weights = w2[...]
     out_weights = do[...]
 
     for m, ref, start in ((0, p5, 0), (1, q1, 3), (2, q2, 0), (3, q3, 3)):
@@ -546,26 +546,39 @@
     )
     l6 = merge_pair(top, bottom, merge_weights, back_weights)
     low1 = low_half((1, samples, 128))
-    l7 = merge_pair(
-        jnp.where(low1, l6[0:1], l6[2:3]),
-        jnp.where(low1, l6[1:2], l6[3:4]),
-        merge_weights,
-        back_weights,
-    )
-    c6s[...] = refine(
-        jnp.broadcast_to(l7, (4, samples, 128)), l6, in_weights, out_weights
-    ).reshape(2, 2, samples, 128)
+    stacked7 = jnp.concatenate(
+        [jnp.where(low1, l6[0:1], l6[2:3]), jnp.where(low1, l6[1:2], l6[3:4])], axis=-1
+    )
+    hidden7 = relu16(dot(stacked7.reshape(samples, 256), merge_weights))
+    part7 = dot(hidden7, w7[...]).reshape(1, samples, 256)
+    c7 = dot(hidden7, back_weights).reshape(1, samples, 128)
+
+    def descend(parent, part, child):
+        count = child.shape[0]
+        flat = child.reshape(count * samples, 128)
+        ahead = dot(flat, child_weights).reshape(count, samples, 256)
+        inner = relu16(ahead + part).reshape(count * samples, 256)
+        step = dot(jnp.concatenate([flat, inner], axis=-1), step_weights)
+        part = part + step.reshape(count, samples, 256)
+        outcome = dot(inner, out_weights).reshape(count, samples, 128)
+        return outcome + child.astype(f32) + parent, part
+
+    c6, part6 = descend(c7, part7, l6)
+    c6s[...] = c6.reshape(2, 2, samples, 128)
+    g6s[...] = part6.reshape(2, 2, samples, 256)
 
     side = jnp.where(core == 0, (wide + 3) % 4, (wide + 1) % 4)
     lines = [(row + d + (n_row - 1)) % n_row for d in range(3)]
     parents5 = []
+    parts5 = []
     children5 = []
     for place_x in (wide, side):
         for line in lines:
             deep = line // 4
             parents5.append(c6s[place_x // 2, deep // 2])
+            parts5.append(g6s[place_x // 2, deep // 2])
             children5.append(l5s[place_x, deep])
-    c5 = refine(jnp.stack(parents5), jnp.stack(children5), in_weights, out_weights)
+    c5, part5 = descend(jnp.stack(parents5), jnp.stack(parts5), jnp.stack(children5))
 
     from_first = jnp.logical_xor(wide_even, core == 0)
     side_cells = jnp.where(from_first, q1[0:3], q3[0:3])
@@ -573,51 +586,56 @@
     side4 = jnp.where(core == 0, side_low, side_high)
     side3 = jnp.where(core == 0, side_high, side_low)
     own4 = a4[...]
-    children4 = jnp.concatenate([own4[:, 0], own4[:, 1], side4], axis=0)
-    parents4 = jnp.concatenate([c5[0:3], c5[0:3], c5[3:6]], axis=0)
-    c4 = refine(parents4, children4, in_weights, out_weights)
+    children4 = jnp.concatenate([own4[:, 0], own4[:, 1], side4, side4], axis=0)
+    parents4 = jnp.concatenate([c5[0:3], c5, c5[3:6]], axis=0)
+    parts4 = jnp.concatenate([part5[0:3], part5, part5[3:6]], axis=0)
+    c4, part4 = descend(parents4, parts4, children4)
     own3_0, own3_1 = both_lanes(a3[:, 0])
     own3_2, own3_3 = both_lanes(a3[:, 1])
-    for k, cells in enumerate((side3, own3_0, own3_1, own3_2, own3_3, side3)):
-        c3s[k] = cells
-    for k, start in enumerate((6, 0, 0, 3, 3, 6)):
-        p3s[k] = c4[start : start + 3]
-    window = pl.ds(2 * core, 4)
-    c3 = refine(
-        p3s[window].reshape(12, samples, 128),
-        c3s[window].reshape(12, samples, 128),
-        in_weights,
-        out_weights,
-    ).reshape(4, 3, samples, 128)
-    parents2 = jnp.stack([c3[j, i] for i in (0, 1, 1, 2) for j in (0, 1, 1, 2, 2, 3)])
-    c2s[...] = refine(
-        parents2, l2[...].reshape(24, samples, 128), in_weights, out_weights
-    ).reshape(4, 6, samples, 128)
+    first_core = core == 0
+
+    def window(blocks):
+        left = jnp.concatenate(blocks[0:4], axis=0)
+        right = jnp.concatenate(blocks[2:6], axis=0)
+        return jnp.where(first_core, left, right)
+
+    starts = (6, 0, 0, 3, 3, 6)
+    c3, part3 = descend(
+        window([c4[k : k + 3] for k in starts]),
+        window([part4[k : k + 3] for k in starts]),
+        window([side3, own3_0, own3_1, own3_2, own3_3, side3]),
+    )
+    above = [3 * j + i for i in (0, 1, 1, 2) for j in (0, 1, 1, 2, 2, 3)]
+    c2, part2 = descend(
+        jnp.stack([c3[k] for k in above]),
+        jnp.stack([part3[k] for k in above]),
+        l2[...].reshape(24, samples, 128),
+    )
+    c2s[...] = c2.reshape(4, 6, samples, 128)
+    p2s[...] = part2.astype(bf16).reshape(4, 6, samples, 256)
 
     rows = 12 * samples
     low11 = low_half((11, samples, 128))
     sub = lax.broadcasted_iota(jnp.int32, (256, 256), 0)
     lane = lax.broadcasted_iota(jnp.int32, (256, 256), 1)
     averager = jnp.where(sub // 64 == lane // 64, 1.0 / 64, 0.0).astype(bf16)
-    for i in range(4):
-        p2s[i] = dot(c2s[i].reshape(6 * samples, 128), dp[...]).reshape(6, samples, 256)
     for i in range(8):
-        parent = c2s[i // 2].astype(f32)[:, None]
+        parent = c2s[i // 2][:, None]
         parent = jnp.broadcast_to(parent, (6, 2, samples, 128)).reshape(rows, 128)
         part = jnp.broadcast_to(p2s[i // 2][:, None], (6, 2, samples, 256)).reshape(rows, 256)
-        inner = relu16(child1[i].astype(f32) + part)
+        inner = relu16(child1[i] + part)
         c1 = dot(inner, out_weights) + l1[i].astype(f32).reshape(rows, 128) + parent
         c1s[i] = c1.astype(bf16)
     for i in range(8):
-        p1s[i] = dot(c1s[i], dp[...])
+        p1s[i] = dot(c1s[i], parent_weights)
     for i in range(8):
         part = p1s[i]
-        part = jnp.concatenate([part, part], axis=-1)
+        part = jnp.concatenate([part, part], axis=-1).astype(bf16)
         context = c1s[i].astype(f32)
         halves = [a for a in range(2) if 0 <= i - (1 - a) < 7]
         fine = []
         for a in halves:
-            inner = relu16(child0[i - (1 - a), a].astype(f32) + part)
+            inner = relu16(child0[i - (1 - a), a] + part)
             child = f3[i, :, :, a * 128 : a * 128 + 128].astype(f32).reshape(rows, 128)
             fine.append(dot(inner, do0[...]) + child + context)
         fine = jnp.concatenate(fine, axis=-1)
@@ -671,7 +689,7 @@
 
     row_a = swap(readouts, lambda r, c: (pair_after(r, n_row), c))
     row_b = swap(readouts, lambda r, c: (pair_before(r, n_row), c))
-    own, wq_up, we, mi, mo, wq_down, di, dc, dp, do0, do, wh = whole_call(
+    own, wq_up, we, mi, mo, wq_down, di, dc, dp, do0, do, wh, w2, w7 = whole_call(
         prep_body,
         (
             arr((8, 16, 256)),
@@ -686,6 +704,8 @@
             arr((512, 128)),
             arr((256, 128)),
             arr((2048, 128)),
+            arr((384, 256)),
+            arr((256, 256)),
         ),
         [
             pltpu.VMEM((3, 9, 64, 64), bf16),
@@ -730,7 +750,7 @@
         smem=(0,),
     )
     i0, col_b, col_a = lax.optimization_barrier((i0, col_b, col_a))
-    s0, s1, s2, s3, own1, l3 = whole_call(
+    s0, s1, s2, s3, own1, l3, cells = whole_call(
         up_own_body,
         (
             arr((2, 7, 3, samples, 256)),
@@ -739,21 +759,24 @@
             arr((2, 4, 2, samples, 256)),
             arr((4, 8, samples, 128)),
             arr((samples, 128)),
+            arr((24, 4, 8, 256), f32),
         ),
-        [ext],
+        [],
         (place, tiles, col_b, col_a, wq_up, we, mi, mo, i0, i1, i2, il1),
         smem=(0,),
     )
 
     pair = jnp.stack([l3, swap(l3, lambda r, c: (r, c ^ 1))])
+    f0 = whole_call(
+        up_ring_embed_body,
+        arr((11, 15, samples, 256)),
+        [],
+        (cells, we, i0, s0),
+    )
+    pair, f0 = lax.optimization_barrier((pair, f0))
     four = jnp.stack([pair] + [swap(pair, lambda r, c, m=m: (r ^ m, c)) for m in high_masks[1:]])
-    s0, pair = lax.optimization_barrier((s0, pair))
     f1 = whole_call(
-        up_ring_first_body,
-        arr((10, 14, samples, 256)),
-        [ext, quads(11, 15)],
-        (place, tiles, col_b, col_a, wq_up, we, i0, s0, i1, s1),
-        smem=(0,),
+        up_ring_first_body, arr((10, 14, samples, 256)), [], (f0, wq_up, i1, s1)
     )
     four, f1 = lax.optimization_barrier((four, f1))
     strips = [four] + [swap(four, lambda r, c, m=m: (r ^ (4 * m), c)) for m in deep_masks[1:]]
@@ -797,11 +820,10 @@
         arr((samples, 8, 64), f32),
         [
             pltpu.VMEM((4, 4, samples, 128), bf16),
-            pltpu.VMEM((2, 2, samples, 128), bf16),
-            pltpu.VMEM((6, 3, samples, 128), bf16),
-            pltpu.VMEM((6, 3, samples, 128), bf16),
-            pltpu.VMEM((4, 6, samples, 128), bf16),
-            pltpu.VMEM((4, 6, samples, 256), f32),
+            pltpu.VMEM((2, 2, samples, 128), f32),
+            pltpu.VMEM((2, 2, samples, 256), f32),
+            pltpu.VMEM((4, 6, samples, 128), f32),
+            pltpu.VMEM((4, 6, samples, 256), bf16),
             pltpu.VMEM((8, 12 * samples, 128), bf16),
             pltpu.VMEM((8, 12 * samples, 256), f32),
             quads(7, 11),
@@ -823,9 +845,11 @@
             l2,
             mi,
             mo,
-            di,
             do,
+            dc,
             dp,
+            w2,
+            w7,
             do0,
             child0,
             child1,

time: 55.1 us -> 53.8 us (0.976)
  starting transfers between devices: 20.8 us -> 19.6 us
  Pallas kernels: 29.4 us -> 28.8 us
  waiting for transfers between devices: 4.51 us -> 5.08 us
    ppermute x14, starting transfers between devices: 20.8 us -> 19.6 us  [swap(): return lax.ppermute(value, ('row', 'col'), pairs)]
    ppermute x14, waiting for transfers between devices: 4.51 us -> 5.08 us  [swap(): return lax.ppermute(value, ('row', 'col'), pairs)]
    pallas_call x8 -> x9, Pallas kernels: 29.4 us -> 28.8 us  [whole_call(): pl.pallas_call(body, out_shape=out_shapes, in_specs=specs, out_specs=jax....]
  transfers between devices with their start and end apart: 14 -> 14, of which waited for: 4 -> 8; matrix products, arithmetic and copies ran while one was open for 0% -> 0% of each run, Pallas kernels for 26% -> 27%
where the time goes in v4:
time: 53.8 us; the launch traced here: 53.7 us
  Pallas kernels  28.8 us (54%)
  starting transfers between devices  19.6 us (36%)
  waiting for transfers between devices  5.08 us (9%)
    pallas_call x9, Pallas kernels, whole_call(): pl.pallas_call(body, out_shape=out_shapes, in_specs=specs, out_specs=jax....  28.8 us
    ppermute x14, starting transfers between devices, swap(): return lax.ppermute(value, ('row', 'col'), pairs)  19.6 us
    ppermute x14, waiting for transfers between devices, swap(): return lax.ppermute(value, ('row', 'col'), pairs)  5.08 us
  transfers between devices with their start and end apart: 14, of which 8 were waited for; matrix products, arithmetic and copies ran while one was open for 0% of the time, Pallas kernels for 27%

profile of v4, /device:TPU:0, one launch (start us, length us, event | category | flops | bytes accessed | tf_op | source)
XLA Modules:
  0.0 53.7 jit_solution(4530141493092120906)
XLA Ops:
  0.0 6.6 %collective-permute-start = (bf16[8,16,256]{2,1,0:T(8,128)(2,1)}, bf16[8,16,256]{2,1,0:T(8,128)(2,1)S(1)}, u32[]{:S(2)}, u32[]{:S(2)}) collective-permute-start(bf16[8,16,256]{2,1,0:T(8,128)(2,1)} %own.1), channel_id=1, source_target_pairs={{0,120},{1,121},{2,122},{3,123},{4,124},{5,125},{6,126},{7,127},{8... | collective-permute-start | bytes 196616 | tf_op jit(solution)/shard_map/ppermute | solution.py:671
  6.6 3.2 %shard_map.100 = (bf16[8,16,256]{2,1,0:T(8,128)(2,1)S(1)}, bf16[3,1024,256]{2,1,0:T(8,128)(2,1)S(1)}, bf16[512,256]{1,0:T(8,128)(2,1)S(1)}, bf16[256,256]{1,0:T(...) custom-call(bf16[8,16,256]{2,1,0:T(8,128)(2,1)} %own.1, ...), custom_call_target="tpu_custom_call" | custom-call | tf_op jit(solution)/shard_map/pallas_call | solution.py:44
  9.8 1.3 %collective-permute-done.1 = bf16[8,16,256]{2,1,0:T(8,128)(2,1)S(1)} collective-permute-done((bf16[8,16,256]{2,1,0:T(8,128)(2,1)}, bf16[8,16,256]{2,1,0:T(8,128)(2,1)S(1)}, u32[]{:S(2)}, u32[]{:S(2)}) %collective-permute-start.1) | collective-permute-done | bytes 65568 | tf_op jit(solution)/shard_map/ppermute | solution.py:671
  11.1 0.8 %collective-permute-start.2 = (bf16[3,8,8,256]{3,2,1,0:T(8,128)(2,1)S(1)}, bf16[3,8,8,256]{3,2,1,0:T(8,128)(2,1)S(1)}, u32[]{:S(2)}, u32[]{:S(2)}) collective-permute-start(bf16[3,8,8,256]{3,2,1,0:T(8,128)(2,1)S(1)} %get-tuple-element.92), channel_id=1, source_target_pairs={{0,7},{1,2},{2,1},{3,4},{4,3},{5,6},{6,5},{7,0},{8,15},{9,10},{10,... | collective-permute-start | bytes 294920 | tf_op jit(solution)/shard_map/ppermute | solution.py:671
  12.0 0.8 %collective-permute-start.3 = (bf16[3,8,8,256]{3,2,1,0:T(8,128)(2,1)S(1)}, bf16[3,8,8,256]{3,2,1,0:T(8,128)(2,1)S(1)}, u32[]{:S(2)}, u32[]{:S(2)}) collective-permute-start(bf16[3,8,8,256]{3,2,1,0:T(8,128)(2,1)S(1)} %get-tuple-element.91), channel_id=1, source_target_pairs={{0,1},{1,0},{2,3},{3,2},{4,5},{5,4},{6,7},{7,6},{8,9},{9,8},{10,11... | collective-permute-start | bytes 294920 | tf_op jit(solution)/shard_map/ppermute | solution.py:671
  12.9 3.1 %shard_map.101 = (bf16[7,7,32,256]{3,2,1,0:T(8,128)(2,1)S(1)}, bf16[6,6,32,256]{3,2,1,0:T(8,128)(2,1)S(1)}, bf16[5,5,32,256]{3,2,1,0:T(8,128)(2,1)S(1)}, bf16[4,...) custom-call(s32[2]{0:T(128)S(1)} %pad_add_fusion.place, bf16[3,8,16,256]{3,2,1,0:T(8,128)(2,1)S(1)} %pad_maximum_fusion.tiles, ...), custom_call_target="tpu_custom_call" | custom-call | tf_op jit(solution)/shard_map/pallas_call | solution.py:44
  15.9 0.5 collective-permute-done.2.col_b
  16.4 3.1 %shard_map.102 = (bf16[2,7,3,32,256]{4,3,2,1,0:T(8,128)(2,1)S(1)}, bf16[2,6,3,32,256]{4,3,2,1,0:T(8,128)(2,1)S(1)}, bf16[2,5,3,32,256]{4,3,2,1,0:T(8,128)(2,1)S(...) custom-call(s32[2]{0:T(128)S(1)} %pad_add_fusion.place, ...), custom_call_target="tpu_custom_call" | custom-call | tf_op jit(solution)/shard_map/pallas_call | solution.py:44
  19.6 1.0 %shard_map.103.f0 = bf16[11,15,32,256]{3,2,1,0:T(8,128)(2,1)S(1)} custom-call(f32[24,4,8,256]{3,2,1,0:T(8,128)S(1)} %get-tuple-element.61.ext, bf16[512,256]{1,0:T(8,128)(2,1)S(1)} %get-tuple-element.50.we, bf16[7,7,32,256]{3,2,1,0:T(8,128)(2,1)S(1)} %get-tuple-element.56.i0, bf16[2,7,3,32,256]{4,3,2,1,0:T(8,128)(2,1)S(1)} %get-tuple-element.62.s0), custom_call_target="tpu_custom_call" | custom-call | tf_op jit(solution)/shard_map/pallas_call | solution.py:44
  20.6 0.2 collective-permute-done.4
  20.8 3.4 %collective-permute-start.6 = (bf16[2,32,128]{2,1,0:T(8,128)(2,1)S(1)}, bf16[2,32,128]{2,1,0:T(8,128)(2,1)S(1)}, u32[]{:S(2)}, u32[]{:S(2)}) collective-permute-start(bf16[2,32,128]{2,1,0:T(8,128)(2,1)S(1)} %pad_maximum_fusion.2), channel_id=1, source_target_pairs={{0,24},{1,25},{2,26},{3,27},{4,28},{5,29},{6,30},{7,31},{8,16},{9,... | collective-permute-start | bytes 49160 | tf_op jit(solution)/shard_map/ppermute | solution.py:671
  24.3 1.7 %shard_map.104.f1 = bf16[10,14,32,256]{3,2,1,0:T(8,128)(2,1)S(1)} custom-call(bf16[11,15,32,256]{3,2,1,0:T(8,128)(2,1)S(1)} %shard_map.103.f0, bf16[3,1024,256]{2,1,0:T(8,128)(2,1)S(1)} %get-tuple-element.49.wq, bf16[6,6,32,256]{3,2,1,0:T(8,128)(2,1)S(1)} %get-tuple-element.57.i1, bf16[2,6,3,32,256]{4,3,2,1,0:T(8,128)(2,1)S(1)} %get-tuple-element.65.s1), custom_call_target="tpu_custom_call" | custom-call | tf_op jit(solution)/shard_map/pallas_call | solution.py:44
  26.1 1.8 %collective-permute-done.7 = bf16[2,32,128]{2,1,0:T(8,128)(2,1)S(1)} collective-permute-done((bf16[2,32,128]{2,1,0:T(8,128)(2,1)S(1)}, bf16[2,32,128]{2,1,0:T(8,128)(2,1)S(1)}, u32[]{:S(2)}, u32[]{:S(2)}) %collective-permute-start.7) | collective-permute-done | bytes 16416 | tf_op jit(solution)/shard_map/ppermute | solution.py:671
  28.0 0.7 %collective-permute-start.8 = (bf16[4,2,32,128]{3,2,1,0:T(8,128)(2,1)S(1)}, bf16[4,2,32,128]{3,2,1,0:T(8,128)(2,1)S(1)}, u32[]{:S(2)}, u32[]{:S(2)}) collective-permute-start(bf16[4,2,32,128]{3,2,1,0:T(8,128)(2,1)S(1)} %pad_maximum_fusion.1.z0), channel_id=1, source_target_pairs={{0,96},{1,97},{2,98},{3,99},{4,100},{5,101},{6,102},{7,103},{8,104... | collective-permute-start | bytes 196616 | tf_op jit(solution)/shard_map/ppermute | solution.py:671
  28.7 2.8 %collective-permute-start.9 = (bf16[4,2,32,128]{3,2,1,0:T(8,128)(2,1)S(1)}, bf16[4,2,32,128]{3,2,1,0:T(8,128)(2,1)S(1)}, u32[]{:S(2)}, u32[]{:S(2)}) collective-permute-start(bf16[4,2,32,128]{3,2,1,0:T(8,128)(2,1)S(1)} %pad_maximum_fusion.1.z0), channel_id=1, source_target_pairs={{0,32},{1,33},{2,34},{3,35},{4,36},{5,37},{6,38},{7,39},{8,40},{9,... | collective-permute-start | bytes 196616 | tf_op jit(solution)/shard_map/ppermute | solution.py:671
  31.5 2.6 %shard_map.105.f3 = bf16[8,12,32,256]{3,2,1,0:T(8,128)(2,1)S(1)} custom-call(bf16[10,14,32,256]{3,2,1,0:T(8,128)(2,1)S(1)} %shard_map.104.f1, bf16[3,1024,256]{2,1,0:T(8,128)(2,1)S(1)} %get-tuple-element.49.wq, bf16[5,5,32,256]{3,2,1,0:T(8,128)(2,1)S(1)} %get-tuple-element.58.i2, bf16[2,5,3,32,256]{4,3,2,1,0:T(8,128)(2,1)S(1)} %get-tuple-element.68.s2, ...), custom_call_target="tpu_custom_call" | custom-call | tf_op jit(solution)/shard_map/pallas_call | solution.py:44
  34.2 0.1 collective-permute-done.8.z1
  34.3 1.2 %shard_map.106 = (bf16[3,2,32,128]{3,2,1,0:T(8,128)(2,1)S(1)}, bf16[3,2,32,128]{3,2,1,0:T(8,128)(2,1)S(1)}, bf16[2,32,128]{2,1,0:T(8,128)(2,1)S(1)}, bf16[5,32,1...) custom-call(s32[2]{0:T(128)S(1)} %pad_add_fusion.place, bf16[4,2,32,128]{3,2,1,0:T(8,128)(2,1)S(1)} %pad_maximum_fusion.1.z0, ...), custom_call_target="tpu_custom_call" | custom-call | tf_op jit(solution)/shard_map/pallas_call | solution.py:44
  35.5 1.1 %collective-permute-start.11 = (bf16[5,32,128]{2,1,0:T(8,128)(2,1)S(1)}, bf16[5,32,128]{2,1,0:T(8,128)(2,1)S(1)}, u32[]{:S(2)}, u32[]{:S(2)}) collective-permute-start(bf16[5,32,128]{2,1,0:T(8,128)(2,1)S(1)} %get-tuple-element.75), channel_id=1, source_target_pairs={{0,2},{1,3},{2,0},{3,1},{4,6},{5,7},{6,4},{7,5},{8,10},{9,11},{10,... | collective-permute-start | bytes 122888 | tf_op jit(solution)/shard_map/ppermute | solution.py:671
  36.6 1.8 %collective-permute-start.13 = (bf16[5,32,128]{2,1,0:T(8,128)(2,1)S(1)}, bf16[5,32,128]{2,1,0:T(8,128)(2,1)S(1)}, u32[]{:S(2)}, u32[]{:S(2)}) collective-permute-start(bf16[5,32,128]{2,1,0:T(8,128)(2,1)S(1)} %get-tuple-element.76), channel_id=1, source_target_pairs={{0,6},{1,7},{2,4},{3,5},{4,2},{5,3},{6,0},{7,1},{8,14},{9,15},{10,... | collective-permute-start | bytes 122888 | tf_op jit(solution)/shard_map/ppermute | solution.py:671
  38.4 1.2 %collective-permute-start.12 = (bf16[2,32,128]{2,1,0:T(8,128)(2,1)S(1)}, bf16[2,32,128]{2,1,0:T(8,128)(2,1)S(1)}, u32[]{:S(2)}, u32[]{:S(2)}) collective-permute-start(bf16[2,32,128]{2,1,0:T(8,128)(2,1)S(1)} %get-tuple-element.74.p5), channel_id=1, source_target_pairs={{0,4},{1,5},{2,6},{3,7},{4,0},{5,1},{6,2},{7,3},{8,12},{9,13},{10,... | collective-permute-start | bytes 49160 | tf_op jit(solution)/shard_map/ppermute | solution.py:671
  39.7 2.9 %shard_map.107 = (bf16[8,12,32,128]{3,2,1,0:T(8,128)(2,1)S(1)}, bf16[4,6,32,128]{3,2,1,0:T(8,128)(2,1)S(1)}, bf16[7,2,384,512]{3,2,1,0:T(8,128)(2,1)S(1)}, bf16[8,384,256]{2,1,0:T(8,128)(2,1)S(1)}) custom-call(bf16[8,12,32,256]{3,2,1,0:T(8,128)(2,1)S(1)} %shard_map.105.f3, bf16[256,256]{1,0:T(8,128)(2,1)S(1)} %get-tuple-element.51.merge_in, ...), custom_call_target="tpu_custom_call" | custom-call | tf_op jit(solution)/shard_map/pallas_call | solution.py:44
  42.6 1.0 %collective-permute-done.12.q2 = bf16[2,32,128]{2,1,0:T(8,128)(2,1)S(1)} collective-permute-done((bf16[2,32,128]{2,1,0:T(8,128)(2,1)S(1)}, bf16[2,32,128]{2,1,0:T(8,128)(2,1)S(1)}, u32[]{:S(2)}, u32[]{:S(2)}) %collective-permute-start.12) | collective-permute-done | bytes 16416 | tf_op jit(solution)/shard_map/ppermute | solution.py:671
  43.7 10.0 %shard_map.108 = f32[32,8,64]{2,1,0:T(8,128)} custom-call(s32[2]{0:T(128)S(1)} %pad_add_fusion.place, s32[8,64]{1,0:T(8,128)S(1)} %bitcast.17, bf16[3,2,32,128]{3,2,1,0:T(8,128)(2,1)S(1)} %get-tuple-element.72.a3, bf16[3,2,32,128]{3,2,1,0:T(8,128)(2,1)S(1)} %get-tuple-element.73.a4, bf16[2,32,128]{2,1,0:T(8,128)(2,1)S(1)} %get-tuple-element.74.p5, ...), custom_call_target="tpu_custom_call" | custom-call | tf_op jit(solution)/shard_map/pallas_call | solution.py:44
  (20 shorter events, 0.5 us)
Async XLA Ops:
  0.0 9.8 %collective-permute-start = (bf16[8,16,256]{2,1,0:T(8,128)(2,1)}, bf16[8,16,256]{2,1,0:T(8,128)(2,1)S(1)}, u32[]{:S(2)}, u32[]{:S(2)}) collective-permute-start(bf16[8,16,256]{2,1,0:T(8,128)(2,1)} %own.1), channel_id=1, source_target_pairs={{0,120},{1,121},{2,122},{3,123},{4,124},{5,125},{6,126},{7,127},{8... | collective-permute-start | bytes 196616 | tf_op jit(solution)/shard_map/ppermute | solution.py:671
  6.6 4.5 %collective-permute-start.1 = (bf16[8,16,256]{2,1,0:T(8,128)(2,1)}, bf16[8,16,256]{2,1,0:T(8,128)(2,1)S(1)}, u32[]{:S(2)}, u32[]{:S(2)}) collective-permute-start(bf16[8,16,256]{2,1,0:T(8,128)(2,1)} %own.1), channel_id=1, source_target_pairs={{0,8},{1,9},{2,10},{3,11},{4,12},{5,13},{6,14},{7,15},{8,0},{9,1},... | collective-permute-start | bytes 196616 | tf_op jit(solution)/shard_map/ppermute | solution.py:671
  11.1 5.3 %collective-permute-start.2 = (bf16[3,8,8,256]{3,2,1,0:T(8,128)(2,1)S(1)}, bf16[3,8,8,256]{3,2,1,0:T(8,128)(2,1)S(1)}, u32[]{:S(2)}, u32[]{:S(2)}) collective-permute-start(bf16[3,8,8,256]{3,2,1,0:T(8,128)(2,1)S(1)} %get-tuple-element.92), channel_id=1, source_target_pairs={{0,7},{1,2},{2,1},{3,4},{4,3},{5,6},{6,5},{7,0},{8,15},{9,10},{10,... | collective-permute-start | bytes 294920 | tf_op jit(solution)/shard_map/ppermute | solution.py:671
  12.0 4.5 %collective-permute-start.3 = (bf16[3,8,8,256]{3,2,1,0:T(8,128)(2,1)S(1)}, bf16[3,8,8,256]{3,2,1,0:T(8,128)(2,1)S(1)}, u32[]{:S(2)}, u32[]{:S(2)}) collective-permute-start(bf16[3,8,8,256]{3,2,1,0:T(8,128)(2,1)S(1)} %get-tuple-element.91), channel_id=1, source_target_pairs={{0,1},{1,0},{2,3},{3,2},{4,5},{5,4},{6,7},{7,6},{8,9},{9,8},{10,11... | collective-permute-start | bytes 294920 | tf_op jit(solution)/shard_map/ppermute | solution.py:671
  19.5 1.3 %collective-permute-start.4 = (bf16[32,128]{1,0:T(8,128)(2,1)S(1)}, bf16[32,128]{1,0:T(8,128)(2,1)S(1)}, u32[]{:S(2)}, u32[]{:S(2)}) collective-permute-start(bf16[32,128]{1,0:T(8,128)(2,1)S(1)} %get-tuple-element.60), channel_id=1, source_target_pairs={{0,1},{1,0},{2,3},{3,2},{4,5},{5,4},{6,7},{7,6},{8,9},{9,8},{10,11... | collective-permute-start | bytes 24584 | tf_op jit(solution)/shard_map/ppermute | solution.py:671
  20.8 5.3 %collective-permute-start.5 = (bf16[2,32,128]{2,1,0:T(8,128)(2,1)S(1)}, bf16[2,32,128]{2,1,0:T(8,128)(2,1)S(1)}, u32[]{:S(2)}, u32[]{:S(2)}) collective-permute-start(bf16[2,32,128]{2,1,0:T(8,128)(2,1)S(1)} %pad_maximum_fusion.2), channel_id=1, source_target_pairs={{0,16},{1,17},{2,18},{3,19},{4,20},{5,21},{6,22},{7,23},{8,24},{9,... | collective-permute-start | bytes 49160 | tf_op jit(solution)/shard_map/ppermute | solution.py:671
  20.8 5.3 %collective-permute-start.6 = (bf16[2,32,128]{2,1,0:T(8,128)(2,1)S(1)}, bf16[2,32,128]{2,1,0:T(8,128)(2,1)S(1)}, u32[]{:S(2)}, u32[]{:S(2)}) collective-permute-start(bf16[2,32,128]{2,1,0:T(8,128)(2,1)S(1)} %pad_maximum_fusion.2), channel_id=1, source_target_pairs={{0,24},{1,25},{2,26},{3,27},{4,28},{5,29},{6,30},{7,31},{8,16},{9,... | collective-permute-start | bytes 49160 | tf_op jit(solution)/shard_map/ppermute | solution.py:671
  24.2 3.7 %collective-permute-start.7 = (bf16[2,32,128]{2,1,0:T(8,128)(2,1)S(1)}, bf16[2,32,128]{2,1,0:T(8,128)(2,1)S(1)}, u32[]{:S(2)}, u32[]{:S(2)}) collective-permute-start(bf16[2,32,128]{2,1,0:T(8,128)(2,1)S(1)} %pad_maximum_fusion.2), channel_id=1, source_target_pairs={{0,8},{1,9},{2,10},{3,11},{4,12},{5,13},{6,14},{7,15},{8,0},{9,1},... | collective-permute-start | bytes 49160 | tf_op jit(solution)/shard_map/ppermute | solution.py:671
  27.9 6.2 %collective-permute-start.10 = (bf16[4,2,32,128]{3,2,1,0:T(8,128)(2,1)S(1)}, bf16[4,2,32,128]{3,2,1,0:T(8,128)(2,1)S(1)}, u32[]{:S(2)}, u32[]{:S(2)}) collective-permute-start(bf16[4,2,32,128]{3,2,1,0:T(8,128)(2,1)S(1)} %pad_maximum_fusion.1.z0), channel_id=1, source_target_pairs={{0,64},{1,65},{2,66},{3,67},{4,68},{5,69},{6,70},{7,71},{8,72},{9,... | collective-permute-start | bytes 196616 | tf_op jit(solution)/shard_map/ppermute | solution.py:671
  28.0 6.3 %collective-permute-start.8 = (bf16[4,2,32,128]{3,2,1,0:T(8,128)(2,1)S(1)}, bf16[4,2,32,128]{3,2,1,0:T(8,128)(2,1)S(1)}, u32[]{:S(2)}, u32[]{:S(2)}) collective-permute-start(bf16[4,2,32,128]{3,2,1,0:T(8,128)(2,1)S(1)} %pad_maximum_fusion.1.z0), channel_id=1, source_target_pairs={{0,96},{1,97},{2,98},{3,99},{4,100},{5,101},{6,102},{7,103},{8,104... | collective-permute-start | bytes 196616 | tf_op jit(solution)/shard_map/ppermute | solution.py:671
  28.7 5.6 %collective-permute-start.9 = (bf16[4,2,32,128]{3,2,1,0:T(8,128)(2,1)S(1)}, bf16[4,2,32,128]{3,2,1,0:T(8,128)(2,1)S(1)}, u32[]{:S(2)}, u32[]{:S(2)}) collective-permute-start(bf16[4,2,32,128]{3,2,1,0:T(8,128)(2,1)S(1)} %pad_maximum_fusion.1.z0), channel_id=1, source_target_pairs={{0,32},{1,33},{2,34},{3,35},{4,36},{5,37},{6,38},{7,39},{8,40},{9,... | collective-permute-start | bytes 196616 | tf_op jit(solution)/shard_map/ppermute | solution.py:671
  34.2 9.5 %copy-start = (s32[8,1,64]{2,1,0:T(1,128)S(1)}, s32[8,1,64]{2,1,0:T(1,128)}, u32[]{:S(2)}) copy-start(s32[8,1,64]{2,1,0:T(1,128)} %param.19) | copy-start | bytes 6148
  35.5 8.2 %collective-permute-start.11 = (bf16[5,32,128]{2,1,0:T(8,128)(2,1)S(1)}, bf16[5,32,128]{2,1,0:T(8,128)(2,1)S(1)}, u32[]{:S(2)}, u32[]{:S(2)}) collective-permute-start(bf16[5,32,128]{2,1,0:T(8,128)(2,1)S(1)} %get-tuple-element.75), channel_id=1, source_target_pairs={{0,2},{1,3},{2,0},{3,1},{4,6},{5,7},{6,4},{7,5},{8,10},{9,11},{10,... | collective-permute-start | bytes 122888 | tf_op jit(solution)/shard_map/ppermute | solution.py:671
  36.6 7.1 %collective-permute-start.13 = (bf16[5,32,128]{2,1,0:T(8,128)(2,1)S(1)}, bf16[5,32,128]{2,1,0:T(8,128)(2,1)S(1)}, u32[]{:S(2)}, u32[]{:S(2)}) collective-permute-start(bf16[5,32,128]{2,1,0:T(8,128)(2,1)S(1)} %get-tuple-element.76), channel_id=1, source_target_pairs={{0,6},{1,7},{2,4},{3,5},{4,2},{5,3},{6,0},{7,1},{8,14},{9,15},{10,... | collective-permute-start | bytes 122888 | tf_op jit(solution)/shard_map/ppermute | solution.py:671
  38.4 5.2 %collective-permute-start.12 = (bf16[2,32,128]{2,1,0:T(8,128)(2,1)S(1)}, bf16[2,32,128]{2,1,0:T(8,128)(2,1)S(1)}, u32[]{:S(2)}, u32[]{:S(2)}) collective-permute-start(bf16[2,32,128]{2,1,0:T(8,128)(2,1)S(1)} %get-tuple-element.74.p5), channel_id=1, source_target_pairs={{0,4},{1,5},{2,6},{3,7},{4,0},{5,1},{6,2},{7,3},{8,12},{9,13},{10,... | collective-permute-start | bytes 49160 | tf_op jit(solution)/shard_map/ppermute | solution.py:671

commit v5 on v4

--- a/solution.py
+++ b/solution.py
@@ -619,16 +619,18 @@
     sub = lax.broadcasted_iota(jnp.int32, (256, 256), 0)
     lane = lax.broadcasted_iota(jnp.int32, (256, 256), 1)
     averager = jnp.where(sub // 64 == lane // 64, 1.0 / 64, 0.0).astype(bf16)
-    for i in range(8):
+    def context_row(i):
         parent = c2s[i // 2][:, None]
         parent = jnp.broadcast_to(parent, (6, 2, samples, 128)).reshape(rows, 128)
         part = jnp.broadcast_to(p2s[i // 2][:, None], (6, 2, samples, 256)).reshape(rows, 256)
         inner = relu16(child1[i] + part)
         c1 = dot(inner, out_weights) + l1[i].astype(f32).reshape(rows, 128) + parent
         c1s[i] = c1.astype(bf16)
-    for i in range(8):
+
+    def part_row(i):
         p1s[i] = dot(c1s[i], parent_weights)
-    for i in range(8):
+
+    def fine_row(i):
         part = p1s[i]
         part = jnp.concatenate([part, part], axis=-1).astype(bf16)
         context = c1s[i].astype(f32)
@@ -647,9 +649,20 @@
             n0[i - (1 - a), :, :, a * 128 : a * 128 + 128] = jnp.where(
                 low11, part16[1:12], part16[0:11]
             )
-    conv_block(n0, r1, wq.at[0], (0, 6), (0, 10), False)
-    conv_block(r1, r2, wq.at[1], (0, 5), (0, 9), True)
-    conv_block(r2, r3, wq.at[2], (0, 4), (0, 8), False)
+
+    for t in range(15):
+        if t < 8:
+            context_row(t)
+        if 0 <= t - 1 < 8:
+            part_row(t - 1)
+        if 0 <= t - 2 < 8:
+            fine_row(t - 2)
+        if 0 <= t - 5 < 6:
+            conv_block(n0, r1, wq.at[0], (t - 5, t - 4), (0, 10), False)
+        if 0 <= t - 7 < 5:
+            conv_block(r1, r2, wq.at[1], (t - 7, t - 6), (0, 9), True)
+        if 0 <= t - 9 < 4:
+            conv_block(r2, r3, wq.at[2], (t - 9, t - 8), (0, 8), False)
     stacked = jnp.concatenate(
         [r3[:, quad].reshape(4 * samples, 256) for quad in range(8)], axis=-1
     )

time: 53.8 us -> 53.7 us (level)
  no operation moved by 1% of the time
where the time goes in v5:
time: 53.7 us; the launch traced here: 53.6 us
  Pallas kernels  28.7 us (53%)
  starting transfers between devices  19.6 us (36%)
  waiting for transfers between devices  5.08 us (9%)
    pallas_call x9, Pallas kernels, whole_call(): pl.pallas_call(body, out_shape=out_shapes, in_specs=specs, out_specs=jax....  28.7 us
    ppermute x14, starting transfers between devices, swap(): return lax.ppermute(value, ('row', 'col'), pairs)  19.6 us
    ppermute x14, waiting for transfers between devices, swap(): return lax.ppermute(value, ('row', 'col'), pairs)  5.08 us
  transfers between devices with their start and end apart: 14, of which 8 were waited for; matrix products, arithmetic and copies ran while one was open for 0% of the time, Pallas kernels for 27%

profile of v5, /device:TPU:0, one launch (start us, length us, event | category | flops | bytes accessed | tf_op | source)
XLA Modules:
  0.0 53.6 jit_solution(18001045687413432036)
XLA Ops:
  0.0 6.6 %collective-permute-start = (bf16[8,16,256]{2,1,0:T(8,128)(2,1)}, bf16[8,16,256]{2,1,0:T(8,128)(2,1)S(1)}, u32[]{:S(2)}, u32[]{:S(2)}) collective-permute-start(bf16[8,16,256]{2,1,0:T(8,128)(2,1)} %own.1), channel_id=1, source_target_pairs={{0,120},{1,121},{2,122},{3,123},{4,124},{5,125},{6,126},{7,127},{8... | collective-permute-start | bytes 196616 | tf_op jit(solution)/shard_map/ppermute | solution.py:684
  6.6 3.2 %shard_map.100 = (bf16[8,16,256]{2,1,0:T(8,128)(2,1)S(1)}, bf16[3,1024,256]{2,1,0:T(8,128)(2,1)S(1)}, bf16[512,256]{1,0:T(8,128)(2,1)S(1)}, bf16[256,256]{1,0:T(...) custom-call(bf16[8,16,256]{2,1,0:T(8,128)(2,1)} %own.1, ...), custom_call_target="tpu_custom_call" | custom-call | tf_op jit(solution)/shard_map/pallas_call | solution.py:44
  9.8 1.3 %collective-permute-done.1 = bf16[8,16,256]{2,1,0:T(8,128)(2,1)S(1)} collective-permute-done((bf16[8,16,256]{2,1,0:T(8,128)(2,1)}, bf16[8,16,256]{2,1,0:T(8,128)(2,1)S(1)}, u32[]{:S(2)}, u32[]{:S(2)}) %collective-permute-start.1) | collective-permute-done | bytes 65568 | tf_op jit(solution)/shard_map/ppermute | solution.py:684
  11.1 0.8 %collective-permute-start.2 = (bf16[3,8,8,256]{3,2,1,0:T(8,128)(2,1)S(1)}, bf16[3,8,8,256]{3,2,1,0:T(8,128)(2,1)S(1)}, u32[]{:S(2)}, u32[]{:S(2)}) collective-permute-start(bf16[3,8,8,256]{3,2,1,0:T(8,128)(2,1)S(1)} %get-tuple-element.92), channel_id=1, source_target_pairs={{0,7},{1,2},{2,1},{3,4},{4,3},{5,6},{6,5},{7,0},{8,15},{9,10},{10,... | collective-permute-start | bytes 294920 | tf_op jit(solution)/shard_map/ppermute | solution.py:684
  12.0 0.8 %collective-permute-start.3 = (bf16[3,8,8,256]{3,2,1,0:T(8,128)(2,1)S(1)}, bf16[3,8,8,256]{3,2,1,0:T(8,128)(2,1)S(1)}, u32[]{:S(2)}, u32[]{:S(2)}) collective-permute-start(bf16[3,8,8,256]{3,2,1,0:T(8,128)(2,1)S(1)} %get-tuple-element.91), channel_id=1, source_target_pairs={{0,1},{1,0},{2,3},{3,2},{4,5},{5,4},{6,7},{7,6},{8,9},{9,8},{10,11... | collective-permute-start | bytes 294920 | tf_op jit(solution)/shard_map/ppermute | solution.py:684
  12.9 3.1 %shard_map.101 = (bf16[7,7,32,256]{3,2,1,0:T(8,128)(2,1)S(1)}, bf16[6,6,32,256]{3,2,1,0:T(8,128)(2,1)S(1)}, bf16[5,5,32,256]{3,2,1,0:T(8,128)(2,1)S(1)}, bf16[4,...) custom-call(s32[2]{0:T(128)S(1)} %pad_add_fusion.place, bf16[3,8,16,256]{3,2,1,0:T(8,128)(2,1)S(1)} %pad_maximum_fusion.tiles, ...), custom_call_target="tpu_custom_call" | custom-call | tf_op jit(solution)/shard_map/pallas_call | solution.py:44
  15.9 0.5 collective-permute-done.2.col_b
  16.4 3.1 %shard_map.102 = (bf16[2,7,3,32,256]{4,3,2,1,0:T(8,128)(2,1)S(1)}, bf16[2,6,3,32,256]{4,3,2,1,0:T(8,128)(2,1)S(1)}, bf16[2,5,3,32,256]{4,3,2,1,0:T(8,128)(2,1)S(...) custom-call(s32[2]{0:T(128)S(1)} %pad_add_fusion.place, ...), custom_call_target="tpu_custom_call" | custom-call | tf_op jit(solution)/shard_map/pallas_call | solution.py:44
  19.6 1.0 %shard_map.103.f0 = bf16[11,15,32,256]{3,2,1,0:T(8,128)(2,1)S(1)} custom-call(f32[24,4,8,256]{3,2,1,0:T(8,128)S(1)} %get-tuple-element.61.ext, bf16[512,256]{1,0:T(8,128)(2,1)S(1)} %get-tuple-element.50.we, bf16[7,7,32,256]{3,2,1,0:T(8,128)(2,1)S(1)} %get-tuple-element.56.i0, bf16[2,7,3,32,256]{4,3,2,1,0:T(8,128)(2,1)S(1)} %get-tuple-element.62.s0), custom_call_target="tpu_custom_call" | custom-call | tf_op jit(solution)/shard_map/pallas_call | solution.py:44
  20.6 0.2 collective-permute-done.4
  20.8 3.4 %collective-permute-start.6 = (bf16[2,32,128]{2,1,0:T(8,128)(2,1)S(1)}, bf16[2,32,128]{2,1,0:T(8,128)(2,1)S(1)}, u32[]{:S(2)}, u32[]{:S(2)}) collective-permute-start(bf16[2,32,128]{2,1,0:T(8,128)(2,1)S(1)} %pad_maximum_fusion.2), channel_id=1, source_target_pairs={{0,24},{1,25},{2,26},{3,27},{4,28},{5,29},{6,30},{7,31},{8,16},{9,... | collective-permute-start | bytes 49160 | tf_op jit(solution)/shard_map/ppermute | solution.py:684
  24.3 1.7 %shard_map.104.f1 = bf16[10,14,32,256]{3,2,1,0:T(8,128)(2,1)S(1)} custom-call(bf16[11,15,32,256]{3,2,1,0:T(8,128)(2,1)S(1)} %shard_map.103.f0, bf16[3,1024,256]{2,1,0:T(8,128)(2,1)S(1)} %get-tuple-element.49.wq, bf16[6,6,32,256]{3,2,1,0:T(8,128)(2,1)S(1)} %get-tuple-element.57.i1, bf16[2,6,3,32,256]{4,3,2,1,0:T(8,128)(2,1)S(1)} %get-tuple-element.65.s1), custom_call_target="tpu_custom_call" | custom-call | tf_op jit(solution)/shard_map/pallas_call | solution.py:44
  26.1 1.8 %collective-permute-done.7 = bf16[2,32,128]{2,1,0:T(8,128)(2,1)S(1)} collective-permute-done((bf16[2,32,128]{2,1,0:T(8,128)(2,1)S(1)}, bf16[2,32,128]{2,1,0:T(8,128)(2,1)S(1)}, u32[]{:S(2)}, u32[]{:S(2)}) %collective-permute-start.7) | collective-permute-done | bytes 16416 | tf_op jit(solution)/shard_map/ppermute | solution.py:684
  28.0 0.7 %collective-permute-start.8 = (bf16[4,2,32,128]{3,2,1,0:T(8,128)(2,1)S(1)}, bf16[4,2,32,128]{3,2,1,0:T(8,128)(2,1)S(1)}, u32[]{:S(2)}, u32[]{:S(2)}) collective-permute-start(bf16[4,2,32,128]{3,2,1,0:T(8,128)(2,1)S(1)} %pad_maximum_fusion.1.z0), channel_id=1, source_target_pairs={{0,96},{1,97},{2,98},{3,99},{4,100},{5,101},{6,102},{7,103},{8,104... | collective-permute-start | bytes 196616 | tf_op jit(solution)/shard_map/ppermute | solution.py:684
  28.7 2.8 %collective-permute-start.9 = (bf16[4,2,32,128]{3,2,1,0:T(8,128)(2,1)S(1)}, bf16[4,2,32,128]{3,2,1,0:T(8,128)(2,1)S(1)}, u32[]{:S(2)}, u32[]{:S(2)}) collective-permute-start(bf16[4,2,32,128]{3,2,1,0:T(8,128)(2,1)S(1)} %pad_maximum_fusion.1.z0), channel_id=1, source_target_pairs={{0,32},{1,33},{2,34},{3,35},{4,36},{5,37},{6,38},{7,39},{8,40},{9,... | collective-permute-start | bytes 196616 | tf_op jit(solution)/shard_map/ppermute | solution.py:684
  31.5 2.6 %shard_map.105.f3 = bf16[8,12,32,256]{3,2,1,0:T(8,128)(2,1)S(1)} custom-call(bf16[10,14,32,256]{3,2,1,0:T(8,128)(2,1)S(1)} %shard_map.104.f1, bf16[3,1024,256]{2,1,0:T(8,128)(2,1)S(1)} %get-tuple-element.49.wq, bf16[5,5,32,256]{3,2,1,0:T(8,128)(2,1)S(1)} %get-tuple-element.58.i2, bf16[2,5,3,32,256]{4,3,2,1,0:T(8,128)(2,1)S(1)} %get-tuple-element.68.s2, ...), custom_call_target="tpu_custom_call" | custom-call | tf_op jit(solution)/shard_map/pallas_call | solution.py:44
  34.2 0.1 collective-permute-done.8.z1
  34.3 1.2 %shard_map.106 = (bf16[3,2,32,128]{3,2,1,0:T(8,128)(2,1)S(1)}, bf16[3,2,32,128]{3,2,1,0:T(8,128)(2,1)S(1)}, bf16[2,32,128]{2,1,0:T(8,128)(2,1)S(1)}, bf16[5,32,1...) custom-call(s32[2]{0:T(128)S(1)} %pad_add_fusion.place, bf16[4,2,32,128]{3,2,1,0:T(8,128)(2,1)S(1)} %pad_maximum_fusion.1.z0, ...), custom_call_target="tpu_custom_call" | custom-call | tf_op jit(solution)/shard_map/pallas_call | solution.py:44
  35.5 1.1 %collective-permute-start.11 = (bf16[5,32,128]{2,1,0:T(8,128)(2,1)S(1)}, bf16[5,32,128]{2,1,0:T(8,128)(2,1)S(1)}, u32[]{:S(2)}, u32[]{:S(2)}) collective-permute-start(bf16[5,32,128]{2,1,0:T(8,128)(2,1)S(1)} %get-tuple-element.75), channel_id=1, source_target_pairs={{0,2},{1,3},{2,0},{3,1},{4,6},{5,7},{6,4},{7,5},{8,10},{9,11},{10,... | collective-permute-start | bytes 122888 | tf_op jit(solution)/shard_map/ppermute | solution.py:684
  36.6 1.8 %collective-permute-start.13 = (bf16[5,32,128]{2,1,0:T(8,128)(2,1)S(1)}, bf16[5,32,128]{2,1,0:T(8,128)(2,1)S(1)}, u32[]{:S(2)}, u32[]{:S(2)}) collective-permute-start(bf16[5,32,128]{2,1,0:T(8,128)(2,1)S(1)} %get-tuple-element.76), channel_id=1, source_target_pairs={{0,6},{1,7},{2,4},{3,5},{4,2},{5,3},{6,0},{7,1},{8,14},{9,15},{10,... | collective-permute-start | bytes 122888 | tf_op jit(solution)/shard_map/ppermute | solution.py:684
  38.4 1.2 %collective-permute-start.12 = (bf16[2,32,128]{2,1,0:T(8,128)(2,1)S(1)}, bf16[2,32,128]{2,1,0:T(8,128)(2,1)S(1)}, u32[]{:S(2)}, u32[]{:S(2)}) collective-permute-start(bf16[2,32,128]{2,1,0:T(8,128)(2,1)S(1)} %get-tuple-element.74.p5), channel_id=1, source_target_pairs={{0,4},{1,5},{2,6},{3,7},{4,0},{5,1},{6,2},{7,3},{8,12},{9,13},{10,... | collective-permute-start | bytes 49160 | tf_op jit(solution)/shard_map/ppermute | solution.py:684
  39.7 2.9 %shard_map.107 = (bf16[8,12,32,128]{3,2,1,0:T(8,128)(2,1)S(1)}, bf16[4,6,32,128]{3,2,1,0:T(8,128)(2,1)S(1)}, bf16[7,2,384,512]{3,2,1,0:T(8,128)(2,1)S(1)}, bf16[8,384,256]{2,1,0:T(8,128)(2,1)S(1)}) custom-call(bf16[8,12,32,256]{3,2,1,0:T(8,128)(2,1)S(1)} %shard_map.105.f3, bf16[256,256]{1,0:T(8,128)(2,1)S(1)} %get-tuple-element.51.merge_in, ...), custom_call_target="tpu_custom_call" | custom-call | tf_op jit(solution)/shard_map/pallas_call | solution.py:44
  42.6 1.0 %collective-permute-done.12.q2 = bf16[2,32,128]{2,1,0:T(8,128)(2,1)S(1)} collective-permute-done((bf16[2,32,128]{2,1,0:T(8,128)(2,1)S(1)}, bf16[2,32,128]{2,1,0:T(8,128)(2,1)S(1)}, u32[]{:S(2)}, u32[]{:S(2)}) %collective-permute-start.12) | collective-permute-done | bytes 16416 | tf_op jit(solution)/shard_map/ppermute | solution.py:684
  43.7 9.9 %shard_map.108 = f32[32,8,64]{2,1,0:T(8,128)} custom-call(s32[2]{0:T(128)S(1)} %pad_add_fusion.place, s32[8,64]{1,0:T(8,128)S(1)} %bitcast.17, bf16[3,2,32,128]{3,2,1,0:T(8,128)(2,1)S(1)} %get-tuple-element.72.a3, bf16[3,2,32,128]{3,2,1,0:T(8,128)(2,1)S(1)} %get-tuple-element.73.a4, bf16[2,32,128]{2,1,0:T(8,128)(2,1)S(1)} %get-tuple-element.74.p5, ...), custom_call_target="tpu_custom_call" | custom-call | tf_op jit(solution)/shard_map/pallas_call | solution.py:44
  (20 shorter events, 0.5 us)
Async XLA Ops:
  0.0 9.8 %collective-permute-start = (bf16[8,16,256]{2,1,0:T(8,128)(2,1)}, bf16[8,16,256]{2,1,0:T(8,128)(2,1)S(1)}, u32[]{:S(2)}, u32[]{:S(2)}) collective-permute-start(bf16[8,16,256]{2,1,0:T(8,128)(2,1)} %own.1), channel_id=1, source_target_pairs={{0,120},{1,121},{2,122},{3,123},{4,124},{5,125},{6,126},{7,127},{8... | collective-permute-start | bytes 196616 | tf_op jit(solution)/shard_map/ppermute | solution.py:684
  6.6 4.5 %collective-permute-start.1 = (bf16[8,16,256]{2,1,0:T(8,128)(2,1)}, bf16[8,16,256]{2,1,0:T(8,128)(2,1)S(1)}, u32[]{:S(2)}, u32[]{:S(2)}) collective-permute-start(bf16[8,16,256]{2,1,0:T(8,128)(2,1)} %own.1), channel_id=1, source_target_pairs={{0,8},{1,9},{2,10},{3,11},{4,12},{5,13},{6,14},{7,15},{8,0},{9,1},... | collective-permute-start | bytes 196616 | tf_op jit(solution)/shard_map/ppermute | solution.py:684
  11.1 5.3 %collective-permute-start.2 = (bf16[3,8,8,256]{3,2,1,0:T(8,128)(2,1)S(1)}, bf16[3,8,8,256]{3,2,1,0:T(8,128)(2,1)S(1)}, u32[]{:S(2)}, u32[]{:S(2)}) collective-permute-start(bf16[3,8,8,256]{3,2,1,0:T(8,128)(2,1)S(1)} %get-tuple-element.92), channel_id=1, source_target_pairs={{0,7},{1,2},{2,1},{3,4},{4,3},{5,6},{6,5},{7,0},{8,15},{9,10},{10,... | collective-permute-start | bytes 294920 | tf_op jit(solution)/shard_map/ppermute | solution.py:684
  12.0 4.5 %collective-permute-start.3 = (bf16[3,8,8,256]{3,2,1,0:T(8,128)(2,1)S(1)}, bf16[3,8,8,256]{3,2,1,0:T(8,128)(2,1)S(1)}, u32[]{:S(2)}, u32[]{:S(2)}) collective-permute-start(bf16[3,8,8,256]{3,2,1,0:T(8,128)(2,1)S(1)} %get-tuple-element.91), channel_id=1, source_target_pairs={{0,1},{1,0},{2,3},{3,2},{4,5},{5,4},{6,7},{7,6},{8,9},{9,8},{10,11... | collective-permute-start | bytes 294920 | tf_op jit(solution)/shard_map/ppermute | solution.py:684
  19.5 1.3 %collective-permute-start.4 = (bf16[32,128]{1,0:T(8,128)(2,1)S(1)}, bf16[32,128]{1,0:T(8,128)(2,1)S(1)}, u32[]{:S(2)}, u32[]{:S(2)}) collective-permute-start(bf16[32,128]{1,0:T(8,128)(2,1)S(1)} %get-tuple-element.60), channel_id=1, source_target_pairs={{0,1},{1,0},{2,3},{3,2},{4,5},{5,4},{6,7},{7,6},{8,9},{9,8},{10,11... | collective-permute-start | bytes 24584 | tf_op jit(solution)/shard_map/ppermute | solution.py:684
  20.8 5.3 %collective-permute-start.5 = (bf16[2,32,128]{2,1,0:T(8,128)(2,1)S(1)}, bf16[2,32,128]{2,1,0:T(8,128)(2,1)S(1)}, u32[]{:S(2)}, u32[]{:S(2)}) collective-permute-start(bf16[2,32,128]{2,1,0:T(8,128)(2,1)S(1)} %pad_maximum_fusion.2), channel_id=1, source_target_pairs={{0,16},{1,17},{2,18},{3,19},{4,20},{5,21},{6,22},{7,23},{8,24},{9,... | collective-permute-start | bytes 49160 | tf_op jit(solution)/shard_map/ppermute | solution.py:684
  20.8 5.3 %collective-permute-start.6 = (bf16[2,32,128]{2,1,0:T(8,128)(2,1)S(1)}, bf16[2,32,128]{2,1,0:T(8,128)(2,1)S(1)}, u32[]{:S(2)}, u32[]{:S(2)}) collective-permute-start(bf16[2,32,128]{2,1,0:T(8,128)(2,1)S(1)} %pad_maximum_fusion.2), channel_id=1, source_target_pairs={{0,24},{1,25},{2,26},{3,27},{4,28},{5,29},{6,30},{7,31},{8,16},{9,... | collective-permute-start | bytes 49160 | tf_op jit(solution)/shard_map/ppermute | solution.py:684
  24.2 3.7 %collective-permute-start.7 = (bf16[2,32,128]{2,1,0:T(8,128)(2,1)S(1)}, bf16[2,32,128]{2,1,0:T(8,128)(2,1)S(1)}, u32[]{:S(2)}, u32[]{:S(2)}) collective-permute-start(bf16[2,32,128]{2,1,0:T(8,128)(2,1)S(1)} %pad_maximum_fusion.2), channel_id=1, source_target_pairs={{0,8},{1,9},{2,10},{3,11},{4,12},{5,13},{6,14},{7,15},{8,0},{9,1},... | collective-permute-start | bytes 49160 | tf_op jit(solution)/shard_map/ppermute | solution.py:684
  27.9 6.2 %collective-permute-start.10 = (bf16[4,2,32,128]{3,2,1,0:T(8,128)(2,1)S(1)}, bf16[4,2,32,128]{3,2,1,0:T(8,128)(2,1)S(1)}, u32[]{:S(2)}, u32[]{:S(2)}) collective-permute-start(bf16[4,2,32,128]{3,2,1,0:T(8,128)(2,1)S(1)} %pad_maximum_fusion.1.z0), channel_id=1, source_target_pairs={{0,64},{1,65},{2,66},{3,67},{4,68},{5,69},{6,70},{7,71},{8,72},{9,... | collective-permute-start | bytes 196616 | tf_op jit(solution)/shard_map/ppermute | solution.py:684
  28.0 6.3 %collective-permute-start.8 = (bf16[4,2,32,128]{3,2,1,0:T(8,128)(2,1)S(1)}, bf16[4,2,32,128]{3,2,1,0:T(8,128)(2,1)S(1)}, u32[]{:S(2)}, u32[]{:S(2)}) collective-permute-start(bf16[4,2,32,128]{3,2,1,0:T(8,128)(2,1)S(1)} %pad_maximum_fusion.1.z0), channel_id=1, source_target_pairs={{0,96},{1,97},{2,98},{3,99},{4,100},{5,101},{6,102},{7,103},{8,104... | collective-permute-start | bytes 196616 | tf_op jit(solution)/shard_map/ppermute | solution.py:684
  28.7 5.6 %collective-permute-start.9 = (bf16[4,2,32,128]{3,2,1,0:T(8,128)(2,1)S(1)}, bf16[4,2,32,128]{3,2,1,0:T(8,128)(2,1)S(1)}, u32[]{:S(2)}, u32[]{:S(2)}) collective-permute-start(bf16[4,2,32,128]{3,2,1,0:T(8,128)(2,1)S(1)} %pad_maximum_fusion.1.z0), channel_id=1, source_target_pairs={{0,32},{1,33},{2,34},{3,35},{4,36},{5,37},{6,38},{7,39},{8,40},{9,... | collective-permute-start | bytes 196616 | tf_op jit(solution)/shard_map/ppermute | solution.py:684
  34.2 9.5 %copy-start = (s32[8,1,64]{2,1,0:T(1,128)S(1)}, s32[8,1,64]{2,1,0:T(1,128)}, u32[]{:S(2)}) copy-start(s32[8,1,64]{2,1,0:T(1,128)} %param.19) | copy-start | bytes 6148
  35.5 8.2 %collective-permute-start.11 = (bf16[5,32,128]{2,1,0:T(8,128)(2,1)S(1)}, bf16[5,32,128]{2,1,0:T(8,128)(2,1)S(1)}, u32[]{:S(2)}, u32[]{:S(2)}) collective-permute-start(bf16[5,32,128]{2,1,0:T(8,128)(2,1)S(1)} %get-tuple-element.75), channel_id=1, source_target_pairs={{0,2},{1,3},{2,0},{3,1},{4,6},{5,7},{6,4},{7,5},{8,10},{9,11},{10,... | collective-permute-start | bytes 122888 | tf_op jit(solution)/shard_map/ppermute | solution.py:684
  36.6 7.1 %collective-permute-start.13 = (bf16[5,32,128]{2,1,0:T(8,128)(2,1)S(1)}, bf16[5,32,128]{2,1,0:T(8,128)(2,1)S(1)}, u32[]{:S(2)}, u32[]{:S(2)}) collective-permute-start(bf16[5,32,128]{2,1,0:T(8,128)(2,1)S(1)} %get-tuple-element.76), channel_id=1, source_target_pairs={{0,6},{1,7},{2,4},{3,5},{4,2},{5,3},{6,0},{7,1},{8,14},{9,15},{10,... | collective-permute-start | bytes 122888 | tf_op jit(solution)/shard_map/ppermute | solution.py:684
  38.4 5.2 %collective-permute-start.12 = (bf16[2,32,128]{2,1,0:T(8,128)(2,1)S(1)}, bf16[2,32,128]{2,1,0:T(8,128)(2,1)S(1)}, u32[]{:S(2)}, u32[]{:S(2)}) collective-permute-start(bf16[2,32,128]{2,1,0:T(8,128)(2,1)S(1)} %get-tuple-element.74.p5), channel_id=1, source_target_pairs={{0,4},{1,5},{2,6},{3,7},{4,0},{5,1},{6,2},{7,3},{8,12},{9,13},{10,... | collective-permute-start | bytes 49160 | tf_op jit(solution)/shard_map/ppermute | solution.py:684

commit v6 on v5

--- a/solution.py
+++ b/solution.py
@@ -669,10 +669,14 @@
     cell_logits = dot(stacked, wh[...]).reshape(4, samples, 128)
     coarse = cell_logits.astype(bf16)
     rest = (cell_logits - coarse.astype(f32)).astype(bf16)
-    places = lax.broadcasted_iota(jnp.int32, (128, 64), 0)
-    for i in range(8):
-        chosen = (places == slots[i : i + 1, :] + 64 * (i % 2)).astype(bf16)
-        out[:, i, :] = dot(coarse[i // 2], chosen) + dot(rest[i // 2], chosen)
+    both = jnp.concatenate([coarse, rest], axis=-1)
+    places = lax.broadcasted_iota(jnp.int32, (256, 128), 0) % 128
+    for i in range(4):
+        wanted = jnp.concatenate([slots[2 * i : 2 * i + 1], slots[2 * i + 1 : 2 * i + 2] + 64], axis=1)
+        chosen = jnp.where(places == wanted, 1.0, 0.0).astype(bf16)
+        picked = dot(both[i], chosen)
+        out[:, 2 * i, :] = picked[:, 0:64]
+        out[:, 2 * i + 1, :] = picked[:, 64:128]
 
 
 def swap(value, partner):

time: 53.7 us -> 53.8 us (level)
  no operation moved by 1% of the time
where the time goes in v6:
time: 53.8 us; the launch traced here: 53.6 us
  Pallas kernels  28.7 us (53%)
  starting transfers between devices  19.6 us (36%)
  waiting for transfers between devices  5.08 us (9%)
    pallas_call x9, Pallas kernels, whole_call(): pl.pallas_call(body, out_shape=out_shapes, in_specs=specs, out_specs=jax....  28.7 us
    ppermute x14, starting transfers between devices, swap(): return lax.ppermute(value, ('row', 'col'), pairs)  19.6 us
    ppermute x14, waiting for transfers between devices, swap(): return lax.ppermute(value, ('row', 'col'), pairs)  5.08 us
  transfers between devices with their start and end apart: 14, of which 8 were waited for; matrix products, arithmetic and copies ran while one was open for 0% of the time, Pallas kernels for 27%

profile of v6, /device:TPU:0, one launch (start us, length us, event | category | flops | bytes accessed | tf_op | source)
XLA Modules:
  0.0 53.6 jit_solution(12373181935439655599)
XLA Ops:
  0.0 6.6 %collective-permute-start = (bf16[8,16,256]{2,1,0:T(8,128)(2,1)}, bf16[8,16,256]{2,1,0:T(8,128)(2,1)S(1)}, u32[]{:S(2)}, u32[]{:S(2)}) collective-permute-start(bf16[8,16,256]{2,1,0:T(8,128)(2,1)} %own.1), channel_id=1, source_target_pairs={{0,120},{1,121},{2,122},{3,123},{4,124},{5,125},{6,126},{7,127},{8... | collective-permute-start | bytes 196616 | tf_op jit(solution)/shard_map/ppermute | solution.py:688
  6.6 3.2 %shard_map.100 = (bf16[8,16,256]{2,1,0:T(8,128)(2,1)S(1)}, bf16[3,1024,256]{2,1,0:T(8,128)(2,1)S(1)}, bf16[512,256]{1,0:T(8,128)(2,1)S(1)}, bf16[256,256]{1,0:T(...) custom-call(bf16[8,16,256]{2,1,0:T(8,128)(2,1)} %own.1, ...), custom_call_target="tpu_custom_call" | custom-call | tf_op jit(solution)/shard_map/pallas_call | solution.py:44
  9.8 1.3 %collective-permute-done.1 = bf16[8,16,256]{2,1,0:T(8,128)(2,1)S(1)} collective-permute-done((bf16[8,16,256]{2,1,0:T(8,128)(2,1)}, bf16[8,16,256]{2,1,0:T(8,128)(2,1)S(1)}, u32[]{:S(2)}, u32[]{:S(2)}) %collective-permute-start.1) | collective-permute-done | bytes 65568 | tf_op jit(solution)/shard_map/ppermute | solution.py:688
  11.1 0.8 %collective-permute-start.2 = (bf16[3,8,8,256]{3,2,1,0:T(8,128)(2,1)S(1)}, bf16[3,8,8,256]{3,2,1,0:T(8,128)(2,1)S(1)}, u32[]{:S(2)}, u32[]{:S(2)}) collective-permute-start(bf16[3,8,8,256]{3,2,1,0:T(8,128)(2,1)S(1)} %get-tuple-element.92), channel_id=1, source_target_pairs={{0,7},{1,2},{2,1},{3,4},{4,3},{5,6},{6,5},{7,0},{8,15},{9,10},{10,... | collective-permute-start | bytes 294920 | tf_op jit(solution)/shard_map/ppermute | solution.py:688
  12.0 0.8 %collective-permute-start.3 = (bf16[3,8,8,256]{3,2,1,0:T(8,128)(2,1)S(1)}, bf16[3,8,8,256]{3,2,1,0:T(8,128)(2,1)S(1)}, u32[]{:S(2)}, u32[]{:S(2)}) collective-permute-start(bf16[3,8,8,256]{3,2,1,0:T(8,128)(2,1)S(1)} %get-tuple-element.91), channel_id=1, source_target_pairs={{0,1},{1,0},{2,3},{3,2},{4,5},{5,4},{6,7},{7,6},{8,9},{9,8},{10,11... | collective-permute-start | bytes 294920 | tf_op jit(solution)/shard_map/ppermute | solution.py:688
  12.9 3.1 %shard_map.101 = (bf16[7,7,32,256]{3,2,1,0:T(8,128)(2,1)S(1)}, bf16[6,6,32,256]{3,2,1,0:T(8,128)(2,1)S(1)}, bf16[5,5,32,256]{3,2,1,0:T(8,128)(2,1)S(1)}, bf16[4,...) custom-call(s32[2]{0:T(128)S(1)} %pad_add_fusion.place, bf16[3,8,16,256]{3,2,1,0:T(8,128)(2,1)S(1)} %pad_maximum_fusion.tiles, ...), custom_call_target="tpu_custom_call" | custom-call | tf_op jit(solution)/shard_map/pallas_call | solution.py:44
  15.9 0.5 collective-permute-done.2.col_b
  16.4 3.1 %shard_map.102 = (bf16[2,7,3,32,256]{4,3,2,1,0:T(8,128)(2,1)S(1)}, bf16[2,6,3,32,256]{4,3,2,1,0:T(8,128)(2,1)S(1)}, bf16[2,5,3,32,256]{4,3,2,1,0:T(8,128)(2,1)S(...) custom-call(s32[2]{0:T(128)S(1)} %pad_add_fusion.place, ...), custom_call_target="tpu_custom_call" | custom-call | tf_op jit(solution)/shard_map/pallas_call | solution.py:44
  19.6 1.0 %shard_map.103.f0 = bf16[11,15,32,256]{3,2,1,0:T(8,128)(2,1)S(1)} custom-call(f32[24,4,8,256]{3,2,1,0:T(8,128)S(1)} %get-tuple-element.61.ext, bf16[512,256]{1,0:T(8,128)(2,1)S(1)} %get-tuple-element.50.we, bf16[7,7,32,256]{3,2,1,0:T(8,128)(2,1)S(1)} %get-tuple-element.56.i0, bf16[2,7,3,32,256]{4,3,2,1,0:T(8,128)(2,1)S(1)} %get-tuple-element.62.s0), custom_call_target="tpu_custom_call" | custom-call | tf_op jit(solution)/shard_map/pallas_call | solution.py:44
  20.6 0.2 collective-permute-done.4
  20.8 3.4 %collective-permute-start.6 = (bf16[2,32,128]{2,1,0:T(8,128)(2,1)S(1)}, bf16[2,32,128]{2,1,0:T(8,128)(2,1)S(1)}, u32[]{:S(2)}, u32[]{:S(2)}) collective-permute-start(bf16[2,32,128]{2,1,0:T(8,128)(2,1)S(1)} %pad_maximum_fusion.2), channel_id=1, source_target_pairs={{0,24},{1,25},{2,26},{3,27},{4,28},{5,29},{6,30},{7,31},{8,16},{9,... | collective-permute-start | bytes 49160 | tf_op jit(solution)/shard_map/ppermute | solution.py:688
  24.3 1.7 %shard_map.104.f1 = bf16[10,14,32,256]{3,2,1,0:T(8,128)(2,1)S(1)} custom-call(bf16[11,15,32,256]{3,2,1,0:T(8,128)(2,1)S(1)} %shard_map.103.f0, bf16[3,1024,256]{2,1,0:T(8,128)(2,1)S(1)} %get-tuple-element.49.wq, bf16[6,6,32,256]{3,2,1,0:T(8,128)(2,1)S(1)} %get-tuple-element.57.i1, bf16[2,6,3,32,256]{4,3,2,1,0:T(8,128)(2,1)S(1)} %get-tuple-element.65.s1), custom_call_target="tpu_custom_call" | custom-call | tf_op jit(solution)/shard_map/pallas_call | solution.py:44
  26.1 1.8 %collective-permute-done.7 = bf16[2,32,128]{2,1,0:T(8,128)(2,1)S(1)} collective-permute-done((bf16[2,32,128]{2,1,0:T(8,128)(2,1)S(1)}, bf16[2,32,128]{2,1,0:T(8,128)(2,1)S(1)}, u32[]{:S(2)}, u32[]{:S(2)}) %collective-permute-start.7) | collective-permute-done | bytes 16416 | tf_op jit(solution)/shard_map/ppermute | solution.py:688
  28.0 0.7 %collective-permute-start.8 = (bf16[4,2,32,128]{3,2,1,0:T(8,128)(2,1)S(1)}, bf16[4,2,32,128]{3,2,1,0:T(8,128)(2,1)S(1)}, u32[]{:S(2)}, u32[]{:S(2)}) collective-permute-start(bf16[4,2,32,128]{3,2,1,0:T(8,128)(2,1)S(1)} %pad_maximum_fusion.1.z0), channel_id=1, source_target_pairs={{0,96},{1,97},{2,98},{3,99},{4,100},{5,101},{6,102},{7,103},{8,104... | collective-permute-start | bytes 196616 | tf_op jit(solution)/shard_map/ppermute | solution.py:688
  28.7 2.8 %collective-permute-start.9 = (bf16[4,2,32,128]{3,2,1,0:T(8,128)(2,1)S(1)}, bf16[4,2,32,128]{3,2,1,0:T(8,128)(2,1)S(1)}, u32[]{:S(2)}, u32[]{:S(2)}) collective-permute-start(bf16[4,2,32,128]{3,2,1,0:T(8,128)(2,1)S(1)} %pad_maximum_fusion.1.z0), channel_id=1, source_target_pairs={{0,32},{1,33},{2,34},{3,35},{4,36},{5,37},{6,38},{7,39},{8,40},{9,... | collective-permute-start | bytes 196616 | tf_op jit(solution)/shard_map/ppermute | solution.py:688
  31.5 2.6 %shard_map.105.f3 = bf16[8,12,32,256]{3,2,1,0:T(8,128)(2,1)S(1)} custom-call(bf16[10,14,32,256]{3,2,1,0:T(8,128)(2,1)S(1)} %shard_map.104.f1, bf16[3,1024,256]{2,1,0:T(8,128)(2,1)S(1)} %get-tuple-element.49.wq, bf16[5,5,32,256]{3,2,1,0:T(8,128)(2,1)S(1)} %get-tuple-element.58.i2, bf16[2,5,3,32,256]{4,3,2,1,0:T(8,128)(2,1)S(1)} %get-tuple-element.68.s2, ...), custom_call_target="tpu_custom_call" | custom-call | tf_op jit(solution)/shard_map/pallas_call | solution.py:44
  34.2 0.1 collective-permute-done.8.z1
  34.3 1.2 %shard_map.106 = (bf16[3,2,32,128]{3,2,1,0:T(8,128)(2,1)S(1)}, bf16[3,2,32,128]{3,2,1,0:T(8,128)(2,1)S(1)}, bf16[2,32,128]{2,1,0:T(8,128)(2,1)S(1)}, bf16[5,32,1...) custom-call(s32[2]{0:T(128)S(1)} %pad_add_fusion.place, bf16[4,2,32,128]{3,2,1,0:T(8,128)(2,1)S(1)} %pad_maximum_fusion.1.z0, ...), custom_call_target="tpu_custom_call" | custom-call | tf_op jit(solution)/shard_map/pallas_call | solution.py:44
  35.5 1.1 %collective-permute-start.11 = (bf16[5,32,128]{2,1,0:T(8,128)(2,1)S(1)}, bf16[5,32,128]{2,1,0:T(8,128)(2,1)S(1)}, u32[]{:S(2)}, u32[]{:S(2)}) collective-permute-start(bf16[5,32,128]{2,1,0:T(8,128)(2,1)S(1)} %get-tuple-element.75), channel_id=1, source_target_pairs={{0,2},{1,3},{2,0},{3,1},{4,6},{5,7},{6,4},{7,5},{8,10},{9,11},{10,... | collective-permute-start | bytes 122888 | tf_op jit(solution)/shard_map/ppermute | solution.py:688
  36.6 1.8 %collective-permute-start.13 = (bf16[5,32,128]{2,1,0:T(8,128)(2,1)S(1)}, bf16[5,32,128]{2,1,0:T(8,128)(2,1)S(1)}, u32[]{:S(2)}, u32[]{:S(2)}) collective-permute-start(bf16[5,32,128]{2,1,0:T(8,128)(2,1)S(1)} %get-tuple-element.76), channel_id=1, source_target_pairs={{0,6},{1,7},{2,4},{3,5},{4,2},{5,3},{6,0},{7,1},{8,14},{9,15},{10,... | collective-permute-start | bytes 122888 | tf_op jit(solution)/shard_map/ppermute | solution.py:688
  38.4 1.2 %collective-permute-start.12 = (bf16[2,32,128]{2,1,0:T(8,128)(2,1)S(1)}, bf16[2,32,128]{2,1,0:T(8,128)(2,1)S(1)}, u32[]{:S(2)}, u32[]{:S(2)}) collective-permute-start(bf16[2,32,128]{2,1,0:T(8,128)(2,1)S(1)} %get-tuple-element.74.p5), channel_id=1, source_target_pairs={{0,4},{1,5},{2,6},{3,7},{4,0},{5,1},{6,2},{7,3},{8,12},{9,13},{10,... | collective-permute-start | bytes 49160 | tf_op jit(solution)/shard_map/ppermute | solution.py:688
  39.7 2.9 %shard_map.107 = (bf16[8,12,32,128]{3,2,1,0:T(8,128)(2,1)S(1)}, bf16[4,6,32,128]{3,2,1,0:T(8,128)(2,1)S(1)}, bf16[7,2,384,512]{3,2,1,0:T(8,128)(2,1)S(1)}, bf16[8,384,256]{2,1,0:T(8,128)(2,1)S(1)}) custom-call(bf16[8,12,32,256]{3,2,1,0:T(8,128)(2,1)S(1)} %shard_map.105.f3, bf16[256,256]{1,0:T(8,128)(2,1)S(1)} %get-tuple-element.51.merge_in, ...), custom_call_target="tpu_custom_call" | custom-call | tf_op jit(solution)/shard_map/pallas_call | solution.py:44
  42.6 1.0 %collective-permute-done.12.q2 = bf16[2,32,128]{2,1,0:T(8,128)(2,1)S(1)} collective-permute-done((bf16[2,32,128]{2,1,0:T(8,128)(2,1)S(1)}, bf16[2,32,128]{2,1,0:T(8,128)(2,1)S(1)}, u32[]{:S(2)}, u32[]{:S(2)}) %collective-permute-start.12) | collective-permute-done | bytes 16416 | tf_op jit(solution)/shard_map/ppermute | solution.py:688
  43.7 10.0 %shard_map.108 = f32[32,8,64]{2,1,0:T(8,128)} custom-call(s32[2]{0:T(128)S(1)} %pad_add_fusion.place, s32[8,64]{1,0:T(8,128)S(1)} %bitcast.17, bf16[3,2,32,128]{3,2,1,0:T(8,128)(2,1)S(1)} %get-tuple-element.72.a3, bf16[3,2,32,128]{3,2,1,0:T(8,128)(2,1)S(1)} %get-tuple-element.73.a4, bf16[2,32,128]{2,1,0:T(8,128)(2,1)S(1)} %get-tuple-element.74.p5, ...), custom_call_target="tpu_custom_call" | custom-call | tf_op jit(solution)/shard_map/pallas_call | solution.py:44
  (20 shorter events, 0.5 us)
Async XLA Ops:
  0.0 9.8 %collective-permute-start = (bf16[8,16,256]{2,1,0:T(8,128)(2,1)}, bf16[8,16,256]{2,1,0:T(8,128)(2,1)S(1)}, u32[]{:S(2)}, u32[]{:S(2)}) collective-permute-start(bf16[8,16,256]{2,1,0:T(8,128)(2,1)} %own.1), channel_id=1, source_target_pairs={{0,120},{1,121},{2,122},{3,123},{4,124},{5,125},{6,126},{7,127},{8... | collective-permute-start | bytes 196616 | tf_op jit(solution)/shard_map/ppermute | solution.py:688
  6.6 4.5 %collective-permute-start.1 = (bf16[8,16,256]{2,1,0:T(8,128)(2,1)}, bf16[8,16,256]{2,1,0:T(8,128)(2,1)S(1)}, u32[]{:S(2)}, u32[]{:S(2)}) collective-permute-start(bf16[8,16,256]{2,1,0:T(8,128)(2,1)} %own.1), channel_id=1, source_target_pairs={{0,8},{1,9},{2,10},{3,11},{4,12},{5,13},{6,14},{7,15},{8,0},{9,1},... | collective-permute-start | bytes 196616 | tf_op jit(solution)/shard_map/ppermute | solution.py:688
  11.1 5.3 %collective-permute-start.2 = (bf16[3,8,8,256]{3,2,1,0:T(8,128)(2,1)S(1)}, bf16[3,8,8,256]{3,2,1,0:T(8,128)(2,1)S(1)}, u32[]{:S(2)}, u32[]{:S(2)}) collective-permute-start(bf16[3,8,8,256]{3,2,1,0:T(8,128)(2,1)S(1)} %get-tuple-element.92), channel_id=1, source_target_pairs={{0,7},{1,2},{2,1},{3,4},{4,3},{5,6},{6,5},{7,0},{8,15},{9,10},{10,... | collective-permute-start | bytes 294920 | tf_op jit(solution)/shard_map/ppermute | solution.py:688
  12.0 4.5 %collective-permute-start.3 = (bf16[3,8,8,256]{3,2,1,0:T(8,128)(2,1)S(1)}, bf16[3,8,8,256]{3,2,1,0:T(8,128)(2,1)S(1)}, u32[]{:S(2)}, u32[]{:S(2)}) collective-permute-start(bf16[3,8,8,256]{3,2,1,0:T(8,128)(2,1)S(1)} %get-tuple-element.91), channel_id=1, source_target_pairs={{0,1},{1,0},{2,3},{3,2},{4,5},{5,4},{6,7},{7,6},{8,9},{9,8},{10,11... | collective-permute-start | bytes 294920 | tf_op jit(solution)/shard_map/ppermute | solution.py:688
  19.5 1.3 %collective-permute-start.4 = (bf16[32,128]{1,0:T(8,128)(2,1)S(1)}, bf16[32,128]{1,0:T(8,128)(2,1)S(1)}, u32[]{:S(2)}, u32[]{:S(2)}) collective-permute-start(bf16[32,128]{1,0:T(8,128)(2,1)S(1)} %get-tuple-element.60), channel_id=1, source_target_pairs={{0,1},{1,0},{2,3},{3,2},{4,5},{5,4},{6,7},{7,6},{8,9},{9,8},{10,11... | collective-permute-start | bytes 24584 | tf_op jit(solution)/shard_map/ppermute | solution.py:688
  20.8 5.3 %collective-permute-start.5 = (bf16[2,32,128]{2,1,0:T(8,128)(2,1)S(1)}, bf16[2,32,128]{2,1,0:T(8,128)(2,1)S(1)}, u32[]{:S(2)}, u32[]{:S(2)}) collective-permute-start(bf16[2,32,128]{2,1,0:T(8,128)(2,1)S(1)} %pad_maximum_fusion.2), channel_id=1, source_target_pairs={{0,16},{1,17},{2,18},{3,19},{4,20},{5,21},{6,22},{7,23},{8,24},{9,... | collective-permute-start | bytes 49160 | tf_op jit(solution)/shard_map/ppermute | solution.py:688
  20.8 5.3 %collective-permute-start.6 = (bf16[2,32,128]{2,1,0:T(8,128)(2,1)S(1)}, bf16[2,32,128]{2,1,0:T(8,128)(2,1)S(1)}, u32[]{:S(2)}, u32[]{:S(2)}) collective-permute-start(bf16[2,32,128]{2,1,0:T(8,128)(2,1)S(1)} %pad_maximum_fusion.2), channel_id=1, source_target_pairs={{0,24},{1,25},{2,26},{3,27},{4,28},{5,29},{6,30},{7,31},{8,16},{9,... | collective-permute-start | bytes 49160 | tf_op jit(solution)/shard_map/ppermute | solution.py:688
  24.2 3.7 %collective-permute-start.7 = (bf16[2,32,128]{2,1,0:T(8,128)(2,1)S(1)}, bf16[2,32,128]{2,1,0:T(8,128)(2,1)S(1)}, u32[]{:S(2)}, u32[]{:S(2)}) collective-permute-start(bf16[2,32,128]{2,1,0:T(8,128)(2,1)S(1)} %pad_maximum_fusion.2), channel_id=1, source_target_pairs={{0,8},{1,9},{2,10},{3,11},{4,12},{5,13},{6,14},{7,15},{8,0},{9,1},... | collective-permute-start | bytes 49160 | tf_op jit(solution)/shard_map/ppermute | solution.py:688
  27.9 6.2 %collective-permute-start.10 = (bf16[4,2,32,128]{3,2,1,0:T(8,128)(2,1)S(1)}, bf16[4,2,32,128]{3,2,1,0:T(8,128)(2,1)S(1)}, u32[]{:S(2)}, u32[]{:S(2)}) collective-permute-start(bf16[4,2,32,128]{3,2,1,0:T(8,128)(2,1)S(1)} %pad_maximum_fusion.1.z0), channel_id=1, source_target_pairs={{0,64},{1,65},{2,66},{3,67},{4,68},{5,69},{6,70},{7,71},{8,72},{9,... | collective-permute-start | bytes 196616 | tf_op jit(solution)/shard_map/ppermute | solution.py:688
  28.0 6.3 %collective-permute-start.8 = (bf16[4,2,32,128]{3,2,1,0:T(8,128)(2,1)S(1)}, bf16[4,2,32,128]{3,2,1,0:T(8,128)(2,1)S(1)}, u32[]{:S(2)}, u32[]{:S(2)}) collective-permute-start(bf16[4,2,32,128]{3,2,1,0:T(8,128)(2,1)S(1)} %pad_maximum_fusion.1.z0), channel_id=1, source_target_pairs={{0,96},{1,97},{2,98},{3,99},{4,100},{5,101},{6,102},{7,103},{8,104... | collective-permute-start | bytes 196616 | tf_op jit(solution)/shard_map/ppermute | solution.py:688
  28.7 5.6 %collective-permute-start.9 = (bf16[4,2,32,128]{3,2,1,0:T(8,128)(2,1)S(1)}, bf16[4,2,32,128]{3,2,1,0:T(8,128)(2,1)S(1)}, u32[]{:S(2)}, u32[]{:S(2)}) collective-permute-start(bf16[4,2,32,128]{3,2,1,0:T(8,128)(2,1)S(1)} %pad_maximum_fusion.1.z0), channel_id=1, source_target_pairs={{0,32},{1,33},{2,34},{3,35},{4,36},{5,37},{6,38},{7,39},{8,40},{9,... | collective-permute-start | bytes 196616 | tf_op jit(solution)/shard_map/ppermute | solution.py:688
  34.2 9.5 %copy-start = (s32[8,1,64]{2,1,0:T(1,128)S(1)}, s32[8,1,64]{2,1,0:T(1,128)}, u32[]{:S(2)}) copy-start(s32[8,1,64]{2,1,0:T(1,128)} %param.19) | copy-start | bytes 6148
  35.5 8.2 %collective-permute-start.11 = (bf16[5,32,128]{2,1,0:T(8,128)(2,1)S(1)}, bf16[5,32,128]{2,1,0:T(8,128)(2,1)S(1)}, u32[]{:S(2)}, u32[]{:S(2)}) collective-permute-start(bf16[5,32,128]{2,1,0:T(8,128)(2,1)S(1)} %get-tuple-element.75), channel_id=1, source_target_pairs={{0,2},{1,3},{2,0},{3,1},{4,6},{5,7},{6,4},{7,5},{8,10},{9,11},{10,... | collective-permute-start | bytes 122888 | tf_op jit(solution)/shard_map/ppermute | solution.py:688
  36.6 7.1 %collective-permute-start.13 = (bf16[5,32,128]{2,1,0:T(8,128)(2,1)S(1)}, bf16[5,32,128]{2,1,0:T(8,128)(2,1)S(1)}, u32[]{:S(2)}, u32[]{:S(2)}) collective-permute-start(bf16[5,32,128]{2,1,0:T(8,128)(2,1)S(1)} %get-tuple-element.76), channel_id=1, source_target_pairs={{0,6},{1,7},{2,4},{3,5},{4,2},{5,3},{6,0},{7,1},{8,14},{9,15},{10,... | collective-permute-start | bytes 122888 | tf_op jit(solution)/shard_map/ppermute | solution.py:688
  38.4 5.2 %collective-permute-start.12 = (bf16[2,32,128]{2,1,0:T(8,128)(2,1)S(1)}, bf16[2,32,128]{2,1,0:T(8,128)(2,1)S(1)}, u32[]{:S(2)}, u32[]{:S(2)}) collective-permute-start(bf16[2,32,128]{2,1,0:T(8,128)(2,1)S(1)} %get-tuple-element.74.p5), channel_id=1, source_target_pairs={{0,4},{1,5},{2,6},{3,7},{4,0},{5,1},{6,2},{7,3},{8,12},{9,13},{10,... | collective-permute-start | bytes 49160 | tf_op jit(solution)/shard_map/ppermute | solution.py:688
